TPU v7x, 32 devices: a whole 2x2x4 slice. The times are simulated.
32 devices in a mesh: group: 2 (over y), out: 4 (over z), in: 2 (over x), tok: 2 (over core).
Axes of the slice: x: 2, y: 2, z: 4, core: 2. Of those that a mesh axis runs over, the one named last changes fastest.
Arguments:
- inputs: bfloat16 [864, 6144], P(('group', 'tok'), 'in'), parts along dimension 0, may hold values from -6 to 6
- grad_act: bfloat16 [864, 24576], P(('group', 'tok'), 'out'), parts along dimension 0, may hold values from -6 to 6
- weight: bfloat16 [6144, 24576], P(('in', 'tok'), 'out'), may hold values from -0.078125 to 0.078125
- score: bfloat16 [6144, 24576], P(('in', 'tok'), 'out'), may hold values from -1.1953125 to 1.1953125
Outputs:
- grad_inputs: bfloat16 [864, 6144], P(('group', 'tok'), 'in'), parts along dimension 0
- new_score: bfloat16 [12288, 24576], P(('group', 'in', 'tok'), 'out'), parts along dimension 0
There are 2 independent parts, one for each index of `group`. A program takes and returns all parts, laid end to end along the dimension named above; an argument that names none is the same for every part. Nothing has to cross between parts.
All inputs are finite; a program needn't handle non-finite values.
Results may differ from a plain program's by a relative error of at most 0.005.
Values may be sent and summed in bfloat16 or wider, within the bound.
A program may use at most 256 MiB of HBM per device.

v0:
```python
import jax
import jax.numpy as jnp
from jax import lax
from jax.sharding import PartitionSpec as P


def gelu_slope(pre):
    cdf = 0.5 * (1.0 + jax.scipy.special.erf(pre * 0.7071067811865476))
    return cdf + pre * jnp.exp(-0.5 * pre * pre) * 0.3989422804014327


def own_columns(whole, width):
    return lax.dynamic_slice_in_dim(whole, lax.axis_index("tok") * width, width, 1)


def on_device(inputs, grad_act, weight, score):
    rows_mine = weight.shape[0]
    full_rows = lax.all_gather(weight, "tok", axis=0, tiled=True)
    partial_value = jnp.dot(inputs, full_rows, preferred_element_type=jnp.float32)
    pre = lax.psum(partial_value, "in")
    grad_pre = (grad_act.astype(jnp.float32) * gelu_slope(pre)).astype(jnp.bfloat16)
    dx_terms = lax.dot_general(
        grad_pre, full_rows, (((1,), (1,)), ((), ())), preferred_element_type=jnp.float32
    )
    grad_inputs = lax.psum(dx_terms, "out").astype(jnp.bfloat16)
    all_inputs, all_grads = (
        lax.all_gather(inputs, "tok", axis=0, tiled=True),
        lax.all_gather(grad_pre, "tok", axis=0, tiled=True),
    )
    mine = own_columns(all_inputs, rows_mine)
    grad_w = lax.dot_general(
        mine, all_grads, (((0,), (0,)), ((), ())), preferred_element_type=jnp.float32
    )
    new_score = (score.astype(jnp.float32) - weight.astype(jnp.float32) * grad_w).astype(
        jnp.bfloat16
    )
    return (grad_inputs, new_score)


def solution(mesh):
    placed = (
        P(("group", "tok"), "in"),
        P(("group", "tok"), "out"),
        P(("in", "tok"), "out"),
        P(("in", "tok"), "out"),
    )
    return jax.shard_map(
        on_device,
        mesh=mesh,
        in_specs=placed,
        out_specs=(P(("group", "tok"), "in"), P(("group", "in", "tok"), "out")),
        check_vma=False,
    )
```

profile of v0, /device:TPU:0, one launch (start us, length us, event | category | flops | bytes accessed | tf_op | source)
XLA Modules:
  0.0 376.9 jit_solution(14252043581522032646)
XLA Ops:
  7.2 0.0 copy-start.1
  7.2 0.0 all-gather.4.cloned.1.call-start
  7.2 0.7 all-gather.4.cloned.1.call-update
  7.9 0.0 all-reduce.3.cloned.1.call-start
  8.0 62.2 %all-gather.4.cloned.1.call-done = bf16[3072,6144]{1,0:T(8,128)(2,1)} async-done(((bf16[1536,6144]{1,0:T(8,128)(2,1)}), bf16[3072,6144]{1,0:T(8,128)(2,1)}) %all-gather.4.cloned.1.call-update) | async-done | bytes 37748752 | tf_op jit(solution)/shard_map/all_gather | solution.py:18
  70.1 0.0 copy-done.1
  70.1 17.6 %fusion.8 = f32[216,6144]{1,0:T(8,128)} fusion(bf16[216,3072]{1,0:T(8,128)(2,1)S(1)} %copy-done.1, bf16[3072,6144]{1,0:T(8,128)(2,1)} %all-gather.4.cloned.1.call-done), kind=kOutput, calls=%fused_computation.10 | convolution fusion | flops 8153726976 | bytes 44384256 | tf_op jit(solution)/shard_map/dot_general | solution.py:19
  87.7 0.0 copy-start
  87.7 0.0 all-reduce.3.cloned.1.call-update
  87.7 0.0 all-gather.6.cloned.1.call-start
  87.8 0.7 all-gather.6.cloned.1.call-update
  88.5 0.0 all-gather.8.cloned.1.call-start
  88.5 132.5 %all-reduce.3.cloned.1.call-done = f32[216,6144]{1,0:T(8,128)} async-done(((f32[216,6144]{1,0:T(8,128)}), f32[216,6144]{1,0:T(8,128)}) %all-reduce.3.cloned.1.call-update) | async-done | bytes 5308432 | tf_op jit(solution)/shard_map/psum | solution.py:20
  221.0 0.0 copy-done
  221.0 5.9 %fusion.5 = bf16[216,6144]{1,0:T(8,128)(2,1)} fusion(f32[216,6144]{1,0:T(8,128)} %all-reduce.3.cloned.1.call-done, bf16[216,6144]{1,0:T(8,128)(2,1)S(1)} %copy-done), kind=kLoop, calls=%fused_computation.7 | loop fusion | flops 14598144 | bytes 10616832 | tf_op jit(solution)/shard_map/convert_element_type | solution.py:21
  226.9 0.0 all-gather.8.cloned.1.call-update
  226.9 19.3 %fusion.9 = f32[216,3072]{1,0:T(8,128)S(1)} fusion(bf16[216,6144]{1,0:T(8,128)(2,1)} %fusion.5, bf16[3072,6144]{1,0:T(8,128)(2,1)} %all-gather.4.cloned.1.call-done), kind=kOutput, calls=%fused_computation.11 | convolution fusion | flops 8153726976 | bytes 43057152 | tf_op jit(solution)/shard_map/dot_general | solution.py:22
  246.2 96.3 %all-reduce.4 = bf16[216,3072]{1,0:T(8,128)(2,1)} all-reduce(f32[216,3072]{1,0:T(8,128)S(1)} %fusion.9), channel_id=1, replica_groups=mesh['group'=2,'out'=4,'in'=2,'tok'=2] {'out'}, use_global_device_ids=true, to_apply=%region_1.0 | all-reduce | flops 663552 | bytes 3981312 | tf_op jit(solution)/shard_map/psum | solution.py:25
  342.5 0.0 all-gather.6.cloned.1.call-done
  342.5 0.0 all-gather.8.cloned.1.call-done
  342.5 27.9 %subtract_convert_fusion = bf16[1536,6144]{1,0:T(8,128)(2,1)} fusion(bf16[1536,6144]{1,0:T(8,128)(2,1)} %param.6, bf16[1536,6144]{1,0:T(8,128)(2,1)} %param.7, bf16[432,6144]{1,0:T(8,128)(2,1)} %all-gather.8.cloned.1.call-done, bf16[432,3072]{1,0:T(8,128)(2,1)} %all-gather.6.cloned.1.call-done, s32[]{:T(128)S(6)} %select_n.3), kind=kOutput, calls=%fused_computation | convolution fusion | flops 8200912896 | bytes 63258628 | tf_op jit(solution)/shard_map/dot_general | solution.py:31
Async XLA Ops:
  7.2 62.9 %copy-start.1 = (bf16[216,3072]{1,0:T(8,128)(2,1)S(1)}, bf16[216,3072]{1,0:T(8,128)(2,1)}, u32[]{:S(2)}) copy-start(bf16[216,3072]{1,0:T(8,128)(2,1)} %param.4) | copy-start | bytes 3981316
  7.2 62.9 %all-gather.4.cloned.1.call-start = ((), (), s32[]{:S(2)}) async-start(), calls=%async_computation | async-start | bytes 56623104 | tf_op jit(solution)/shard_map/all_gather | solution.py:18
  7.9 213.1 %all-reduce.3.cloned.1.call-start = ((), (), s32[]{:S(2)}) async-start(), calls=%async_computation.1 | async-start | bytes 10616832 | tf_op jit(solution)/shard_map/psum | solution.py:20
  87.7 133.3 %copy-start = (bf16[216,6144]{1,0:T(8,128)(2,1)S(1)}, bf16[216,6144]{1,0:T(8,128)(2,1)}, u32[]{:S(2)}) copy-start(bf16[216,6144]{1,0:T(8,128)(2,1)} %param.5) | copy-start | bytes 7962628
  87.7 254.8 %all-gather.6.cloned.1.call-start = ((), (), s32[]{:S(2)}) async-start(), calls=%async_computation.2 | async-start | bytes 3981312 | tf_op jit(solution)/shard_map/all_gather | solution.py:27
  88.5 254.0 %all-gather.8.cloned.1.call-start = ((), (), s32[]{:S(2)}) async-start(), calls=%async_computation.3 | async-start | bytes 7962624 | tf_op jit(solution)/shard_map/all_gather | solution.py:28
Sparse Core Ops, SparseCore 0:
  9.6 60.4 all-gather.3
  87.8 133.1 all-reduce.2
  222.5 11.3 all-gather.5
  235.9 16.4 all-gather.7
where the time goes:
time: 377 us
  waiting for transfers between devices  196 us (52%)
  blocking collectives  96.3 us (26%)
  matrix products  64.7 us (17%)
  between operations  13.8 us (4%)
  other arithmetic  5.88 us (2%)
    psum x1, waiting for transfers between devices, on_device(): pre = lax.psum(partial_value, 'in')  132 us
    psum x1, blocking collectives, on_device(): grad_inputs = lax.psum(dx_terms, 'out').astype(jnp.bfloat16)  96.3 us
    all_gather x1, waiting for transfers between devices, on_device(): full_rows = lax.all_gather(weight, 'tok', axis=0, tiled=True)  62.2 us
    dot_general x1, matrix products, on_device(): lax.dot_general(mine, all_grads, (((0,), (0,)), ((), ())), preferred_elem...  27.9 us
    dot_general x1, matrix products, on_device(): lax.dot_general(grad_pre, full_rows, (((1,), (1,)), ((), ())), preferred_...  19.3 us
    dot_general x1, matrix products, on_device(): jnp.dot(inputs, full_rows, preferred_element_type=jnp.float32)  17.6 us
  transfers between devices with their start and end apart: 4, of which 2 were waited for; matrix products, arithmetic and copies ran while one was open for 7% of the time, Pallas kernels for 0%

commit v1 on v0

v1 whole, which is shorter than its diff:
```python
import jax
import jax.numpy as jnp
from jax import lax
from jax.sharding import PartitionSpec as P

BF = jnp.bfloat16
F32 = jnp.float32


def gelu_slope(pre):
    cdf = 0.5 * (1.0 + jax.scipy.special.erf(pre * 0.7071067811865476))
    return cdf + pre * jnp.exp(-0.5 * pre * pre) * 0.3989422804014327


def swap(x):
    return lax.ppermute(x, "tok", [(0, 1), (1, 0)])


def mm(a, b, dims):
    return lax.dot_general(a, b, (dims, ((), ())), preferred_element_type=F32)


def sum_over(x, axis, n):
    if n == 1:
        return x
    if n == 2:
        return x + lax.ppermute(x.astype(BF), axis, [(0, 1), (1, 0)]).astype(F32)
    return lax.psum(x, axis)


def reduce_out(x, axis, n):
    if n == 1:
        return x.astype(BF)
    if n > 8 or x.shape[1] % (128 * n):
        return lax.psum(x, axis).astype(BF)
    w = x.shape[1] // n
    me = lax.axis_index(axis)
    total = lax.dynamic_slice_in_dim(x, me * w, w, 1)
    xb = x.astype(BF)
    for k in range(1, n):
        to = lax.rem(me + k, n)
        piece = lax.dynamic_slice_in_dim(xb, to * w, w, 1)
        got = lax.ppermute(piece, axis, [(i, (i + k) % n) for i in range(n)])
        total = total + got.astype(F32)
    mine = total.astype(BF)
    out = jnp.zeros(x.shape, BF)
    out = lax.dynamic_update_slice_in_dim(out, mine, me * w, 1)
    for k in range(1, n):
        got = lax.ppermute(mine, axis, [(i, (i + k) % n) for i in range(n)])
        out = lax.dynamic_update_slice_in_dim(out, got, lax.rem(me - k + n, n) * w, 1)
    return out


def make(n_in, n_out):
    def on_device(inputs, grad_act, weight, score):
        rows, ff = weight.shape
        t = lax.axis_index("tok")
        x_mine = lax.dynamic_slice_in_dim(inputs, t * rows, rows, 1)
        x_other = swap(lax.dynamic_slice_in_dim(inputs, (1 - t) * rows, rows, 1))
        chunks = 4 if ff % (4 * 256) == 0 else 1
        w = ff // chunks
        gm, go = [], []
        for c in range(chunks):
            wc = weight[:, c * w : (c + 1) * w]
            send = mm(x_other, wc, ((1,), (0,))).astype(BF)
            part = mm(x_mine, wc, ((1,), (0,))) + swap(send).astype(F32)
            pre = sum_over(part, "in", n_in)
            g = (grad_act[:, c * w : (c + 1) * w].astype(F32) * gelu_slope(pre)).astype(BF)
            gm.append(g)
            go.append(swap(g))
        gm = jnp.concatenate(gm, axis=1)
        go = jnp.concatenate(go, axis=1)
        dx_other = mm(go, weight, ((1,), (1,))).astype(BF)
        dx_mine = mm(gm, weight, ((1,), (1,)))
        dx_got = swap(dx_other).astype(F32)
        lo = jnp.where(t == 0, dx_mine, dx_got)
        hi = jnp.where(t == 0, dx_got, dx_mine)
        grad_inputs = reduce_out(jnp.concatenate([lo, hi], axis=1), "out", n_out)
        xs = jnp.concatenate([x_mine, x_other], axis=0)
        gs = jnp.concatenate([gm, go], axis=0)
        grad_w = mm(xs, gs, ((0,), (0,)))
        new_score = (score.astype(F32) - weight.astype(F32) * grad_w).astype(BF)
        return grad_inputs, new_score

    return on_device


def solution(mesh):
    placed = (
        P(("group", "tok"), "in"),
        P(("group", "tok"), "out"),
        P(("in", "tok"), "out"),
        P(("in", "tok"), "out"),
    )
    return jax.shard_map(
        make(mesh.shape["in"], mesh.shape["out"]),
        mesh=mesh,
        in_specs=placed,
        out_specs=(P(("group", "tok"), "in"), P(("group", "in", "tok"), "out")),
        check_vma=False,
    )
```

time: 377 us -> 185 us (0.49)
  waiting for transfers between devices: 196 us -> 80.3 us
  blocking collectives: 96.3 us -> 0 us
  starting transfers between devices: 0.16 us -> 23.9 us
  between operations: 13.8 us -> 0.93 us
  matrix products: 64.7 us -> 70.4 us
  local copies, waits for them, and re-layouts: 0.01 us -> 4.17 us
    psum x1 -> x0, waiting for transfers between devices: 132 us -> none  [on_device(): pre = lax.psum(partial_value, 'in')]
    psum x1 -> x0, blocking collectives: 96.3 us -> none  [on_device(): grad_inputs = lax.psum(dx_terms, 'out').astype(jnp.bfloat16)]
    ppermute x0 -> x20, waiting for transfers between devices: none -> 80.3 us  [the longest x4 51.7 us: sum_over(): return x + lax.ppermute(x.astype(BF), axis, [(0, 1), (1, 0)]).astype(F32)]
    all_gather x3 -> x0, waiting for transfers between devices: 62.2 us -> none  [the longest x1 62.2 us: on_device(): full_rows = lax.all_gather(weight, 'tok', axis=0, tiled=True)]
    ppermute x0 -> x20, starting transfers between devices: none -> 23.9 us  [the longest x3 9.92 us: reduce_out(): got = lax.ppermute(mine, axis, [(i, (i + k) % n) for i in range(n)])]
    dot_general x3 -> x11, matrix products: 64.7 us -> 70.4 us  [mm(): return lax.dot_general(a, b, (dims, ((), ())), preferred_element_type=F32)]
  transfers between devices with their start and end apart: 4 -> 20, of which waited for: 2 -> 12; matrix products, arithmetic and copies ran while one was open for 7% -> 24% of each run, Pallas kernels for 0% -> 0%
where the time goes in v1:
time: 185 us
  waiting for transfers between devices  80.3 us (43%)
  matrix products  70.4 us (38%)
  starting transfers between devices  23.9 us (13%)
  other arithmetic  5.63 us (3%)
  local copies, waits for them, and re-layouts  4.17 us (2%)
    dot_general x11, matrix products, mm(): return lax.dot_general(a, b, (dims, ((), ())), preferred_element_type=F32)  70.4 us
    ppermute x4, waiting for transfers between devices, sum_over(): return x + lax.ppermute(x.astype(BF), axis, [(0, 1), (1, 0)]).astype(F32)  51.7 us
    ppermute x3, waiting for transfers between devices, reduce_out(): got = lax.ppermute(piece, axis, [(i, (i + k) % n) for i in range(n)])  20.9 us
    ppermute x3, starting transfers between devices, reduce_out(): got = lax.ppermute(mine, axis, [(i, (i + k) % n) for i in range(n)])  9.92 us
    ppermute x10, waiting for transfers between devices, swap(): return lax.ppermute(x, 'tok', [(0, 1), (1, 0)])  7.71 us
    ppermute x3, starting transfers between devices, reduce_out(): got = lax.ppermute(piece, axis, [(i, (i + k) % n) for i in range(n)])  5.76 us
    ppermute x4, starting transfers between devices, sum_over(): return x + lax.ppermute(x.astype(BF), axis, [(0, 1), (1, 0)]).astype(F32)  5.19 us
  transfers between devices with their start and end apart: 20, of which 12 were waited for; matrix products, arithmetic and copies ran while one was open for 24% of the time, Pallas kernels for 0%

profile of v1, /device:TPU:0, one launch (start us, length us, event | category | flops | bytes accessed | tf_op | source)
XLA Modules:
  0.0 185.3 jit_solution(2989080802798670080)
XLA Ops:
  0.6 1.5 constant_dynamic-slice_fusion.3
  2.2 0.5 collective-permute-start
  2.7 1.7 collective-permute-done
  4.4 4.5 %fusion.37 = bf16[216,1536]{1,0:T(8,128)(2,1)S(1)} fusion(bf16[216,1536]{1,0:T(8,128)(2,1)S(1)} %collective-permute-done, bf16[1536,6144]{1,0:T(8,128)(2,1)} %param.6), kind=kOutput, calls=%fused_computation.39 | convolution fusion | flops 1019547648 | bytes 6045696 | tf_op jit(solution)/shard_map/dot_general | solution.py:20
  9.0 0.4 collective-permute-start.3
  9.4 3.5 %fusion.40 = bf16[216,1536]{1,0:T(8,128)(2,1)S(1)} fusion(bf16[216,1536]{1,0:T(8,128)(2,1)S(1)} %collective-permute-done, bf16[1536,6144]{1,0:T(8,128)(2,1)} %param.6), kind=kOutput, calls=%fused_computation.40 | convolution fusion | flops 1019547648 | bytes 6045696 | tf_op jit(solution)/shard_map/dot_general | solution.py:20
  13.0 0.2 collective-permute-start.5
  13.2 1.3 fusion.43
  14.4 0.4 collective-permute-start.7
  14.9 1.3 fusion.34
  16.1 0.2 collective-permute-start.1
  16.3 1.3 fusion.74
  17.6 2.9 %collective-permute-start.4 = (bf16[216,1536]{1,0:T(8,128)(2,1)S(1)}, bf16[216,1536]{1,0:T(8,128)(2,1)S(1)}, u32[]{:S(2)}, u32[]{:S(2)}) collective-permute-start(bf16[216,1536]{1,0:T(8,128)(2,1)S(1)} %get-tuple-element.17), channel_id=1, source_target_pairs={{0,2},{2,0},{1,3},{3,1},{4,6},{6,4},{5,7},{7,5},{8,10},{10,8},{9,1... | collective-permute-start | bytes 1990664 | tf_op jit(solution)/shard_map/ppermute | solution.py:27
  20.6 1.3 fusion.75
  21.8 0.1 collective-permute-start.6
  21.9 1.3 fusion.76
  23.2 2.1 %collective-permute-start.8 = (bf16[216,1536]{1,0:T(8,128)(2,1)S(1)}, bf16[216,1536]{1,0:T(8,128)(2,1)S(1)}, u32[]{:S(2)}, u32[]{:S(2)}) collective-permute-start(bf16[216,1536]{1,0:T(8,128)(2,1)S(1)} %get-tuple-element.19), channel_id=1, source_target_pairs={{0,2},{2,0},{1,3},{3,1},{4,6},{6,4},{5,7},{7,5},{8,10},{10,8},{9,1... | collective-permute-start | bytes 1990664 | tf_op jit(solution)/shard_map/ppermute | solution.py:27
  25.3 1.3 fusion.73
  26.6 0.1 collective-permute-start.2
  26.7 9.6 %collective-permute-done.4 = bf16[216,1536]{1,0:T(8,128)(2,1)S(1)} collective-permute-done((bf16[216,1536]{1,0:T(8,128)(2,1)S(1)}, bf16[216,1536]{1,0:T(8,128)(2,1)S(1)}, u32[]{:S(2)}, u32[]{:S(2)}) %collective-permute-start.4) | collective-permute-done | bytes 663584 | tf_op jit(solution)/shard_map/ppermute | solution.py:27
  36.3 14.2 %collective-permute-done.6 = bf16[216,1536]{1,0:T(8,128)(2,1)S(1)} collective-permute-done((bf16[216,1536]{1,0:T(8,128)(2,1)S(1)}, bf16[216,1536]{1,0:T(8,128)(2,1)S(1)}, u32[]{:S(2)}, u32[]{:S(2)}) %collective-permute-start.6) | collective-permute-done | bytes 663584 | tf_op jit(solution)/shard_map/ppermute | solution.py:27
  50.5 14.2 %collective-permute-done.8 = bf16[216,1536]{1,0:T(8,128)(2,1)S(1)} collective-permute-done((bf16[216,1536]{1,0:T(8,128)(2,1)S(1)}, bf16[216,1536]{1,0:T(8,128)(2,1)S(1)}, u32[]{:S(2)}, u32[]{:S(2)}) %collective-permute-start.8) | collective-permute-done | bytes 663584 | tf_op jit(solution)/shard_map/ppermute | solution.py:27
  64.7 13.7 %collective-permute-done.2 = bf16[216,1536]{1,0:T(8,128)(2,1)S(1)} collective-permute-done((bf16[216,1536]{1,0:T(8,128)(2,1)S(1)}, bf16[216,1536]{1,0:T(8,128)(2,1)S(1)}, u32[]{:S(2)}, u32[]{:S(2)}) %collective-permute-start.2) | collective-permute-done | bytes 663584 | tf_op jit(solution)/shard_map/ppermute | solution.py:27
  78.4 3.2 %fusion.51 = (bf16[216,1536]{1,0:T(8,128)(2,1)S(1)}, bf16[216,1536]{1,0:T(8,128)(2,1)S(1)}, bf16[216,1536]{1,0:T(8,128)(2,1)S(1)}, bf16[216,1536]{1,0:T(8,128)(2,1)S(1)}) fusion(bf16[216,1536]{1,0:T(8,128)(2,1)S(1)} %collective-permute-done.2, f32[216,1536]{1,0:T(8,128)S(1)} %get-tuple-element.16, bf16[216,1536]{1,0:T(8,128)(2,1)S(1)} %collective-permute-done.1, ...), kind=kLoop, calls=%fused_computation.54 | loop fusion | flops 19906560 | bytes 15925248 | tf_op jit(solution)/shard_map/convert_element_type | solution.py:68
  81.8 0.5 collective-permute-start.10
  82.4 0.4 collective-permute-start.12
  82.8 1.1 collective-permute-done.9
  84.0 0.9 collective-permute-done.10
  84.9 0.8 collective-permute-done.11
  85.9 0.9 collective-permute-done.12
  86.8 11.7 %convolution_convert_fusion = bf16[216,1536]{1,0:T(8,128)(2,1)} fusion(bf16[216,6144]{1,0:T(8,128)(2,1)S(1)} %constant_dynamic-update-slice_fusion, bf16[1536,6144]{1,0:T(8,128)(2,1)} %param.6), kind=kOutput, calls=%fused_computation.42 | convolution fusion | flops 4077195264 | bytes 22192128 | tf_op jit(solution)/shard_map/dot_general | solution.py:20
  98.5 0.1 collective-permute-start.13
  98.7 2.3 %collective-permute-done.13 = bf16[216,1536]{1,0:T(8,128)(2,1)} collective-permute-done((bf16[216,1536]{1,0:T(8,128)(2,1)}, bf16[216,1536]{1,0:T(8,128)(2,1)}, u32[]{:S(2)}, u32[]{:S(2)}) %collective-permute-start.13) | collective-permute-done | bytes 663584 | tf_op jit(solution)/shard_map/ppermute | solution.py:16
  101.0 10.3 %convert_select_fusion.1 = (f32[216,1536]{1,0:T(8,128)S(1)}, f32[216,1536]{1,0:T(8,128)S(1)}) fusion(bf16[216,1536]{1,0:T(8,128)(2,1)} %collective-permute-done.13, pred[]{:T(512)S(6)} %eq.4, bf16[1536,6144]{1,0:T(8,128)(2,1)} %param.6, bf16[216,1536]{1,0:T(8,128)(2,1)} %copy-done.4, bf16[216,1536]{1,0:T(8,128)(2,1)} %copy-done.6, ...), kind=kOutput, calls=%fused_computation.48 | convolution fusion | flops 4088475648 | bytes 24846336 | tf_op jit(solution)/shard_map/dot_general | solution.py:20
  111.4 0.1 fusion.25
  111.5 1.0 constant_dynamic-slice_fusion.2
  112.5 1.8 collective-permute-start.14
  114.3 2.6 %collective-permute-start.15 = (bf16[216,768]{1,0:T(8,128)(2,1)}, bf16[216,768]{1,0:T(8,128)(2,1)}, u32[]{:S(2)}, u32[]{:S(2)}) collective-permute-start(bf16[216,768]{1,0:T(8,128)(2,1)} %get-tuple-element.12), channel_id=1, source_target_pairs={{0,8},{4,12},{8,0},{12,4},{1,9},{5,13},{9,1},{13,5},{2,10},{6,14},... | collective-permute-start | bytes 995336 | tf_op jit(solution)/shard_map/ppermute | solution.py:43
  116.9 1.3 collective-permute-start.16
  118.3 7.1 %collective-permute-done.14 = bf16[216,768]{1,0:T(8,128)(2,1)} collective-permute-done((bf16[216,768]{1,0:T(8,128)(2,1)}, bf16[216,768]{1,0:T(8,128)(2,1)}, u32[]{:S(2)}, u32[]{:S(2)}) %collective-permute-start.14) | collective-permute-done | bytes 331808 | tf_op jit(solution)/shard_map/ppermute | solution.py:43
  125.4 13.7 %collective-permute-done.15 = bf16[216,768]{1,0:T(8,128)(2,1)} collective-permute-done((bf16[216,768]{1,0:T(8,128)(2,1)}, bf16[216,768]{1,0:T(8,128)(2,1)}, u32[]{:S(2)}, u32[]{:S(2)}) %collective-permute-start.15) | collective-permute-done | bytes 331808 | tf_op jit(solution)/shard_map/ppermute | solution.py:43
  139.1 0.1 broadcast_in_dim.3
  139.3 2.3 %constant_dynamic-update-slice_fusion.7 = (bf16[216,3072]{1,0:T(8,128)(2,1)S(1)}, bf16[216,768]{1,0:T(8,128)(2,1)}) fusion(bf16[216,3072]{1,0:T(8,128)(2,1)S(1)} %broadcast_in_dim.3, s32[]{:T(128)S(6)} %select_n.39, bf16[216,768]{1,0:T(8,128)(2,1)} %collective-permute-done.16, bf16[216,768]{1,0:T(8,128)(2,1)} %collective-permute-done.15, ...), kind=kLoop, calls=%fused_computation.96 | loop fusion | flops 1327104 | bytes 4313092 | tf_op jit(solution)/shard_map/dynamic_update_slice | solution.py:47
  141.6 7.6 %collective-permute-start.17 = (bf16[216,768]{1,0:T(8,128)(2,1)}, bf16[216,768]{1,0:T(8,128)(2,1)S(1)}, u32[]{:S(2)}, u32[]{:S(2)}) collective-permute-start(bf16[216,768]{1,0:T(8,128)(2,1)} %get-tuple-element.3), channel_id=1, source_target_pairs={{0,4},{4,8},{8,12},{12,0},{1,5},{5,9},{9,13},{13,1},{2,6},{6,10},{... | collective-permute-start | bytes 995336 | tf_op jit(solution)/shard_map/ppermute | solution.py:49
  149.1 1.6 collective-permute-start.18
  150.7 0.8 collective-permute-start.19
  151.5 32.6 %subtract_convert_fusion = bf16[1536,6144]{1,0:T(8,128)(2,1)} fusion(bf16[1536,6144]{1,0:T(8,128)(2,1)} %param.6, bf16[1536,6144]{1,0:T(8,128)(2,1)} %param.7, bf16[216,6144]{1,0:T(8,128)(2,1)} %copy-done.8, bf16[216,1536]{1,0:T(8,128)(2,1)S(1)} %copy-done.5, bf16[216,1536]{1,0:T(8,128)(2,1)} %copy-done.6, bf16[216,1536]{1,0:T(8,128)(2,1)S(1)} %copy-done.3, ...), kind=kOutput, calls=%fused_computation | convolution fusion | flops 8230109184 | bytes 63258624 | tf_op jit(solution)/shard_map/dot_general | solution.py:20
  184.2 1.1 copy-done.1
  (38 shorter events, 0.6 us)
Async XLA Ops:
  0.6 12.5 %copy-start.9 = (bf16[1536,6144]{1,0:T(8,128)(2,1)S(1)}, bf16[1536,6144]{1,0:T(8,128)(2,1)}, u32[]{:S(2)}) copy-start(bf16[1536,6144]{1,0:T(8,128)(2,1)} %param.6) | copy-start | bytes 56623108
  2.2 23.1 %copy-start.7 = (bf16[216,1536]{1,0:T(8,128)(2,1)}, bf16[216,1536]{1,0:T(8,128)(2,1)S(1)}, u32[]{:S(2)}) copy-start(bf16[216,1536]{1,0:T(8,128)(2,1)S(1)} %get-tuple-element.14) | copy-start | bytes 1990660
  2.2 2.3 %collective-permute-start = (bf16[216,1536]{1,0:T(8,128)(2,1)S(1)}, bf16[216,1536]{1,0:T(8,128)(2,1)S(1)}, u32[]{:S(2)}, u32[]{:S(2)}) collective-permute-start(bf16[216,1536]{1,0:T(8,128)(2,1)S(1)} %get-tuple-element.13), channel_id=1, source_target_pairs={{0,1},{1,0},{2,3},{3,2},{4,5},{5,4},{6,7},{7,6},{8,9},{9,8},{10,11... | collective-permute-start | bytes 1990664 | tf_op jit(solution)/shard_map/ppermute | solution.py:16
  4.4 10.4 %copy-start.10 = (bf16[216,1536]{1,0:T(8,128)(2,1)}, bf16[216,1536]{1,0:T(8,128)(2,1)S(1)}, u32[]{:S(2)}) copy-start(bf16[216,1536]{1,0:T(8,128)(2,1)S(1)} %collective-permute-done) | copy-start | bytes 1990660
  9.0 7.4 %collective-permute-start.3 = (bf16[216,1536]{1,0:T(8,128)(2,1)S(1)}, bf16[216,1536]{1,0:T(8,128)(2,1)S(1)}, u32[]{:S(2)}, u32[]{:S(2)}) collective-permute-start(bf16[216,1536]{1,0:T(8,128)(2,1)S(1)} %fusion.37), channel_id=1, source_target_pairs={{0,1},{1,0},{2,3},{3,2},{4,5},{5,4},{6,7},{7,6},{8,9},{9,8},{10,11... | collective-permute-start | bytes 1990664 | tf_op jit(solution)/shard_map/ppermute | solution.py:16
  13.0 7.6 %collective-permute-start.5 = (bf16[216,1536]{1,0:T(8,128)(2,1)S(1)}, bf16[216,1536]{1,0:T(8,128)(2,1)S(1)}, u32[]{:S(2)}, u32[]{:S(2)}) collective-permute-start(bf16[216,1536]{1,0:T(8,128)(2,1)S(1)} %fusion.40), channel_id=1, source_target_pairs={{0,1},{1,0},{2,3},{3,2},{4,5},{5,4},{6,7},{7,6},{8,9},{9,8},{10,11... | collective-permute-start | bytes 1990664 | tf_op jit(solution)/shard_map/ppermute | solution.py:16
  14.4 7.5 %collective-permute-start.7 = (bf16[216,1536]{1,0:T(8,128)(2,1)S(1)}, bf16[216,1536]{1,0:T(8,128)(2,1)S(1)}, u32[]{:S(2)}, u32[]{:S(2)}) collective-permute-start(bf16[216,1536]{1,0:T(8,128)(2,1)S(1)} %fusion.43), channel_id=1, source_target_pairs={{0,1},{1,0},{2,3},{3,2},{4,5},{5,4},{6,7},{7,6},{8,9},{9,8},{10,11... | collective-permute-start | bytes 1990664 | tf_op jit(solution)/shard_map/ppermute | solution.py:16
  16.1 9.2 %collective-permute-start.1 = (bf16[216,1536]{1,0:T(8,128)(2,1)S(1)}, bf16[216,1536]{1,0:T(8,128)(2,1)S(1)}, u32[]{:S(2)}, u32[]{:S(2)}) collective-permute-start(bf16[216,1536]{1,0:T(8,128)(2,1)S(1)} %fusion.34), channel_id=1, source_target_pairs={{0,1},{1,0},{2,3},{3,2},{4,5},{5,4},{6,7},{7,6},{8,9},{9,8},{10,11... | collective-permute-start | bytes 1990664 | tf_op jit(solution)/shard_map/ppermute | solution.py:16
  17.6 18.6 %collective-permute-start.4 = (bf16[216,1536]{1,0:T(8,128)(2,1)S(1)}, bf16[216,1536]{1,0:T(8,128)(2,1)S(1)}, u32[]{:S(2)}, u32[]{:S(2)}) collective-permute-start(bf16[216,1536]{1,0:T(8,128)(2,1)S(1)} %get-tuple-element.17), channel_id=1, source_target_pairs={{0,2},{2,0},{1,3},{3,1},{4,6},{6,4},{5,7},{7,5},{8,10},{10,8},{9,1... | collective-permute-start | bytes 1990664 | tf_op jit(solution)/shard_map/ppermute | solution.py:27
  21.8 28.6 %collective-permute-start.6 = (bf16[216,1536]{1,0:T(8,128)(2,1)S(1)}, bf16[216,1536]{1,0:T(8,128)(2,1)S(1)}, u32[]{:S(2)}, u32[]{:S(2)}) collective-permute-start(bf16[216,1536]{1,0:T(8,128)(2,1)S(1)} %get-tuple-element.21), channel_id=1, source_target_pairs={{0,2},{2,0},{1,3},{3,1},{4,6},{6,4},{5,7},{7,5},{8,10},{10,8},{9,1... | collective-permute-start | bytes 1990664 | tf_op jit(solution)/shard_map/ppermute | solution.py:27
  23.2 41.5 %collective-permute-start.8 = (bf16[216,1536]{1,0:T(8,128)(2,1)S(1)}, bf16[216,1536]{1,0:T(8,128)(2,1)S(1)}, u32[]{:S(2)}, u32[]{:S(2)}) collective-permute-start(bf16[216,1536]{1,0:T(8,128)(2,1)S(1)} %get-tuple-element.19), channel_id=1, source_target_pairs={{0,2},{2,0},{1,3},{3,1},{4,6},{6,4},{5,7},{7,5},{8,10},{10,8},{9,1... | collective-permute-start | bytes 1990664 | tf_op jit(solution)/shard_map/ppermute | solution.py:27
  25.3 53.1 %copy-start = (bf16[216,6144]{1,0:T(8,128)(2,1)S(1)}, bf16[216,6144]{1,0:T(8,128)(2,1)}, u32[]{:S(2)}) copy-start(bf16[216,6144]{1,0:T(8,128)(2,1)} %param.5) | copy-start | bytes 7962628
  26.6 51.9 %collective-permute-start.2 = (bf16[216,1536]{1,0:T(8,128)(2,1)S(1)}, bf16[216,1536]{1,0:T(8,128)(2,1)S(1)}, u32[]{:S(2)}, u32[]{:S(2)}) collective-permute-start(bf16[216,1536]{1,0:T(8,128)(2,1)S(1)} %get-tuple-element.15), channel_id=1, source_target_pairs={{0,2},{2,0},{1,3},{3,1},{4,6},{6,4},{5,7},{7,5},{8,10},{10,8},{9,1... | collective-permute-start | bytes 1990664 | tf_op jit(solution)/shard_map/ppermute | solution.py:27
  81.7 3.2 %copy-start.2 = (bf16[216,1536]{1,0:T(8,128)(2,1)}, bf16[216,1536]{1,0:T(8,128)(2,1)S(1)}, u32[]{:S(2)}) copy-start(bf16[216,1536]{1,0:T(8,128)(2,1)S(1)} %get-tuple-element.5) | copy-start | bytes 1990660
  81.7 3.2 %copy-start.4 = (bf16[216,1536]{1,0:T(8,128)(2,1)}, bf16[216,1536]{1,0:T(8,128)(2,1)S(1)}, u32[]{:S(2)}) copy-start(bf16[216,1536]{1,0:T(8,128)(2,1)S(1)} %get-tuple-element.6) | copy-start | bytes 1990660
  81.7 3.2 %copy-start.6 = (bf16[216,1536]{1,0:T(8,128)(2,1)}, bf16[216,1536]{1,0:T(8,128)(2,1)S(1)}, u32[]{:S(2)}) copy-start(bf16[216,1536]{1,0:T(8,128)(2,1)S(1)} %get-tuple-element.7) | copy-start | bytes 1990660
  81.7 2.2 %collective-permute-start.9 = (bf16[216,1536]{1,0:T(8,128)(2,1)S(1)}, bf16[216,1536]{1,0:T(8,128)(2,1)S(1)}, u32[]{:S(2)}, u32[]{:S(2)}) collective-permute-start(bf16[216,1536]{1,0:T(8,128)(2,1)S(1)} %get-tuple-element.4), channel_id=1, source_target_pairs={{0,1},{1,0},{2,3},{3,2},{4,5},{5,4},{6,7},{7,6},{8,9},{9,8},{10,11... | collective-permute-start | bytes 1990664 | tf_op jit(solution)/shard_map/ppermute | solution.py:16
  81.8 3.0 %collective-permute-start.10 = (bf16[216,1536]{1,0:T(8,128)(2,1)S(1)}, bf16[216,1536]{1,0:T(8,128)(2,1)S(1)}, u32[]{:S(2)}, u32[]{:S(2)}) collective-permute-start(bf16[216,1536]{1,0:T(8,128)(2,1)S(1)} %get-tuple-element.5), channel_id=1, source_target_pairs={{0,1},{1,0},{2,3},{3,2},{4,5},{5,4},{6,7},{7,6},{8,9},{9,8},{10,11... | collective-permute-start | bytes 1990664 | tf_op jit(solution)/shard_map/ppermute | solution.py:16
  82.3 3.5 %collective-permute-start.11 = (bf16[216,1536]{1,0:T(8,128)(2,1)S(1)}, bf16[216,1536]{1,0:T(8,128)(2,1)S(1)}, u32[]{:S(2)}, u32[]{:S(2)}) collective-permute-start(bf16[216,1536]{1,0:T(8,128)(2,1)S(1)} %get-tuple-element.7), channel_id=1, source_target_pairs={{0,1},{1,0},{2,3},{3,2},{4,5},{5,4},{6,7},{7,6},{8,9},{9,8},{10,11... | collective-permute-start | bytes 1990664 | tf_op jit(solution)/shard_map/ppermute | solution.py:16
  82.4 4.4 %collective-permute-start.12 = (bf16[216,1536]{1,0:T(8,128)(2,1)S(1)}, bf16[216,1536]{1,0:T(8,128)(2,1)S(1)}, u32[]{:S(2)}, u32[]{:S(2)}) collective-permute-start(bf16[216,1536]{1,0:T(8,128)(2,1)S(1)} %get-tuple-element.6), channel_id=1, source_target_pairs={{0,1},{1,0},{2,3},{3,2},{4,5},{5,4},{6,7},{7,6},{8,9},{9,8},{10,11... | collective-permute-start | bytes 1990664 | tf_op jit(solution)/shard_map/ppermute | solution.py:16
  86.8 11.7 %copy-start.8 = (bf16[216,6144]{1,0:T(8,128)(2,1)}, bf16[216,6144]{1,0:T(8,128)(2,1)S(1)}, u32[]{:S(2)}) copy-start(bf16[216,6144]{1,0:T(8,128)(2,1)S(1)} %constant_dynamic-update-slice_fusion) | copy-start | bytes 7962628
  98.5 2.5 %collective-permute-start.13 = (bf16[216,1536]{1,0:T(8,128)(2,1)}, bf16[216,1536]{1,0:T(8,128)(2,1)}, u32[]{:S(2)}, u32[]{:S(2)}) collective-permute-start(bf16[216,1536]{1,0:T(8,128)(2,1)} %convolution_convert_fusion), channel_id=1, source_target_pairs={{0,1},{1,0},{2,3},{3,2},{4,5},{5,4},{6,7},{7,6},{8,9},{9,8},{10,11... | collective-permute-start | bytes 1990664 | tf_op jit(solution)/shard_map/ppermute | solution.py:16
  112.5 12.9 %collective-permute-start.14 = (bf16[216,768]{1,0:T(8,128)(2,1)}, bf16[216,768]{1,0:T(8,128)(2,1)}, u32[]{:S(2)}, u32[]{:S(2)}) collective-permute-start(bf16[216,768]{1,0:T(8,128)(2,1)} %get-tuple-element.10), channel_id=1, source_target_pairs={{0,4},{4,8},{8,12},{12,0},{1,5},{5,9},{9,13},{13,1},{2,6},{6,10},{... | collective-permute-start | bytes 995336 | tf_op jit(solution)/shard_map/ppermute | solution.py:43
  114.3 24.8 %collective-permute-start.15 = (bf16[216,768]{1,0:T(8,128)(2,1)}, bf16[216,768]{1,0:T(8,128)(2,1)}, u32[]{:S(2)}, u32[]{:S(2)}) collective-permute-start(bf16[216,768]{1,0:T(8,128)(2,1)} %get-tuple-element.12), channel_id=1, source_target_pairs={{0,8},{4,12},{8,0},{12,4},{1,9},{5,13},{9,1},{13,5},{2,10},{6,14},... | collective-permute-start | bytes 995336 | tf_op jit(solution)/shard_map/ppermute | solution.py:43
  116.9 22.2 %collective-permute-start.16 = (bf16[216,768]{1,0:T(8,128)(2,1)}, bf16[216,768]{1,0:T(8,128)(2,1)}, u32[]{:S(2)}, u32[]{:S(2)}) collective-permute-start(bf16[216,768]{1,0:T(8,128)(2,1)} %get-tuple-element.11), channel_id=1, source_target_pairs={{0,12},{4,0},{8,4},{12,8},{1,13},{5,1},{9,5},{13,9},{2,14},{6,2},{... | collective-permute-start | bytes 995336 | tf_op jit(solution)/shard_map/ppermute | solution.py:43
  139.3 12.2 %copy-start.3 = (bf16[216,1536]{1,0:T(8,128)(2,1)S(1)}, bf16[216,1536]{1,0:T(8,128)(2,1)}, u32[]{:S(2)}) copy-start(bf16[216,1536]{1,0:T(8,128)(2,1)} %copy-done.2) | copy-start | bytes 1990660
  139.3 12.2 %copy-start.5 = (bf16[216,1536]{1,0:T(8,128)(2,1)S(1)}, bf16[216,1536]{1,0:T(8,128)(2,1)}, u32[]{:S(2)}) copy-start(bf16[216,1536]{1,0:T(8,128)(2,1)} %copy-done.4) | copy-start | bytes 1990660
  141.6 42.5 %collective-permute-start.17 = (bf16[216,768]{1,0:T(8,128)(2,1)}, bf16[216,768]{1,0:T(8,128)(2,1)S(1)}, u32[]{:S(2)}, u32[]{:S(2)}) collective-permute-start(bf16[216,768]{1,0:T(8,128)(2,1)} %get-tuple-element.3), channel_id=1, source_target_pairs={{0,4},{4,8},{8,12},{12,0},{1,5},{5,9},{9,13},{13,1},{2,6},{6,10},{... | collective-permute-start | bytes 995336 | tf_op jit(solution)/shard_map/ppermute | solution.py:49
  149.1 35.0 %collective-permute-start.18 = (bf16[216,768]{1,0:T(8,128)(2,1)}, bf16[216,768]{1,0:T(8,128)(2,1)S(1)}, u32[]{:S(2)}, u32[]{:S(2)}) collective-permute-start(bf16[216,768]{1,0:T(8,128)(2,1)} %get-tuple-element.3), channel_id=1, source_target_pairs={{0,8},{4,12},{8,0},{12,4},{1,9},{5,13},{9,1},{13,5},{2,10},{6,14},... | collective-permute-start | bytes 995336 | tf_op jit(solution)/shard_map/ppermute | solution.py:49
  150.7 33.5 %collective-permute-start.19 = (bf16[216,768]{1,0:T(8,128)(2,1)}, bf16[216,768]{1,0:T(8,128)(2,1)S(1)}, u32[]{:S(2)}, u32[]{:S(2)}) collective-permute-start(bf16[216,768]{1,0:T(8,128)(2,1)} %get-tuple-element.3), channel_id=1, source_target_pairs={{0,12},{4,0},{8,4},{12,8},{1,13},{5,1},{9,5},{13,9},{2,14},{6,2},{... | collective-permute-start | bytes 995336 | tf_op jit(solution)/shard_map/ppermute | solution.py:49
  184.2 1.1 copy-start.1

commit v2 on v1

--- a/solution.py
+++ b/solution.py
@@ -1,6 +1,8 @@
 import jax
 import jax.numpy as jnp
 from jax import lax
+from jax.experimental import pallas as pl
+from jax.experimental.pallas import tpu as pltpu
 from jax.sharding import PartitionSpec as P
 
 BF = jnp.bfloat16
@@ -51,35 +53,143 @@
     return out
 
 
+def block_of(n, sizes):
+    for b in sizes:
+        if n % b == 0:
+            return b
+    return n
+
+
+def dx_kernel(g_ref, w_ref, o_ref):
+    @pl.when(pl.program_id(0) == 0)
+    def _():
+        o_ref[...] = jnp.zeros_like(o_ref)
+
+    o_ref[...] += lax.dot_general(
+        g_ref[...], w_ref[...], (((1,), (1,)), ((), ())), preferred_element_type=F32
+    )
+
+
+def dx_partial(g, weight):
+    rows, ff = weight.shape
+    m = g.shape[0]
+    w = block_of(ff, (768, 512, 256, 128))
+    return pl.pallas_call(
+        dx_kernel,
+        grid=(ff // w,),
+        in_specs=[
+            pl.BlockSpec((m, w), lambda i: (0, i)),
+            pl.BlockSpec((rows, w), lambda i: (0, i)),
+        ],
+        out_specs=pl.BlockSpec((m, rows), lambda i: (0, 0)),
+        out_shape=jax.ShapeDtypeStruct((m, rows), F32),
+        cost_estimate=pl.CostEstimate(
+            flops=2 * m * rows * ff, bytes_accessed=2 * rows * ff, transcendentals=0
+        ),
+        compiler_params=pltpu.CompilerParams(vmem_limit_bytes=32 * 2**20),
+    )(g, weight)
+
+
+def score_kernel(x_ref, g_ref, w_ref, s_ref, *rest):
+    o_ref = rest[-1]
+    rows = w_ref.shape[0]
+    step = block_of(rows, (384, 256, 128))
+    for r in range(0, rows, step):
+        part = pl.ds(r, step)
+        gw = jnp.dot(x_ref[part, :], g_ref[...], preferred_element_type=F32)
+        o_ref[part, :] = (
+            s_ref[part, :].astype(F32) - w_ref[part, :].astype(F32) * gw
+        ).astype(BF)
+
+
+def score_part(x_t, g, weight, score, first, count, w, earlier):
+    rows, ff = weight.shape
+    m = g.shape[0]
+    block = pl.BlockSpec((rows, w), lambda i: (0, i + first))
+    specs = [
+        pl.BlockSpec((rows, m), lambda i: (0, 0)),
+        pl.BlockSpec((m, w), lambda i: (0, i + first)),
+        block,
+        block,
+    ]
+    args = [x_t, g, weight, score]
+    alias = {}
+    if earlier is not None:
+        specs.append(pl.BlockSpec(memory_space=pl.ANY))
+        args.append(earlier)
+        alias = {4: 0}
+    return pl.pallas_call(
+        score_kernel,
+        grid=(count,),
+        in_specs=specs,
+        out_specs=block,
+        out_shape=jax.ShapeDtypeStruct((rows, ff), BF),
+        input_output_aliases=alias,
+        cost_estimate=pl.CostEstimate(
+            flops=2 * m * rows * w * count,
+            bytes_accessed=6 * rows * w * count,
+            transcendentals=0,
+        ),
+        compiler_params=pltpu.CompilerParams(vmem_limit_bytes=40 * 2**20),
+    )(*args)
+
+
 def make(n_in, n_out):
     def on_device(inputs, grad_act, weight, score):
         rows, ff = weight.shape
+        tokens = inputs.shape[0]
         t = lax.axis_index("tok")
         x_mine = lax.dynamic_slice_in_dim(inputs, t * rows, rows, 1)
         x_other = swap(lax.dynamic_slice_in_dim(inputs, (1 - t) * rows, rows, 1))
-        chunks = 4 if ff % (4 * 256) == 0 else 1
+        chunks = 2 if ff % 512 == 0 else 1
         w = ff // chunks
-        gm, go = [], []
-        for c in range(chunks):
-            wc = weight[:, c * w : (c + 1) * w]
-            send = mm(x_other, wc, ((1,), (0,))).astype(BF)
-            part = mm(x_mine, wc, ((1,), (0,))) + swap(send).astype(F32)
-            pre = sum_over(part, "in", n_in)
-            g = (grad_act[:, c * w : (c + 1) * w].astype(F32) * gelu_slope(pre)).astype(BF)
-            gm.append(g)
-            go.append(swap(g))
-        gm = jnp.concatenate(gm, axis=1)
-        go = jnp.concatenate(go, axis=1)
-        dx_other = mm(go, weight, ((1,), (1,))).astype(BF)
-        dx_mine = mm(gm, weight, ((1,), (1,)))
-        dx_got = swap(dx_other).astype(F32)
-        lo = jnp.where(t == 0, dx_mine, dx_got)
-        hi = jnp.where(t == 0, dx_got, dx_mine)
-        grad_inputs = reduce_out(jnp.concatenate([lo, hi], axis=1), "out", n_out)
-        xs = jnp.concatenate([x_mine, x_other], axis=0)
-        gs = jnp.concatenate([gm, go], axis=0)
-        grad_w = mm(xs, gs, ((0,), (0,)))
-        new_score = (score.astype(F32) - weight.astype(F32) * grad_w).astype(BF)
+        cut = -(-tokens // 32) * 16
+        spans = [(0, cut), (cut, tokens)]
+        parts = []
+        token = None
+        for lo, hi in spans:
+            xs = jnp.concatenate([x_mine[lo:hi], x_other[lo:hi]], axis=0)
+            sends = []
+            for c in range(chunks):
+                if token is not None:
+                    xs, token = lax.optimization_barrier((xs, token))
+                both = mm(xs, weight[:, c * w : (c + 1) * w], ((1,), (0,)))
+                token = both[hi - lo :].astype(BF)
+                sends.append(both[: hi - lo] + swap(token).astype(F32))
+            parts.append(sends)
+        gs, terms = [], []
+        for (lo, hi), sends in zip(spans, parts):
+            gm, go = [], []
+            for c in range(chunks):
+                pre = sum_over(sends[c], "in", n_in)
+                act = grad_act[lo:hi, c * w : (c + 1) * w]
+                g = (act.astype(F32) * gelu_slope(pre)).astype(BF)
+                gm.append(g)
+                go.append(swap(g))
+            g = jnp.concatenate(
+                [jnp.concatenate(gm, axis=1), jnp.concatenate(go, axis=1)], axis=0
+            )
+            gs.append(g)
+            dx = dx_partial(g, weight)
+            mine, got = dx[: hi - lo], swap(dx[hi - lo :].astype(BF)).astype(F32)
+            left = jnp.where(t == 0, mine, got)
+            right = jnp.where(t == 0, got, mine)
+            terms.append(jnp.concatenate([left, right], axis=1))
+        grad_inputs = jnp.concatenate(
+            [reduce_out(term, "out", n_out) for term in terms], axis=0
+        )
+        x_t = jnp.concatenate(
+            [x[lo:hi] for lo, hi in spans for x in (x_mine, x_other)], axis=0
+        ).T
+        g = jnp.concatenate(gs, axis=0)
+        wb = block_of(ff, (512, 256, 128))
+        half = ff // wb // 2
+        new_score = None
+        for first, count in ((0, half), (half, ff // wb - half)):
+            if count:
+                new_score = score_part(
+                    x_t, g, weight, score, first, count, wb, new_score
+                )
         return grad_inputs, new_score
 
     return on_device

time: 185 us -> 199 us (1.076)
  matrix products: 70.4 us -> 13.1 us
  Pallas kernels: 0 us -> 44.2 us
  other arithmetic: 5.63 us -> 22.9 us
  local copies, waits for them, and re-layouts: 4.17 us -> 18.5 us
  waiting for transfers between devices: 80.3 us -> 75.8 us
    dot_general x11 -> x4, matrix products: 70.4 us -> 13.1 us  [mm(): return lax.dot_general(a, b, (dims, ((), ())), preferred_element_type=F32)]
    pallas_call x0 -> x4, Pallas kernels: none -> 44.2 us  [the longest x2 27 us: score_part(): pl.pallas_call(score_kernel, grid=(count,), in_specs=specs, out_specs=blo...]
    ppermute x3 -> x6, waiting for transfers between devices: 0.01 us -> 22.6 us  [reduce_out(): got = lax.ppermute(mine, axis, [(i, (i + k) % n) for i in range(n)])]
    ppermute x3 -> x6, waiting for transfers between devices: 20.9 us -> 2.09 us  [reduce_out(): got = lax.ppermute(piece, axis, [(i, (i + k) % n) for i in range(n)])]
    concatenate x0 -> x6, other arithmetic: none -> 11.9 us  [the longest x1 9.59 us: on_device(): g = jnp.concatenate(gs, axis=0)]
    unnamed x25 -> x48, local copies, waits for them, and re-layouts: 1.32 us -> 12.3 us
    ppermute x10 -> x11, waiting for transfers between devices: 7.71 us -> 1.43 us  [swap(): return lax.ppermute(x, 'tok', [(0, 1), (1, 0)])]
    convert_element_type x1 -> x6, other arithmetic: 3.23 us -> 9.4 us  [the longest x2 5.19 us: on_device(): g = (act.astype(F32) * gelu_slope(pre)).astype(BF)]
  transfers between devices with their start and end apart: 20 -> 27, of which waited for: 12 -> 10; matrix products, arithmetic and copies ran while one was open for 24% -> 16% of each run, Pallas kernels for 0% -> 22%
where the time goes in v2:
time: 199 us
  waiting for transfers between devices  75.8 us (38%)
  Pallas kernels  44.2 us (22%)
  starting transfers between devices  22.9 us (12%)
  other arithmetic  22.9 us (12%)
  local copies, waits for them, and re-layouts  18.5 us (9%)
  matrix products  13.1 us (7%)
    ppermute x4, waiting for transfers between devices, sum_over(): return x + lax.ppermute(x.astype(BF), axis, [(0, 1), (1, 0)]).astype(F32)  49.7 us
    pallas_call x2, Pallas kernels, score_part(): pl.pallas_call(score_kernel, grid=(count,), in_specs=specs, out_specs=blo...  27 us
    ppermute x6, waiting for transfers between devices, reduce_out(): got = lax.ppermute(mine, axis, [(i, (i + k) % n) for i in range(n)])  22.6 us
    pallas_call x2, Pallas kernels, dx_partial(): pl.pallas_call(dx_kernel, grid=(ff // w,), in_specs=[pl.BlockSpec((m, w),...  17.2 us
    dot_general x4, matrix products, mm(): return lax.dot_general(a, b, (dims, ((), ())), preferred_element_type=F32)  13.1 us
    unnamed x48, local copies, waits for them, and re-layouts  12.3 us
    concatenate x1, other arithmetic, on_device(): g = jnp.concatenate(gs, axis=0)  9.59 us
    ppermute x6, starting transfers between devices, reduce_out(): got = lax.ppermute(piece, axis, [(i, (i + k) % n) for i in range(n)])  8.78 us
  transfers between devices with their start and end apart: 27, of which 10 were waited for; matrix products, arithmetic and copies ran while one was open for 16% of the time, Pallas kernels for 22%

profile of v2, /device:TPU:0, one launch (start us, length us, event | category | flops | bytes accessed | tf_op | source)
XLA Modules:
  0.0 198.7 jit_solution(905379046124072776)
XLA Ops:
  0.6 2.1 %constant_dynamic-slice_fusion.7 = bf16[216,1536]{1,0:T(8,128)(2,1)} fusion(bf16[216,3072]{1,0:T(8,128)(2,1)} %param.4, s32[]{:T(128)S(6)} %select_n.56), kind=kLoop, calls=%fused_computation.98 | loop fusion | bytes 1327108 | tf_op jit(solution)/shard_map/dynamic_slice | solution.py:143
  2.7 0.5 collective-permute-start
  3.7 1.4 collective-permute-done
  6.1 6.3 %fusion.6 = f32[224,3072]{1,0:T(8,128)S(1)} fusion(bf16[1536,6144]{1,0:T(8,128)(2,1)} %w_ref.7, bf16[112,1536]{0,1:T(8,128)(2,1)S(1)} %copy.14, bf16[112,1536]{0,1:T(8,128)(2,1)S(1)} %copy.13), kind=kOutput, calls=%fused_computation.6 | convolution fusion | flops 2115305472 | bytes 12877824 | tf_op jit(solution)/shard_map/dot_general | solution.py:22
  12.4 0.9 slice.157
  13.7 1.7 copy-done
  15.4 2.4 %fusion.2 = f32[224,3072]{1,0:T(8,128)S(1)} fusion(bf16[224,1536]{0,1:T(8,128)(2,1)S(1)} %pad_maximum_fusion.6, bf16[1536,6144]{1,0:T(8,128)(2,1)S(1)} %copy-done), kind=kOutput, calls=%fused_computation.2 | convolution fusion | flops 2113929216 | bytes 12976128 | tf_op jit(solution)/shard_map/dot_general | solution.py:22
  17.9 0.9 slice.156
  19.5 2.2 %fusion.4 = f32[208,3072]{1,0:T(8,128)S(1)} fusion(bf16[208,1536]{0,1:T(8,128)(2,1)S(1)} %pad_maximum_fusion.7, bf16[1536,6144]{1,0:T(8,128)(2,1)S(1)} %copy-done), kind=kOutput, calls=%fused_computation.4 | convolution fusion | flops 1962934272 | bytes 12779520 | tf_op jit(solution)/shard_map/dot_general | solution.py:22
  21.7 0.9 slice.159
  22.8 2.2 %fusion = f32[208,3072]{1,0:T(8,128)S(1)} fusion(bf16[208,1536]{0,1:T(8,128)(2,1)S(1)} %pad_maximum_fusion.7, bf16[1536,6144]{1,0:T(8,128)(2,1)S(1)} %copy-done), kind=kOutput, calls=%fused_computation | convolution fusion | flops 1962934272 | bytes 12779520 | tf_op jit(solution)/shard_map/dot_general | solution.py:22
  25.6 0.7 copy-done.11
  26.7 0.9 maximum_bitcast_fusion.x_ref
  27.6 1.6 fusion.36
  29.2 2.9 %collective-permute-start.15 = (bf16[104,3072]{1,0:T(8,128)(2,1)S(1)}, bf16[104,3072]{1,0:T(8,128)(2,1)S(1)}, u32[]{:S(2)}, u32[]{:S(2)}) collective-permute-start(bf16[104,3072]{1,0:T(8,128)(2,1)S(1)} %fusion.36), channel_id=1, source_target_pairs={{0,2},{2,0},{1,3},{3,1},{4,6},{6,4},{5,7},{7,5},{8,10},{10,8},{9,1... | collective-permute-start | bytes 1916936 | tf_op jit(solution)/shard_map/ppermute | solution.py:29
  32.4 1.2 fusion.34
  33.6 2.1 %collective-permute-start.2 = (bf16[112,3072]{1,0:T(8,128)(2,1)S(1)}, bf16[112,3072]{1,0:T(8,128)(2,1)S(1)}, u32[]{:S(2)}, u32[]{:S(2)}) collective-permute-start(bf16[112,3072]{1,0:T(8,128)(2,1)S(1)} %fusion.34), channel_id=1, source_target_pairs={{0,2},{2,0},{1,3},{3,1},{4,6},{6,4},{5,7},{7,5},{8,10},{10,8},{9,1... | collective-permute-start | bytes 2064392 | tf_op jit(solution)/shard_map/ppermute | solution.py:29
  35.7 1.2 fusion.35
  37.2 10.1 %collective-permute-done.15 = bf16[104,3072]{1,0:T(8,128)(2,1)S(1)} collective-permute-done((bf16[104,3072]{1,0:T(8,128)(2,1)S(1)}, bf16[104,3072]{1,0:T(8,128)(2,1)S(1)}, u32[]{:S(2)}, u32[]{:S(2)}) %collective-permute-start.15) | collective-permute-done | bytes 639008 | tf_op jit(solution)/shard_map/ppermute | solution.py:29
  47.3 13.7 %collective-permute-done.17 = bf16[104,3072]{1,0:T(8,128)(2,1)S(1)} collective-permute-done((bf16[104,3072]{1,0:T(8,128)(2,1)S(1)}, bf16[104,3072]{1,0:T(8,128)(2,1)S(1)}, u32[]{:S(2)}, u32[]{:S(2)}) %collective-permute-start.17) | collective-permute-done | bytes 639008 | tf_op jit(solution)/shard_map/ppermute | solution.py:29
  61.0 2.5 %fusion.33 = (bf16[104,3072]{1,0:T(8,128)(2,1)S(1)}, bf16[104,3072]{1,0:T(8,128)(2,1)S(1)}) fusion(bf16[104,3072]{1,0:T(8,128)(2,1)S(1)} %collective-permute-done.17, bf16[104,3072]{1,0:T(8,128)(2,1)S(1)} %collective-permute-done.16, f32[208,3072]{1,0:T(8,128)S(1)} %copy-done.9, bf16[216,6144]{1,0:T(8,128)(2,1)S(1)} %copy-done.14, ...), kind=kLoop, calls=%fused_computation.52 | loop fusion | flops 9584640 | bytes 7667712 | tf_op jit(solution)/shard_map/convert_element_type | solution.py:166
  63.6 0.5 collective-permute-start.18
  64.1 11.6 %collective-permute-done.2 = bf16[112,3072]{1,0:T(8,128)(2,1)S(1)} collective-permute-done((bf16[112,3072]{1,0:T(8,128)(2,1)S(1)}, bf16[112,3072]{1,0:T(8,128)(2,1)S(1)}, u32[]{:S(2)}, u32[]{:S(2)}) %collective-permute-start.2) | collective-permute-done | bytes 688160 | tf_op jit(solution)/shard_map/ppermute | solution.py:29
  75.8 14.3 %collective-permute-done.4 = bf16[112,3072]{1,0:T(8,128)(2,1)S(1)} collective-permute-done((bf16[112,3072]{1,0:T(8,128)(2,1)S(1)}, bf16[112,3072]{1,0:T(8,128)(2,1)S(1)}, u32[]{:S(2)}, u32[]{:S(2)}) %collective-permute-start.4) | collective-permute-done | bytes 688160 | tf_op jit(solution)/shard_map/ppermute | solution.py:29
  90.0 2.7 %fusion.20 = (bf16[112,3072]{1,0:T(8,128)(2,1)S(1)}, bf16[112,3072]{1,0:T(8,128)(2,1)S(1)}) fusion(bf16[112,3072]{1,0:T(8,128)(2,1)S(1)} %collective-permute-done.4, bf16[112,3072]{1,0:T(8,128)(2,1)} %collective-permute-done.3, f32[224,3072]{1,0:T(8,128)S(1)} %fusion.2, bf16[216,6144]{1,0:T(8,128)(2,1)S(1)} %copy-done.14, ...), kind=kLoop, calls=%fused_computation.34 | loop fusion | flops 10321920 | bytes 8257536 | tf_op jit(solution)/shard_map/convert_element_type | solution.py:166
  92.8 0.5 collective-permute-start.5
  93.8 0.8 slice-done.4
  94.6 8.7 %shard_map.60 = f32[208,1536]{1,0:T(8,128)S(1)} custom-call(bf16[208,6144]{1,0:T(8,128)(2,1)S(1)} %pad_maximum_fusion.2.g_ref, bf16[1536,6144]{1,0:T(8,128)(2,1)S(1)} %bitcast.6), custom_call_target="tpu_custom_call" | custom-call | flops 3925868544 | bytes 18874368 | tf_op jit(solution)/shard_map/pallas_call | solution.py:77
  103.3 0.8 slice.161
  104.5 0.7 copy-done.3
  105.5 9.6 %pad_maximum_fusion.g_ref = bf16[432,6144]{1,0:T(8,128)(2,1)S(1)} fusion(bf16[104,6144]{1,0:T(8,128)(2,1)S(1)} %constant_dynamic-update-slice_fusion.2, bf16[104,3072]{1,0:T(8,128)(2,1)S(1)} %copy-done.5, bf16[104,3072]{1,0:T(8,128)(2,1)S(1)} %copy-done.7, bf16[112,6144]{1,0:T(8,128)(2,1)S(1)} %constant_dynamic-update-slice_fusion, ...), kind=kLoop, calls=%fused_computation.8 | loop fusion | flops 31850496 | bytes 10616832 | tf_op jit(solution)/shard_map/concatenate | solution.py:184
  115.4 6.4 %copy-done.1 = bf16[1536,6144]{1,0:T(8,128)(2,1)S(1)} copy-done((bf16[1536,6144]{1,0:T(8,128)(2,1)S(1)}, bf16[1536,6144]{1,0:T(8,128)(2,1)}, u32[]{:S(2)}) %copy-start.1) | copy-done | bytes 18874392
  121.8 8.6 %shard_map.59 = f32[224,1536]{1,0:T(8,128)S(1)} custom-call(bf16[224,6144]{1,0:T(8,128)(2,1)S(1)} %pad_maximum_fusion.1.g_ref, bf16[1536,6144]{1,0:T(8,128)(2,1)S(1)} %copy-done.1), custom_call_target="tpu_custom_call" | custom-call | flops 4227858432 | bytes 18874368 | tf_op jit(solution)/shard_map/pallas_call | solution.py:77
  131.0 1.9 collective-permute-start.21
  132.9 2.1 %collective-permute-start.23 = (bf16[104,768]{1,0:T(8,128)(2,1)S(1)}, bf16[104,768]{1,0:T(8,128)(2,1)S(1)}, u32[]{:S(2)}, u32[]{:S(2)}) collective-permute-start(bf16[104,768]{1,0:T(8,128)(2,1)S(1)} %get-tuple-element.24), channel_id=1, source_target_pairs={{0,12},{4,0},{8,4},{12,8},{1,13},{5,1},{9,5},{13,9},{2,14},{6,2},{... | collective-permute-start | bytes 479240 | tf_op jit(solution)/shard_map/ppermute | solution.py:45
  135.0 0.9 collective-permute-start.22
  135.9 13.5 %shard_map.61.rest_0_ = bf16[1536,6144]{1,0:T(8,128)(2,1)} custom-call(bf16[1536,432]{1,0:T(8,128)(2,1)S(1)} %maximum_bitcast_fusion.x_ref, bf16[432,6144]{1,0:T(8,128)(2,1)S(1)} %pad_maximum_fusion.g_ref, bf16[1536,6144]{1,0:T(8,128)(2,1)} %w_ref.7, bf16[1536,6144]{1,0:T(8,128)(2,1)} %s_ref.3), custom_call_target="tpu_custom_call" | custom-call | flops 4076863488 | bytes 28311552 | tf_op jit(solution)/shard_map/pallas_call | solution.py:121
  149.8 1.4 collective-permute-start.24
  151.5 1.0 collective-permute-start.8
  152.6 2.9 %collective-permute-start.10 = (bf16[112,768]{1,0:T(8,128)(2,1)S(1)}, bf16[112,768]{1,0:T(8,128)(2,1)S(1)}, u32[]{:S(2)}, u32[]{:S(2)}) collective-permute-start(bf16[112,768]{1,0:T(8,128)(2,1)S(1)} %get-tuple-element.21), channel_id=1, source_target_pairs={{0,12},{4,0},{8,4},{12,8},{1,13},{5,1},{9,5},{13,9},{2,14},{6,2},{... | collective-permute-start | bytes 516104 | tf_op jit(solution)/shard_map/ppermute | solution.py:45
  155.4 13.5 %shard_map.62 = bf16[1536,6144]{1,0:T(8,128)(2,1)} custom-call(bf16[1536,432]{1,0:T(8,128)(2,1)S(1)} %maximum_bitcast_fusion.x_ref, bf16[432,6144]{1,0:T(8,128)(2,1)S(1)} %pad_maximum_fusion.g_ref, bf16[1536,6144]{1,0:T(8,128)(2,1)} %w_ref.7, bf16[1536,6144]{1,0:T(8,128)(2,1)} %s_ref.3, ...), custom_call_target="tpu_custom_call", output_to_operand_aliasing={{}: (4, {})} | custom-call | flops 4076863488 | bytes 28311552 | tf_op jit(solution)/shard_map/pallas_call | solution.py:121
  168.9 2.9 %collective-permute-start.25 = (bf16[104,768]{1,0:T(8,128)(2,1)S(1)}, bf16[104,768]{1,0:T(8,128)(2,1)S(1)}, u32[]{:S(2)}, u32[]{:S(2)}) collective-permute-start(bf16[104,768]{1,0:T(8,128)(2,1)S(1)} %get-tuple-element.11), channel_id=1, source_target_pairs={{0,8},{4,12},{8,0},{12,4},{1,9},{5,13},{9,1},{13,5},{2,10},{6,14},... | collective-permute-start | bytes 479240 | tf_op jit(solution)/shard_map/ppermute | solution.py:51
  171.9 0.7 collective-permute-start.26
  172.6 1.8 collective-permute-done.9
  174.7 10.3 %collective-permute-done.25 = bf16[104,768]{1,0:T(8,128)(2,1)S(1)} collective-permute-done((bf16[104,768]{1,0:T(8,128)(2,1)S(1)}, bf16[104,768]{1,0:T(8,128)(2,1)S(1)}, u32[]{:S(2)}, u32[]{:S(2)}) %collective-permute-start.25) | collective-permute-done | bytes 159776 | tf_op jit(solution)/shard_map/ppermute | solution.py:51
  185.2 8.8 %collective-permute-done.12 = bf16[112,768]{1,0:T(8,128)(2,1)S(1)} collective-permute-done((bf16[112,768]{1,0:T(8,128)(2,1)S(1)}, bf16[112,768]{1,0:T(8,128)(2,1)S(1)}, u32[]{:S(2)}, u32[]{:S(2)}) %collective-permute-start.12) | collective-permute-done | bytes 172064 | tf_op jit(solution)/shard_map/ppermute | solution.py:51
  194.0 3.5 %collective-permute-done.13 = bf16[112,768]{1,0:T(8,128)(2,1)S(1)} collective-permute-done((bf16[112,768]{1,0:T(8,128)(2,1)S(1)}, bf16[112,768]{1,0:T(8,128)(2,1)S(1)}, u32[]{:S(2)}, u32[]{:S(2)}) %collective-permute-start.13) | collective-permute-done | bytes 172064 | tf_op jit(solution)/shard_map/ppermute | solution.py:51
  197.5 1.2 pad_maximum_fusion.5
  (105 shorter events, 7.5 us)
Async XLA Ops:
  0.6 2.5 %copy-start.15 = (bf16[216,3072]{1,0:T(8,128)(2,1)S(1)}, bf16[216,3072]{1,0:T(8,128)(2,1)}, u32[]{:S(2)}) copy-start(bf16[216,3072]{1,0:T(8,128)(2,1)} %param.4) | copy-start | bytes 3981316
  2.7 2.4 %collective-permute-start = (bf16[216,1536]{1,0:T(8,128)(2,1)}, bf16[216,1536]{1,0:T(8,128)(2,1)S(1)}, u32[]{:S(2)}, u32[]{:S(2)}) collective-permute-start(bf16[216,1536]{1,0:T(8,128)(2,1)} %constant_dynamic-slice_fusion.7), channel_id=1, source_target_pairs={{0,1},{1,0},{2,3},{3,2},{4,5},{5,4},{6,7},{7,6},{8,9},{9,8},{10,11... | collective-permute-start | bytes 1990664 | tf_op jit(solution)/shard_map/ppermute | solution.py:18
  5.4 0.8 copy-start.10
  5.6 13.5 %copy-start.12 = (bf16[104,1536]{0,1:T(8,128)(2,1)}, bf16[104,1536]{0,1:T(8,128)(2,1)S(1)}, u32[]{:S(2)}) copy-start(bf16[104,1536]{0,1:T(8,128)(2,1)S(1)} %copy.16) | copy-start | bytes 958468
  6.1 9.3 %copy-start = (bf16[1536,6144]{1,0:T(8,128)(2,1)S(1)}, bf16[1536,6144]{1,0:T(8,128)(2,1)}, u32[]{:S(2)}) copy-start(bf16[1536,6144]{1,0:T(8,128)(2,1)} %w_ref.7) | copy-start | bytes 56623108
  13.3 19.0 %collective-permute-start.1 = (bf16[112,3072]{1,0:T(8,128)(2,1)}, bf16[112,3072]{1,0:T(8,128)(2,1)}, u32[]{:S(2)}, u32[]{:S(2)}) collective-permute-start(bf16[112,3072]{1,0:T(8,128)(2,1)} %slice.157), channel_id=1, source_target_pairs={{0,1},{1,0},{2,3},{3,2},{4,5},{5,4},{6,7},{7,6},{8,9},{9,8},{10,11... | collective-permute-start | bytes 2064392 | tf_op jit(solution)/shard_map/ppermute | solution.py:18
  18.8 16.9 %collective-permute-start.3 = (bf16[112,3072]{1,0:T(8,128)(2,1)}, bf16[112,3072]{1,0:T(8,128)(2,1)}, u32[]{:S(2)}, u32[]{:S(2)}) collective-permute-start(bf16[112,3072]{1,0:T(8,128)(2,1)} %slice.156), channel_id=1, source_target_pairs={{0,1},{1,0},{2,3},{3,2},{4,5},{5,4},{6,7},{7,6},{8,9},{9,8},{10,11... | collective-permute-start | bytes 2064392 | tf_op jit(solution)/shard_map/ppermute | solution.py:18
  22.6 4.9 %collective-permute-start.14 = (bf16[104,3072]{1,0:T(8,128)(2,1)}, bf16[104,3072]{1,0:T(8,128)(2,1)}, u32[]{:S(2)}, u32[]{:S(2)}) collective-permute-start(bf16[104,3072]{1,0:T(8,128)(2,1)} %slice.159), channel_id=1, source_target_pairs={{0,1},{1,0},{2,3},{3,2},{4,5},{5,4},{6,7},{7,6},{8,9},{9,8},{10,11... | collective-permute-start | bytes 1916936 | tf_op jit(solution)/shard_map/ppermute | solution.py:18
  25.0 7.2 %copy-start.8 = (f32[208,3072]{1,0:T(8,128)}, f32[208,3072]{1,0:T(8,128)S(1)}, u32[]{:S(2)}) copy-start(f32[208,3072]{1,0:T(8,128)S(1)} %fusion) | copy-start | bytes 7667716
  25.0 1.3 copy-start.11
  25.0 1.7 copy-start.13
  25.1 7.1 %collective-permute-start.16 = (bf16[104,3072]{1,0:T(8,128)(2,1)S(1)}, bf16[104,3072]{1,0:T(8,128)(2,1)S(1)}, u32[]{:S(2)}, u32[]{:S(2)}) collective-permute-start(bf16[104,3072]{1,0:T(8,128)(2,1)S(1)} %slice.158), channel_id=1, source_target_pairs={{0,1},{1,0},{2,3},{3,2},{4,5},{5,4},{6,7},{7,6},{8,9},{9,8},{10,11... | collective-permute-start | bytes 1916936 | tf_op jit(solution)/shard_map/ppermute | solution.py:18
  26.7 67.0 %slice-start = ((s8[18874368]{0:T(1024)(128)(4,1)}), s8[4194304]{0:T(1024)(128)(4,1)S(1)}, s32[]{:S(2)}) async-start(s8[18874368]{0:T(1024)(128)(4,1)} %bitcast.5), calls=%async_computation | async-start | bytes 8388608
  27.6 33.5 %copy-start.14 = (bf16[216,6144]{1,0:T(8,128)(2,1)S(1)}, bf16[216,6144]{1,0:T(8,128)(2,1)}, u32[]{:S(2)}) copy-start(bf16[216,6144]{1,0:T(8,128)(2,1)} %param.5) | copy-start | bytes 7962628
  29.2 64.5 %slice-start.1 = ((s8[18874368]{0:T(1024)(128)(4,1)}), s8[4194304]{0:T(1024)(128)(4,1)S(1)}, s32[]{:S(2)}) async-start(s8[18874368]{0:T(1024)(128)(4,1)} %bitcast.5), calls=%async_computation.1 | async-start | bytes 8388608
  29.2 18.1 %collective-permute-start.15 = (bf16[104,3072]{1,0:T(8,128)(2,1)S(1)}, bf16[104,3072]{1,0:T(8,128)(2,1)S(1)}, u32[]{:S(2)}, u32[]{:S(2)}) collective-permute-start(bf16[104,3072]{1,0:T(8,128)(2,1)S(1)} %fusion.36), channel_id=1, source_target_pairs={{0,2},{2,0},{1,3},{3,1},{4,6},{6,4},{5,7},{7,5},{8,10},{10,8},{9,1... | collective-permute-start | bytes 1916936 | tf_op jit(solution)/shard_map/ppermute | solution.py:29
  32.3 28.7 %collective-permute-start.17 = (bf16[104,3072]{1,0:T(8,128)(2,1)S(1)}, bf16[104,3072]{1,0:T(8,128)(2,1)S(1)}, u32[]{:S(2)}, u32[]{:S(2)}) collective-permute-start(bf16[104,3072]{1,0:T(8,128)(2,1)S(1)} %fusion.37), channel_id=1, source_target_pairs={{0,2},{2,0},{1,3},{3,1},{4,6},{6,4},{5,7},{7,5},{8,10},{10,8},{9,1... | collective-permute-start | bytes 1916936 | tf_op jit(solution)/shard_map/ppermute | solution.py:29
  33.6 27.4 %copy-start.9 = (f32[208,3072]{1,0:T(8,128)S(1)}, f32[208,3072]{1,0:T(8,128)}, u32[]{:S(2)}) copy-start(f32[208,3072]{1,0:T(8,128)} %copy-done.8) | copy-start | bytes 7667716
  33.6 42.1 %collective-permute-start.2 = (bf16[112,3072]{1,0:T(8,128)(2,1)S(1)}, bf16[112,3072]{1,0:T(8,128)(2,1)S(1)}, u32[]{:S(2)}, u32[]{:S(2)}) collective-permute-start(bf16[112,3072]{1,0:T(8,128)(2,1)S(1)} %fusion.34), channel_id=1, source_target_pairs={{0,2},{2,0},{1,3},{3,1},{4,6},{6,4},{5,7},{7,5},{8,10},{10,8},{9,1... | collective-permute-start | bytes 2064392 | tf_op jit(solution)/shard_map/ppermute | solution.py:29
  37.0 56.8 %slice-start.2 = ((s8[18874368]{0:T(1024)(128)(4,1)}), s8[4194304]{0:T(1024)(128)(4,1)S(1)}, s32[]{:S(2)}) async-start(s8[18874368]{0:T(1024)(128)(4,1)} %bitcast.5), calls=%async_computation.2 | async-start | bytes 8388608
  37.0 53.1 %collective-permute-start.4 = (bf16[112,3072]{1,0:T(8,128)(2,1)S(1)}, bf16[112,3072]{1,0:T(8,128)(2,1)S(1)}, u32[]{:S(2)}, u32[]{:S(2)}) collective-permute-start(bf16[112,3072]{1,0:T(8,128)(2,1)S(1)} %fusion.35), channel_id=1, source_target_pairs={{0,2},{2,0},{1,3},{3,1},{4,6},{6,4},{5,7},{7,5},{8,10},{10,8},{9,1... | collective-permute-start | bytes 2064392 | tf_op jit(solution)/shard_map/ppermute | solution.py:29
  63.5 29.9 %copy-start.4 = (bf16[104,3072]{1,0:T(8,128)(2,1)}, bf16[104,3072]{1,0:T(8,128)(2,1)S(1)}, u32[]{:S(2)}) copy-start(bf16[104,3072]{1,0:T(8,128)(2,1)S(1)} %get-tuple-element.14) | copy-start | bytes 1916932
  63.5 29.9 %copy-start.6 = (bf16[104,3072]{1,0:T(8,128)(2,1)}, bf16[104,3072]{1,0:T(8,128)(2,1)S(1)}, u32[]{:S(2)}) copy-start(bf16[104,3072]{1,0:T(8,128)(2,1)S(1)} %get-tuple-element.15) | copy-start | bytes 1916932
  63.6 29.8 %collective-permute-start.19 = (bf16[104,3072]{1,0:T(8,128)(2,1)S(1)}, bf16[104,3072]{1,0:T(8,128)(2,1)S(1)}, u32[]{:S(2)}, u32[]{:S(2)}) collective-permute-start(bf16[104,3072]{1,0:T(8,128)(2,1)S(1)} %get-tuple-element.14), channel_id=1, source_target_pairs={{0,1},{1,0},{2,3},{3,2},{4,5},{5,4},{6,7},{7,6},{8,9},{9,8},{10,11... | collective-permute-start | bytes 1916936 | tf_op jit(solution)/shard_map/ppermute | solution.py:18
  63.6 30.1 %slice-start.3 = ((s8[18874368]{0:T(1024)(128)(4,1)}), s8[4194304]{0:T(1024)(128)(4,1)S(1)}, s32[]{:S(2)}) async-start(s8[18874368]{0:T(1024)(128)(4,1)} %bitcast.5), calls=%async_computation.3 | async-start | bytes 8388608
  63.6 29.7 %collective-permute-start.18 = (bf16[104,3072]{1,0:T(8,128)(2,1)S(1)}, bf16[104,3072]{1,0:T(8,128)(2,1)S(1)}, u32[]{:S(2)}, u32[]{:S(2)}) collective-permute-start(bf16[104,3072]{1,0:T(8,128)(2,1)S(1)} %get-tuple-element.15), channel_id=1, source_target_pairs={{0,1},{1,0},{2,3},{3,2},{4,5},{5,4},{6,7},{7,6},{8,9},{9,8},{10,11... | collective-permute-start | bytes 1916936 | tf_op jit(solution)/shard_map/ppermute | solution.py:18
  92.7 1.0 copy-start.2
  92.8 11.7 %collective-permute-start.6 = (bf16[112,3072]{1,0:T(8,128)(2,1)S(1)}, bf16[112,3072]{1,0:T(8,128)(2,1)S(1)}, u32[]{:S(2)}, u32[]{:S(2)}) collective-permute-start(bf16[112,3072]{1,0:T(8,128)(2,1)S(1)} %get-tuple-element.12), channel_id=1, source_target_pairs={{0,1},{1,0},{2,3},{3,2},{4,5},{5,4},{6,7},{7,6},{8,9},{9,8},{10,11... | collective-permute-start | bytes 2064392 | tf_op jit(solution)/shard_map/ppermute | solution.py:18
  92.8 1.8 slice-start.4
  92.8 11.5 %collective-permute-start.5 = (bf16[112,3072]{1,0:T(8,128)(2,1)S(1)}, bf16[112,3072]{1,0:T(8,128)(2,1)S(1)}, u32[]{:S(2)}, u32[]{:S(2)}) collective-permute-start(bf16[112,3072]{1,0:T(8,128)(2,1)S(1)} %get-tuple-element.13), channel_id=1, source_target_pairs={{0,1},{1,0},{2,3},{3,2},{4,5},{5,4},{6,7},{7,6},{8,9},{9,8},{10,11... | collective-permute-start | bytes 2064392 | tf_op jit(solution)/shard_map/ppermute | solution.py:18
  104.0 1.1 copy-start.3
  104.0 1.3 copy-start.5
  104.1 1.5 copy-start.7
  104.1 26.7 %collective-permute-start.20 = (bf16[104,1536]{1,0:T(8,128)(2,1)}, bf16[104,1536]{1,0:T(8,128)(2,1)S(1)}, u32[]{:S(2)}, u32[]{:S(2)}) collective-permute-start(bf16[104,1536]{1,0:T(8,128)(2,1)} %slice.161), channel_id=1, source_target_pairs={{0,1},{1,0},{2,3},{3,2},{4,5},{5,4},{6,7},{7,6},{8,9},{9,8},{10,11... | collective-permute-start | bytes 958472 | tf_op jit(solution)/shard_map/ppermute | solution.py:18
  115.4 6.4 %copy-start.1 = (bf16[1536,6144]{1,0:T(8,128)(2,1)S(1)}, bf16[1536,6144]{1,0:T(8,128)(2,1)}, u32[]{:S(2)}) copy-start(bf16[1536,6144]{1,0:T(8,128)(2,1)} %w_ref.7) | copy-start | bytes 56623108
  130.4 20.9 %collective-permute-start.7 = (bf16[112,1536]{1,0:T(8,128)(2,1)S(1)}, bf16[112,1536]{1,0:T(8,128)(2,1)S(1)}, u32[]{:S(2)}, u32[]{:S(2)}) collective-permute-start(bf16[112,1536]{1,0:T(8,128)(2,1)S(1)} %slice.160), channel_id=1, source_target_pairs={{0,1},{1,0},{2,3},{3,2},{4,5},{5,4},{6,7},{7,6},{8,9},{9,8},{10,11... | collective-permute-start | bytes 1032200 | tf_op jit(solution)/shard_map/ppermute | solution.py:18
  131.0 18.4 %collective-permute-start.21 = (bf16[104,768]{1,0:T(8,128)(2,1)S(1)}, bf16[104,768]{1,0:T(8,128)(2,1)S(1)}, u32[]{:S(2)}, u32[]{:S(2)}) collective-permute-start(bf16[104,768]{1,0:T(8,128)(2,1)S(1)} %get-tuple-element.23), channel_id=1, source_target_pairs={{0,4},{4,8},{8,12},{12,0},{1,5},{5,9},{9,13},{13,1},{2,6},{6,10},{... | collective-permute-start | bytes 479240 | tf_op jit(solution)/shard_map/ppermute | solution.py:45
  132.9 16.5 %collective-permute-start.23 = (bf16[104,768]{1,0:T(8,128)(2,1)S(1)}, bf16[104,768]{1,0:T(8,128)(2,1)S(1)}, u32[]{:S(2)}, u32[]{:S(2)}) collective-permute-start(bf16[104,768]{1,0:T(8,128)(2,1)S(1)} %get-tuple-element.24), channel_id=1, source_target_pairs={{0,12},{4,0},{8,4},{12,8},{1,13},{5,1},{9,5},{13,9},{2,14},{6,2},{... | collective-permute-start | bytes 479240 | tf_op jit(solution)/shard_map/ppermute | solution.py:45
  135.0 14.7 %collective-permute-start.22 = (bf16[104,768]{1,0:T(8,128)(2,1)S(1)}, bf16[104,768]{1,0:T(8,128)(2,1)S(1)}, u32[]{:S(2)}, u32[]{:S(2)}) collective-permute-start(bf16[104,768]{1,0:T(8,128)(2,1)S(1)} %get-tuple-element.25), channel_id=1, source_target_pairs={{0,8},{4,12},{8,0},{12,4},{1,9},{5,13},{9,1},{13,5},{2,10},{6,14},... | collective-permute-start | bytes 479240 | tf_op jit(solution)/shard_map/ppermute | solution.py:45
  149.8 22.0 %collective-permute-start.24 = (bf16[104,768]{1,0:T(8,128)(2,1)S(1)}, bf16[104,768]{1,0:T(8,128)(2,1)S(1)}, u32[]{:S(2)}, u32[]{:S(2)}) collective-permute-start(bf16[104,768]{1,0:T(8,128)(2,1)S(1)} %get-tuple-element.11), channel_id=1, source_target_pairs={{0,4},{4,8},{8,12},{12,0},{1,5},{5,9},{9,13},{13,1},{2,6},{6,10},{... | collective-permute-start | bytes 479240 | tf_op jit(solution)/shard_map/ppermute | solution.py:51
  151.5 21.0 %collective-permute-start.8 = (bf16[112,768]{1,0:T(8,128)(2,1)S(1)}, bf16[112,768]{1,0:T(8,128)(2,1)S(1)}, u32[]{:S(2)}, u32[]{:S(2)}) collective-permute-start(bf16[112,768]{1,0:T(8,128)(2,1)S(1)} %get-tuple-element.20), channel_id=1, source_target_pairs={{0,4},{4,8},{8,12},{12,0},{1,5},{5,9},{9,13},{13,1},{2,6},{6,10},{... | collective-permute-start | bytes 516104 | tf_op jit(solution)/shard_map/ppermute | solution.py:45
  152.6 20.0 %collective-permute-start.10 = (bf16[112,768]{1,0:T(8,128)(2,1)S(1)}, bf16[112,768]{1,0:T(8,128)(2,1)S(1)}, u32[]{:S(2)}, u32[]{:S(2)}) collective-permute-start(bf16[112,768]{1,0:T(8,128)(2,1)S(1)} %get-tuple-element.21), channel_id=1, source_target_pairs={{0,12},{4,0},{8,4},{12,8},{1,13},{5,1},{9,5},{13,9},{2,14},{6,2},{... | collective-permute-start | bytes 516104 | tf_op jit(solution)/shard_map/ppermute | solution.py:45
  155.4 19.0 %collective-permute-start.9 = (bf16[112,768]{1,0:T(8,128)(2,1)S(1)}, bf16[112,768]{1,0:T(8,128)(2,1)S(1)}, u32[]{:S(2)}, u32[]{:S(2)}) collective-permute-start(bf16[112,768]{1,0:T(8,128)(2,1)S(1)} %get-tuple-element.22), channel_id=1, source_target_pairs={{0,8},{4,12},{8,0},{12,4},{1,9},{5,13},{9,1},{13,5},{2,10},{6,14},... | collective-permute-start | bytes 516104 | tf_op jit(solution)/shard_map/ppermute | solution.py:45
  168.9 16.0 %collective-permute-start.25 = (bf16[104,768]{1,0:T(8,128)(2,1)S(1)}, bf16[104,768]{1,0:T(8,128)(2,1)S(1)}, u32[]{:S(2)}, u32[]{:S(2)}) collective-permute-start(bf16[104,768]{1,0:T(8,128)(2,1)S(1)} %get-tuple-element.11), channel_id=1, source_target_pairs={{0,8},{4,12},{8,0},{12,4},{1,9},{5,13},{9,1},{13,5},{2,10},{6,14},... | collective-permute-start | bytes 479240 | tf_op jit(solution)/shard_map/ppermute | solution.py:51
  171.9 13.2 %collective-permute-start.26 = (bf16[104,768]{1,0:T(8,128)(2,1)S(1)}, bf16[104,768]{1,0:T(8,128)(2,1)S(1)}, u32[]{:S(2)}, u32[]{:S(2)}) collective-permute-start(bf16[104,768]{1,0:T(8,128)(2,1)S(1)} %get-tuple-element.11), channel_id=1, source_target_pairs={{0,12},{4,0},{8,4},{12,8},{1,13},{5,1},{9,5},{13,9},{2,14},{6,2},{... | collective-permute-start | bytes 479240 | tf_op jit(solution)/shard_map/ppermute | solution.py:51
  174.6 10.5 %collective-permute-start.11 = (bf16[112,768]{1,0:T(8,128)(2,1)S(1)}, bf16[112,768]{1,0:T(8,128)(2,1)S(1)}, u32[]{:S(2)}, u32[]{:S(2)}) collective-permute-start(bf16[112,768]{1,0:T(8,128)(2,1)S(1)} %get-tuple-element.9), channel_id=1, source_target_pairs={{0,4},{4,8},{8,12},{12,0},{1,5},{5,9},{9,13},{13,1},{2,6},{6,10},{... | collective-permute-start | bytes 516104 | tf_op jit(solution)/shard_map/ppermute | solution.py:51
  185.0 9.0 %collective-permute-start.12 = (bf16[112,768]{1,0:T(8,128)(2,1)S(1)}, bf16[112,768]{1,0:T(8,128)(2,1)S(1)}, u32[]{:S(2)}, u32[]{:S(2)}) collective-permute-start(bf16[112,768]{1,0:T(8,128)(2,1)S(1)} %get-tuple-element.9), channel_id=1, source_target_pairs={{0,8},{4,12},{8,0},{12,4},{1,9},{5,13},{9,1},{13,5},{2,10},{6,14},... | collective-permute-start | bytes 516104 | tf_op jit(solution)/shard_map/ppermute | solution.py:51
  185.1 12.4 %collective-permute-start.13 = (bf16[112,768]{1,0:T(8,128)(2,1)S(1)}, bf16[112,768]{1,0:T(8,128)(2,1)S(1)}, u32[]{:S(2)}, u32[]{:S(2)}) collective-permute-start(bf16[112,768]{1,0:T(8,128)(2,1)S(1)} %get-tuple-element.9), channel_id=1, source_target_pairs={{0,12},{4,0},{8,4},{12,8},{1,13},{5,1},{9,5},{13,9},{2,14},{6,2},{... | collective-permute-start | bytes 516104 | tf_op jit(solution)/shard_map/ppermute | solution.py:51

commit v3 on v1

v3 whole, which is shorter than its diff:
```python
import functools

import jax
import jax.numpy as jnp
from jax import lax
from jax.experimental import pallas as pl
from jax.experimental.pallas import tpu as pltpu
from jax.sharding import PartitionSpec as P

BF = jnp.bfloat16
F32 = jnp.float32


def gelu_slope(pre):
    cdf = 0.5 * (1.0 + jax.scipy.special.erf(pre * 0.7071067811865476))
    return cdf + pre * jnp.exp(-0.5 * pre * pre) * 0.3989422804014327


def swap(x):
    return lax.ppermute(x, "tok", [(0, 1), (1, 0)])


def mm(a, b, dims):
    return lax.dot_general(a, b, (dims, ((), ())), preferred_element_type=F32)


def after(x, *others):
    return lax.optimization_barrier((x,) + others)[0]


def send_partial(part, n):
    if n == 2:
        return part, lax.ppermute(part.astype(BF), "in", [(0, 1), (1, 0)])
    return None, lax.psum(part, "in")


def direct(x, n):
    return 1 < n <= 8 and x.shape[1] % (128 * n) == 0


def scatter_out(x, n):
    w = x.shape[1] // n
    me = lax.axis_index("out")
    total = lax.dynamic_slice_in_dim(x, me * w, w, 1)
    xb = x.astype(BF)
    for k in range(1, n):
        to = lax.rem(me + k, n)
        piece = lax.dynamic_slice_in_dim(xb, to * w, w, 1)
        got = lax.ppermute(piece, "out", [(i, (i + k) % n) for i in range(n)])
        total = total + got.astype(F32)
    return total.astype(BF), xb


def gather_out(mine, n):
    w = mine.shape[1]
    me = lax.axis_index("out")
    out = jnp.zeros((mine.shape[0], w * n), BF)
    out = lax.dynamic_update_slice_in_dim(out, mine, me * w, 1)
    for k in range(1, n):
        got = lax.ppermute(mine, "out", [(i, (i + k) % n) for i in range(n)])
        out = lax.dynamic_update_slice_in_dim(out, got, lax.rem(me - k + n, n) * w, 1)
    return out


def block_of(n, sizes):
    for b in sizes:
        if n % b == 0:
            return b
    return n


def dx_kernel(m_ref, o_ref, w_ref, init_ref, sum_ref):
    @pl.when(pl.program_id(0) == 0)
    def _():
        sum_ref[...] = init_ref[...]

    g = jnp.concatenate([m_ref[...], o_ref[...]], axis=0)
    sum_ref[...] += lax.dot_general(
        g, w_ref[...], (((1,), (1,)), ((), ())), preferred_element_type=F32
    )


def dx_partial(mine, other, weight, start, unit, init):
    rows = weight.shape[0]
    m, width = mine.shape
    first = start // unit
    g_block = pl.BlockSpec((m, unit), lambda i: (0, i))
    whole = pl.BlockSpec((2 * m, rows), lambda i: (0, 0))
    return pl.pallas_call(
        dx_kernel,
        grid=(width // unit,),
        in_specs=[
            g_block,
            g_block,
            pl.BlockSpec((rows, unit), lambda i: (0, i + first)),
            whole,
        ],
        out_specs=whole,
        out_shape=jax.ShapeDtypeStruct((2 * m, rows), F32),
        cost_estimate=pl.CostEstimate(
            flops=4 * m * rows * width, bytes_accessed=2 * rows * width, transcendentals=0
        ),
        compiler_params=pltpu.CompilerParams(vmem_limit_bytes=32 * 2**20),
    )(mine, other, weight, init)


def score_kernel(parts, x_ref, *refs):
    g_refs, (w_ref, s_ref), o_ref = refs[:parts], refs[parts : parts + 2], refs[-1]
    rows = w_ref.shape[0]
    step = block_of(rows, (384, 256, 128))
    g = jnp.concatenate([ref[...] for ref in g_refs], axis=0)
    for r in range(0, rows, step):
        part = pl.ds(r, step)
        gw = jnp.dot(x_ref[part, :], g, preferred_element_type=F32)
        o_ref[part, :] = (
            s_ref[part, :].astype(F32) - w_ref[part, :].astype(F32) * gw
        ).astype(BF)


def score_part(x_t, gs, weight, score, start, w, earlier):
    rows, ff = weight.shape
    m, width = gs[0].shape
    first, count = start // w, width // w
    block = pl.BlockSpec((rows, w), lambda i: (0, i + first))
    specs = [pl.BlockSpec(x_t.shape, lambda i: (0, 0))]
    specs += [pl.BlockSpec((m, w), lambda i: (0, i)) for _ in gs]
    specs += [block, block]
    args = [x_t, *gs, weight, score]
    alias = {}
    if earlier is not None:
        alias = {len(args): 0}
        specs.append(pl.BlockSpec(memory_space=pl.ANY))
        args.append(earlier)
    return pl.pallas_call(
        functools.partial(score_kernel, len(gs)),
        grid=(count,),
        in_specs=specs,
        out_specs=block,
        out_shape=jax.ShapeDtypeStruct((rows, ff), BF),
        input_output_aliases=alias,
        cost_estimate=pl.CostEstimate(
            flops=2 * x_t.shape[1] * rows * width,
            bytes_accessed=6 * rows * width,
            transcendentals=0,
        ),
        compiler_params=pltpu.CompilerParams(vmem_limit_bytes=40 * 2**20),
    )(*args)


def make(n_in, n_out):
    def on_device(inputs, grad_act, weight, score):
        rows, ff = weight.shape
        tokens = inputs.shape[0]
        t = lax.axis_index("tok")
        cut = -(-tokens // 32) * 16
        pad = ((0, 2 * cut - tokens), (0, 0))
        spans = [(0, cut), (cut, tokens)]
        x_other = swap(lax.dynamic_slice_in_dim(inputs, (1 - t) * rows, rows, 1))
        x_mine = lax.dynamic_slice_in_dim(inputs, t * rows, rows, 1)
        unit = block_of(ff, (512, 256, 128))
        small = max(1, ff // unit // 4) * unit
        chunks = [(0, small), (small, ff)] if small < ff else [(0, ff)]
        sent = {}
        token = None
        for h, (lo, hi) in enumerate(spans):
            for a, b in chunks if h == 0 else chunks[::-1]:
                theirs, own = x_other[lo:hi], x_mine[lo:hi]
                if token is not None:
                    theirs = after(theirs, token)
                wc = weight[:, a:b]
                token = mm(theirs, wc, ((1,), (0,))).astype(BF)
                part = mm(own, wc, ((1,), (0,))) + swap(token).astype(F32)
                if not sent:
                    token = part
                sent[h, a] = send_partial(part, n_in)
        g_of, outs = {}, []
        waits = [[], []]
        for h, (lo, hi) in enumerate(spans):
            total = jnp.zeros((2 * cut, rows), F32)
            order = chunks if h == 0 else chunks[::-1]
            for i, (a, b) in enumerate(order):
                own, got = sent[h, a]
                if h == 1:
                    got = after(got, *waits[0 if i == 0 else 1])
                pre = got.astype(F32) if own is None else own + got.astype(F32)
                g = (grad_act[lo:hi, a:b].astype(F32) * gelu_slope(pre)).astype(BF)
                if hi - lo < cut:
                    g = jnp.pad(g, pad)
                g_of[h, a] = (g, swap(g))
                total = dx_partial(*g_of[h, a], weight, a, unit, total)
            mine, theirs = total[: hi - lo], total[cut : cut + hi - lo]
            got = swap(theirs.astype(BF)).astype(F32)
            left, right = jnp.where(t == 0, mine, got), jnp.where(t == 0, got, mine)
            term = jnp.concatenate([left, right], axis=1)
            if direct(term, n_out):
                piece, ready = scatter_out(term, n_out)
                waits = [[ready], [piece]]
                outs.append(gather_out(piece, n_out))
            else:
                waits = [[term], [term]]
                outs.append(lax.psum(term, "out").astype(BF))
        xs = []
        for lo, hi in spans:
            for x in (x_mine, x_other):
                xs.append(x[lo:hi] if hi - lo == cut else jnp.pad(x[lo:hi], pad))
        x_t = jnp.concatenate(xs, axis=0).T
        new_score = None
        for i, (a, b) in enumerate(chunks[::-1]):
            x_now = after(x_t, *waits[0 if i == 0 else 1])
            gs = [*g_of[0, a], *g_of[1, a]]
            new_score = score_part(x_now, gs, weight, score, a, unit, new_score)
        return jnp.concatenate(outs, axis=0), new_score

    return on_device


def solution(mesh):
    placed = (
        P(("group", "tok"), "in"),
        P(("group", "tok"), "out"),
        P(("in", "tok"), "out"),
        P(("in", "tok"), "out"),
    )
    return jax.shard_map(
        make(mesh.shape["in"], mesh.shape["out"]),
        mesh=mesh,
        in_specs=placed,
        out_specs=(P(("group", "tok"), "in"), P(("group", "in", "tok"), "out")),
        check_vma=False,
    )
```

time: 185 us -> 198 us (1.070)
  Pallas kernels: 0 us -> 55.1 us
  matrix products: 70.4 us -> 37.1 us
  waiting for transfers between devices: 80.3 us -> 47.7 us
  local copies, waits for them, and re-layouts: 4.17 us -> 20.7 us
  other arithmetic: 5.63 us -> 9.97 us
  starting transfers between devices: 23.9 us -> 25.9 us
    pallas_call x0 -> x6, Pallas kernels: none -> 55.1 us  [the longest x2 28.9 us: score_part(): pl.pallas_call(functools.partial(score_kernel, len(gs)), grid=(count,), i...]
    dot_general x11 -> x8, matrix products: 70.4 us -> 37.1 us  [mm(): return lax.dot_general(a, b, (dims, ((), ())), preferred_element_type=F32)]
    ppermute x10 -> x16, waiting for transfers between devices: 72.6 us -> 45.4 us  [the longest x4 31.3 us: send_partial(): return (part, lax.ppermute(part.astype(BF), 'in', [(0, 1), (1, 0)]))]
    unnamed x25 -> x35, local copies, waits for them, and re-layouts: 1.32 us -> 16.7 us
    ppermute x10 -> x11, waiting for transfers between devices: 7.71 us -> 2.25 us  [swap(): return lax.ppermute(x, 'tok', [(0, 1), (1, 0)])]
    convert_element_type x2 -> x7, other arithmetic: 3.37 us -> 7.37 us  [the longest x4 6.38 us: on_device(): g = (grad_act[lo:hi, a:b].astype(F32) * gelu_slope(pre)).astype(BF)]
    ppermute x10 -> x16, starting transfers between devices: 20.9 us -> 23.7 us  [the longest x6 9.56 us: scatter_out(): got = lax.ppermute(piece, 'out', [(i, (i + k) % n) for i in range(n)])]
    dynamic_update_slice x1 -> x2, other arithmetic: 2.26 us -> 0.25 us  [gather_out(): out = lax.dynamic_update_slice_in_dim(out, mine, me * w, 1)]
  transfers between devices with their start and end apart: 20 -> 27, of which waited for: 12 -> 9; matrix products, arithmetic and copies ran while one was open for 24% -> 16% of each run, Pallas kernels for 0% -> 28%
where the time goes in v3:
time: 198 us
  Pallas kernels  55.1 us (28%)
  waiting for transfers between devices  47.7 us (24%)
  matrix products  37.1 us (19%)
  starting transfers between devices  25.9 us (13%)
  local copies, waits for them, and re-layouts  20.7 us (10%)
  other arithmetic  9.97 us (5%)
    dot_general x8, matrix products, mm(): return lax.dot_general(a, b, (dims, ((), ())), preferred_element_type=F32)  37.1 us
    ppermute x4, waiting for transfers between devices, send_partial(): return (part, lax.ppermute(part.astype(BF), 'in', [(0, 1), (1, 0)]))  31.3 us
    pallas_call x2, Pallas kernels, score_part(): pl.pallas_call(functools.partial(score_kernel, len(gs)), grid=(count,), i...  28.9 us
    pallas_call x4, Pallas kernels, dx_partial(): pl.pallas_call(dx_kernel, grid=(width // unit,), in_specs=[g_block, g_blo...  26.3 us
    unnamed x35, local copies, waits for them, and re-layouts  16.7 us
    ppermute x6, waiting for transfers between devices, scatter_out(): got = lax.ppermute(piece, 'out', [(i, (i + k) % n) for i in range(n)])  10.4 us
    ppermute x6, starting transfers between devices, scatter_out(): got = lax.ppermute(piece, 'out', [(i, (i + k) % n) for i in range(n)])  9.56 us
    ppermute x4, starting transfers between devices, send_partial(): return (part, lax.ppermute(part.astype(BF), 'in', [(0, 1), (1, 0)]))  7.45 us
  transfers between devices with their start and end apart: 27, of which 9 were waited for; matrix products, arithmetic and copies ran while one was open for 16% of the time, Pallas kernels for 28%

profile of v3, /device:TPU:0, one launch (start us, length us, event | category | flops | bytes accessed | tf_op | source)
XLA Modules:
  0.0 197.7 jit_solution(11315359000867596672)
XLA Ops:
  0.6 1.1 constant_dynamic-slice_fusion.7
  2.3 1.0 constant_dynamic-slice_fusion
  4.0 3.2 %fusion.25 = bf16[112,1536]{1,0:T(8,128)(2,1)S(1)} fusion(bf16[1536,6144]{1,0:T(8,128)(2,1)} %refs_4_.3, bf16[216,1536]{1,0:T(8,128)(2,1)S(1)} %collective-permute-done), kind=kOutput, calls=%fused_computation.26 | convolution fusion | flops 528654336 | bytes 5406720 | tf_op jit(solution)/shard_map/dot_general | solution.py:24
  7.6 3.2 %fusion.23 = f32[112,1536]{1,0:T(8,128)S(1)} fusion(bf16[112,1536]{1,0:T(8,128)(2,1)S(1)} %constant_dynamic-slice_fusion, bf16[1536,6144]{1,0:T(8,128)(2,1)} %refs_4_.3), kind=kOutput, calls=%fused_computation.23 | convolution fusion | flops 528482304 | bytes 5750784 | tf_op jit(solution)/shard_map/dot_general | solution.py:24
  11.1 0.9 fusion.76
  11.9 8.2 %fusion.8 = bf16[112,4608]{1,0:T(8,128)(2,1)} fusion(bf16[112,1536]{0,1:T(8,128)(2,1)S(1)} %copy.14, bf16[1536,6144]{1,0:T(8,128)(2,1)} %refs_4_.3), kind=kOutput, calls=%fused_computation.8 | convolution fusion | flops 1585963008 | bytes 15532032 | tf_op jit(solution)/shard_map/dot_general | solution.py:24
  20.3 0.9 copy.13
  21.2 1.0 dynamic-slice.1
  22.2 0.9 copy.15
  23.1 0.8 slice.71
  23.9 1.3 copy.16
  25.3 7.6 %fusion.46 = (bf16[112,4608]{1,0:T(8,128)(2,1)S(1)}, f32[112,4608]{1,0:T(8,128)S(1)}) fusion(bf16[112,4608]{1,0:T(8,128)(2,1)} %collective-permute-done.2, bf16[112,1536]{1,0:T(8,128)(2,1)S(1)} %constant_dynamic-slice_fusion, bf16[1536,6144]{1,0:T(8,128)(2,1)} %refs_4_.3), kind=kOutput, calls=%fused_computation.51 | convolution fusion | flops 1586995200 | bytes 18628608 | tf_op jit(solution)/shard_map/dot_general | solution.py:24
  32.9 2.9 %collective-permute-start.3 = (bf16[112,4608]{1,0:T(8,128)(2,1)S(1)}, bf16[112,4608]{1,0:T(8,128)(2,1)S(1)}, u32[]{:S(2)}, u32[]{:S(2)}) collective-permute-start(bf16[112,4608]{1,0:T(8,128)(2,1)S(1)} %get-tuple-element.34), channel_id=1, source_target_pairs={{0,2},{2,0},{1,3},{3,1},{4,6},{6,4},{5,7},{7,5},{8,10},{10,8},{9,1... | collective-permute-start | bytes 3096584 | tf_op jit(solution)/shard_map/ppermute | solution.py:33
  35.8 3.5 %fusion.11 = bf16[104,4608]{1,0:T(8,128)(2,1)} fusion(bf16[104,1536]{0,1:T(8,128)(2,1)S(1)} %copy.16, bf16[1536,6144]{1,0:T(8,128)(2,1)S(1)} %bitcast.10), kind=kOutput, calls=%fused_computation.9 | convolution fusion | flops 1472679936 | bytes 15507456 | tf_op jit(solution)/shard_map/dot_general | solution.py:24
  39.3 2.4 %collective-permute-start.5 = (bf16[112,1536]{1,0:T(8,128)(2,1)S(1)}, bf16[112,1536]{1,0:T(8,128)(2,1)S(1)}, u32[]{:S(2)}, u32[]{:S(2)}) collective-permute-start(bf16[112,1536]{1,0:T(8,128)(2,1)S(1)} %copy-done.9), channel_id=1, source_target_pairs={{0,2},{2,0},{1,3},{3,1},{4,6},{6,4},{5,7},{7,5},{8,10},{10,8},{9,1... | collective-permute-start | bytes 1032200 | tf_op jit(solution)/shard_map/ppermute | solution.py:33
  41.7 0.9 fusion.28
  42.7 23.5 %collective-permute-done.5 = bf16[112,1536]{1,0:T(8,128)(2,1)S(1)} collective-permute-done((bf16[112,1536]{1,0:T(8,128)(2,1)S(1)}, bf16[112,1536]{1,0:T(8,128)(2,1)S(1)}, u32[]{:S(2)}, u32[]{:S(2)}) %collective-permute-start.5) | collective-permute-done | bytes 344096 | tf_op jit(solution)/shard_map/ppermute | solution.py:33
  66.7 2.3 %fusion.36.m_ref.refs_0_ = bf16[112,4608]{1,0:T(8,128)(2,1)S(1)} fusion(bf16[112,4608]{1,0:T(8,128)(2,1)S(1)} %collective-permute-done.3, f32[112,4608]{1,0:T(8,128)S(1)} %get-tuple-element.35, bf16[112,4608]{1,0:T(8,128)(2,1)} %collective-permute-done.2, bf16[216,6144]{1,0:T(8,128)(2,1)S(1)} %copy-done.2), kind=kLoop, calls=%fused_computation.33 | loop fusion | flops 7741440 | bytes 6193152 | tf_op jit(solution)/shard_map/convert_element_type | solution.py:186
  69.7 6.4 %copy-done = bf16[1536,6144]{1,0:T(8,128)(2,1)S(1)} copy-done((bf16[1536,6144]{1,0:T(8,128)(2,1)S(1)}, bf16[1536,6144]{1,0:T(8,128)(2,1)}, u32[]{:S(2)}) %copy-start) | copy-done | bytes 18874392
  76.1 2.5 %shard_map.59.init_ref = f32[224,1536]{1,0:T(8,128)S(1)} custom-call(bf16[112,1536]{1,0:T(8,128)(2,1)S(1)} %fusion.55.m_ref.refs_0_, bf16[112,1536]{1,0:T(8,128)(2,1)S(1)} %collective-permute-done.6.o_ref.refs_1_, bf16[1536,6144]{1,0:T(8,128)(2,1)S(1)} %copy-done, f32[224,1536]{1,0:T(8,128)S(1)} %broadcast_1_init_ref.2.init_ref), custom_call_target="tpu_custom_call" | custom-call | flops 1056964608 | bytes 4718592 | tf_op jit(solution)/shard_map/pallas_call | solution.py:89
  78.6 7.5 %fusion.48 = (bf16[104,4608]{1,0:T(8,128)(2,1)S(1)}, f32[104,4608]{1,0:T(8,128)S(1)}) fusion(bf16[104,4608]{1,0:T(8,128)(2,1)} %collective-permute-done.17, bf16[104,1536]{1,0:T(8,128)(2,1)S(1)} %copy-done.8, bf16[1536,6144]{1,0:T(8,128)(2,1)} %refs_4_.3), kind=kOutput, calls=%fused_computation.54 | convolution fusion | flops 1473638400 | bytes 18309120 | tf_op jit(solution)/shard_map/dot_general | solution.py:24
  86.1 1.8 collective-permute-start.18
  87.9 10.6 %shard_map.60 = f32[224,1536]{1,0:T(8,128)S(1)} custom-call(bf16[112,4608]{1,0:T(8,128)(2,1)S(1)} %fusion.36.m_ref.refs_0_, bf16[112,4608]{1,0:T(8,128)(2,1)S(1)} %collective-permute-done.4.o_ref.refs_1_, bf16[1536,6144]{1,0:T(8,128)(2,1)} %refs_4_.3, f32[224,1536]{1,0:T(8,128)S(1)} %shard_map.59.init_ref), custom_call_target="tpu_custom_call" | custom-call | flops 3170893824 | bytes 14155776 | tf_op jit(solution)/shard_map/pallas_call | solution.py:89
  98.7 3.2 %fusion.62 = (bf16[104,1536]{1,0:T(8,128)(2,1)S(1)}, f32[104,1536]{1,0:T(8,128)S(1)}) fusion(bf16[104,1536]{1,0:T(8,128)(2,1)S(1)} %collective-permute-done.14, bf16[104,1536]{1,0:T(8,128)(2,1)S(1)} %copy-done.8, bf16[1536,6144]{1,0:T(8,128)(2,1)} %refs_4_.3), kind=kOutput, calls=%fused_computation.78 | convolution fusion | flops 491212800 | bytes 6316032 | tf_op jit(solution)/shard_map/dot_general | solution.py:24
  102.5 7.8 %collective-permute-done.18 = bf16[104,4608]{1,0:T(8,128)(2,1)S(1)} collective-permute-done((bf16[104,4608]{1,0:T(8,128)(2,1)S(1)}, bf16[104,4608]{1,0:T(8,128)(2,1)S(1)}, u32[]{:S(2)}, u32[]{:S(2)}) %collective-permute-start.18) | collective-permute-done | bytes 958496 | tf_op jit(solution)/shard_map/ppermute | solution.py:33
  110.3 1.9 collective-permute-start.8
  112.2 2.1 %collective-permute-start.10 = (bf16[112,768]{1,0:T(8,128)(2,1)S(1)}, bf16[112,768]{1,0:T(8,128)(2,1)S(1)}, u32[]{:S(2)}, u32[]{:S(2)}) collective-permute-start(bf16[112,768]{1,0:T(8,128)(2,1)S(1)} %get-tuple-element.27), channel_id=1, source_target_pairs={{0,12},{4,0},{8,4},{12,8},{1,13},{5,1},{9,5},{13,9},{2,14},{6,2},{... | collective-permute-start | bytes 516104 | tf_op jit(solution)/shard_map/ppermute | solution.py:49
  114.3 1.0 collective-permute-start.9
  115.2 2.3 %fusion.42 = bf16[104,4608]{1,0:T(8,128)(2,1)S(1)} fusion(bf16[104,4608]{1,0:T(8,128)(2,1)S(1)} %collective-permute-done.18, f32[104,4608]{1,0:T(8,128)S(1)} %get-tuple-element.37, bf16[104,4608]{1,0:T(8,128)(2,1)} %collective-permute-done.17, bf16[216,6144]{1,0:T(8,128)(2,1)} %param.5), kind=kLoop, calls=%fused_computation.40 | loop fusion | flops 7188480 | bytes 5750784 | tf_op jit(solution)/shard_map/convert_element_type | solution.py:186
  117.7 1.9 collective-permute-done.8
  120.1 7.9 %collective-permute-done.9 = bf16[112,768]{1,0:T(8,128)(2,1)S(1)} collective-permute-done((bf16[112,768]{1,0:T(8,128)(2,1)S(1)}, bf16[112,768]{1,0:T(8,128)(2,1)S(1)}, u32[]{:S(2)}, u32[]{:S(2)}) %collective-permute-start.9) | collective-permute-done | bytes 172064 | tf_op jit(solution)/shard_map/ppermute | solution.py:49
  128.3 1.4 fusion.61
  129.9 0.9 fusion.45.x_ref
  130.8 1.8 collective-permute-start.13
  133.3 10.6 %shard_map.61.init_ref = f32[224,1536]{1,0:T(8,128)S(1)} custom-call(bf16[112,4608]{1,0:T(8,128)(2,1)S(1)} %pad.15.m_ref.refs_2_, bf16[112,4608]{1,0:T(8,128)(2,1)S(1)} %collective-permute-done.19.o_ref.refs_3_, bf16[1536,6144]{1,0:T(8,128)(2,1)} %refs_4_.3, f32[224,1536]{1,0:T(8,128)S(1)} %broadcast_1_init_ref.2.init_ref), custom_call_target="tpu_custom_call" | custom-call | flops 3170893824 | bytes 14155776 | tf_op jit(solution)/shard_map/pallas_call | solution.py:89
  143.9 6.4 %copy-done.1 = bf16[1536,6144]{1,0:T(8,128)(2,1)S(1)} copy-done((bf16[1536,6144]{1,0:T(8,128)(2,1)S(1)}, bf16[1536,6144]{1,0:T(8,128)(2,1)}, u32[]{:S(2)}) %copy-start.1) | copy-done | bytes 18874392
  150.3 2.5 %shard_map.62 = f32[224,1536]{1,0:T(8,128)S(1)} custom-call(bf16[112,1536]{1,0:T(8,128)(2,1)S(1)} %pad.14.m_ref.refs_2_, bf16[112,1536]{1,0:T(8,128)(2,1)S(1)} %collective-permute-done.16.o_ref.refs_3_, bf16[1536,6144]{1,0:T(8,128)(2,1)S(1)} %copy-done.1, f32[224,1536]{1,0:T(8,128)S(1)} %shard_map.61.init_ref), custom_call_target="tpu_custom_call" | custom-call | flops 1056964608 | bytes 4718592 | tf_op jit(solution)/shard_map/pallas_call | solution.py:89
  153.0 1.5 collective-permute-done.20
  154.8 2.9 %collective-permute-start.21 = (bf16[104,768]{1,0:T(8,128)(2,1)S(1)}, bf16[104,768]{1,0:T(8,128)(2,1)S(1)}, u32[]{:S(2)}, u32[]{:S(2)}) collective-permute-start(bf16[104,768]{1,0:T(8,128)(2,1)S(1)} %get-tuple-element.29), channel_id=1, source_target_pairs={{0,4},{4,8},{8,12},{12,0},{1,5},{5,9},{9,13},{13,1},{2,6},{6,10},{... | collective-permute-start | bytes 479240 | tf_op jit(solution)/shard_map/ppermute | solution.py:49
  157.7 1.0 collective-permute-start.23
  158.7 0.8 collective-permute-start.22
  159.4 20.6 %shard_map.63.refs_6_ = bf16[1536,6144]{1,0:T(8,128)(2,1)} custom-call(bf16[1536,448]{1,0:T(8,128)(2,1)S(1)} %fusion.45.x_ref, bf16[112,4608]{1,0:T(8,128)(2,1)S(1)} %fusion.36.m_ref.refs_0_, bf16[112,4608]{1,0:T(8,128)(2,1)S(1)} %collective-permute-done.4.o_ref.refs_1_, bf16[112,4608]{1,0:T(8,128)(2,1)S(1)} %pad.15.m_ref.refs_2_, ...), custom_call_target="tpu_custom_call" | custom-call | flops 6341787648 | bytes 42467328 | tf_op jit(solution)/shard_map/pallas_call | solution.py:134
  180.2 2.7 %collective-permute-start.26 = (bf16[104,768]{1,0:T(8,128)(2,1)S(1)}, bf16[104,768]{1,0:T(8,128)(2,1)S(1)}, u32[]{:S(2)}, u32[]{:S(2)}) collective-permute-start(bf16[104,768]{1,0:T(8,128)(2,1)S(1)} %get-tuple-element.19), channel_id=1, source_target_pairs={{0,12},{4,0},{8,4},{12,8},{1,13},{5,1},{9,5},{13,9},{2,14},{6,2},{... | collective-permute-start | bytes 479240 | tf_op jit(solution)/shard_map/ppermute | solution.py:60
  182.9 1.5 collective-permute-start.24
  184.5 8.3 %shard_map.64 = bf16[1536,6144]{1,0:T(8,128)(2,1)} custom-call(bf16[1536,448]{1,0:T(8,128)(2,1)S(1)} %fusion.45.x_ref, bf16[112,1536]{1,0:T(8,128)(2,1)S(1)} %fusion.55.m_ref.refs_0_, bf16[112,1536]{1,0:T(8,128)(2,1)S(1)} %collective-permute-done.6.o_ref.refs_1_, bf16[112,1536]{1,0:T(8,128)(2,1)S(1)} %pad.14.m_ref.refs_2_, ...), custom_call_target="tpu_custom_call", output_to_operand_aliasing={{}: (7, {})} | custom-call | flops 2113929216 | bytes 14155776 | tf_op jit(solution)/shard_map/pallas_call | solution.py:134
  192.7 1.3 collective-permute-done.24
  194.0 2.4 %collective-permute-done.25 = bf16[104,768]{1,0:T(8,128)(2,1)S(1)} collective-permute-done((bf16[104,768]{1,0:T(8,128)(2,1)S(1)}, bf16[104,768]{1,0:T(8,128)(2,1)S(1)}, u32[]{:S(2)}, u32[]{:S(2)}) %collective-permute-start.25) | collective-permute-done | bytes 159776 | tf_op jit(solution)/shard_map/ppermute | solution.py:60
  196.5 1.2 pad_maximum_fusion.2
  (88 shorter events, 6.4 us)
Async XLA Ops:
  1.8 2.3 %collective-permute-start = (bf16[216,1536]{1,0:T(8,128)(2,1)S(1)}, bf16[216,1536]{1,0:T(8,128)(2,1)S(1)}, u32[]{:S(2)}, u32[]{:S(2)}) collective-permute-start(bf16[216,1536]{1,0:T(8,128)(2,1)S(1)} %constant_dynamic-slice_fusion.7), channel_id=1, source_target_pairs={{0,1},{1,0},{2,3},{3,2},{4,5},{5,4},{6,7},{7,6},{8,9},{9,8},{10,11... | collective-permute-start | bytes 1990664 | tf_op jit(solution)/shard_map/ppermute | solution.py:20
  7.2 3.9 %collective-permute-start.1 = (bf16[112,1536]{1,0:T(8,128)(2,1)S(1)}, bf16[112,1536]{1,0:T(8,128)(2,1)S(1)}, u32[]{:S(2)}, u32[]{:S(2)}) collective-permute-start(bf16[112,1536]{1,0:T(8,128)(2,1)S(1)} %fusion.25), channel_id=1, source_target_pairs={{0,1},{1,0},{2,3},{3,2},{4,5},{5,4},{6,7},{7,6},{8,9},{9,8},{10,11... | collective-permute-start | bytes 1032200 | tf_op jit(solution)/shard_map/ppermute | solution.py:20
  11.1 9.1 %copy-start.3 = (bf16[112,1536]{0,1:T(8,128)(2,1)}, bf16[112,1536]{0,1:T(8,128)(2,1)S(1)}, u32[]{:S(2)}) copy-start(bf16[112,1536]{0,1:T(8,128)(2,1)S(1)} %copy.14) | copy-start | bytes 1032196
  20.1 5.2 %collective-permute-start.2 = (bf16[112,4608]{1,0:T(8,128)(2,1)}, bf16[112,4608]{1,0:T(8,128)(2,1)}, u32[]{:S(2)}, u32[]{:S(2)}) collective-permute-start(bf16[112,4608]{1,0:T(8,128)(2,1)} %fusion.8), channel_id=1, source_target_pairs={{0,1},{1,0},{2,3},{3,2},{4,5},{5,4},{6,7},{7,6},{8,9},{9,8},{10,11... | collective-permute-start | bytes 3096584 | tf_op jit(solution)/shard_map/ppermute | solution.py:20
  22.2 0.9 copy-start.7
  23.9 11.9 %slice-start = ((s8[18874368]{0:T(1024)(128)(4,1)}), s8[2097152]{0:T(1024)(128)(4,1)S(1)}, s32[]{:S(2)}) async-start(s8[18874368]{0:T(1024)(128)(4,1)} %bitcast.9), calls=%async_computation | async-start | bytes 4194304
  25.2 10.6 %slice-start.1 = ((s8[18874368]{0:T(1024)(128)(4,1)}), s8[4194304]{0:T(1024)(128)(4,1)S(1)}, s32[]{:S(2)}) async-start(s8[18874368]{0:T(1024)(128)(4,1)} %bitcast.9), calls=%async_computation.1 | async-start | bytes 8388608
  25.3 10.5 %slice-start.2 = ((s8[18874368]{0:T(1024)(128)(4,1)}), s8[4194304]{0:T(1024)(128)(4,1)S(1)}, s32[]{:S(2)}) async-start(s8[18874368]{0:T(1024)(128)(4,1)} %bitcast.9), calls=%async_computation.2 | async-start | bytes 8388608
  25.3 10.5 %slice-start.3 = ((s8[18874368]{0:T(1024)(128)(4,1)}), s8[4194304]{0:T(1024)(128)(4,1)S(1)}, s32[]{:S(2)}) async-start(s8[18874368]{0:T(1024)(128)(4,1)} %bitcast.9), calls=%async_computation.3 | async-start | bytes 8388608
  25.3 10.5 %slice-start.4 = ((s8[18874368]{0:T(1024)(128)(4,1)}), s8[4194304]{0:T(1024)(128)(4,1)S(1)}, s32[]{:S(2)}) async-start(s8[18874368]{0:T(1024)(128)(4,1)} %bitcast.9), calls=%async_computation.4 | async-start | bytes 8388608
  32.9 6.4 %copy-start.9 = (bf16[112,1536]{1,0:T(8,128)(2,1)S(1)}, bf16[112,1536]{1,0:T(8,128)(2,1)}, u32[]{:S(2)}) copy-start(bf16[112,1536]{1,0:T(8,128)(2,1)} %get-tuple-element.20) | copy-start | bytes 1032196
  32.9 33.8 %collective-permute-start.3 = (bf16[112,4608]{1,0:T(8,128)(2,1)S(1)}, bf16[112,4608]{1,0:T(8,128)(2,1)S(1)}, u32[]{:S(2)}, u32[]{:S(2)}) collective-permute-start(bf16[112,4608]{1,0:T(8,128)(2,1)S(1)} %get-tuple-element.34), channel_id=1, source_target_pairs={{0,2},{2,0},{1,3},{3,1},{4,6},{6,4},{5,7},{7,5},{8,10},{10,8},{9,1... | collective-permute-start | bytes 3096584 | tf_op jit(solution)/shard_map/ppermute | solution.py:33
  39.3 39.3 %collective-permute-start.17 = (bf16[104,4608]{1,0:T(8,128)(2,1)}, bf16[104,4608]{1,0:T(8,128)(2,1)}, u32[]{:S(2)}, u32[]{:S(2)}) collective-permute-start(bf16[104,4608]{1,0:T(8,128)(2,1)} %fusion.11), channel_id=1, source_target_pairs={{0,1},{1,0},{2,3},{3,2},{4,5},{5,4},{6,7},{7,6},{8,9},{9,8},{10,11... | collective-permute-start | bytes 2875400 | tf_op jit(solution)/shard_map/ppermute | solution.py:20
  39.3 26.9 %copy-start.2 = (bf16[216,6144]{1,0:T(8,128)(2,1)S(1)}, bf16[216,6144]{1,0:T(8,128)(2,1)}, u32[]{:S(2)}) copy-start(bf16[216,6144]{1,0:T(8,128)(2,1)} %param.5) | copy-start | bytes 7962628
  39.3 26.9 %collective-permute-start.5 = (bf16[112,1536]{1,0:T(8,128)(2,1)S(1)}, bf16[112,1536]{1,0:T(8,128)(2,1)S(1)}, u32[]{:S(2)}, u32[]{:S(2)}) collective-permute-start(bf16[112,1536]{1,0:T(8,128)(2,1)S(1)} %copy-done.9), channel_id=1, source_target_pairs={{0,2},{2,0},{1,3},{3,1},{4,6},{6,4},{5,7},{7,5},{8,10},{10,8},{9,1... | collective-permute-start | bytes 1032200 | tf_op jit(solution)/shard_map/ppermute | solution.py:33
  42.6 56.1 %collective-permute-start.14 = (bf16[104,1536]{1,0:T(8,128)(2,1)S(1)}, bf16[104,1536]{1,0:T(8,128)(2,1)S(1)}, u32[]{:S(2)}, u32[]{:S(2)}) collective-permute-start(bf16[104,1536]{1,0:T(8,128)(2,1)S(1)} %fusion.28), channel_id=1, source_target_pairs={{0,1},{1,0},{2,3},{3,2},{4,5},{5,4},{6,7},{7,6},{8,9},{9,8},{10,11... | collective-permute-start | bytes 958472 | tf_op jit(solution)/shard_map/ppermute | solution.py:20
  66.6 2.9 %collective-permute-start.6 = (bf16[112,1536]{1,0:T(8,128)(2,1)S(1)}, bf16[112,1536]{1,0:T(8,128)(2,1)S(1)}, u32[]{:S(2)}, u32[]{:S(2)}) collective-permute-start(bf16[112,1536]{1,0:T(8,128)(2,1)S(1)} %fusion.55.m_ref.refs_0_), channel_id=1, source_target_pairs={{0,1},{1,0},{2,3},{3,2},{4,5},{5,4},{6,7},{7,6},{8,9},{9,8},{10,11... | collective-permute-start | bytes 1032200 | tf_op jit(solution)/shard_map/ppermute | solution.py:20
  69.0 18.9 %collective-permute-start.4 = (bf16[112,4608]{1,0:T(8,128)(2,1)S(1)}, bf16[112,4608]{1,0:T(8,128)(2,1)S(1)}, u32[]{:S(2)}, u32[]{:S(2)}) collective-permute-start(bf16[112,4608]{1,0:T(8,128)(2,1)S(1)} %fusion.36.m_ref.refs_0_), channel_id=1, source_target_pairs={{0,1},{1,0},{2,3},{3,2},{4,5},{5,4},{6,7},{7,6},{8,9},{9,8},{10,11... | collective-permute-start | bytes 3096584 | tf_op jit(solution)/shard_map/ppermute | solution.py:20
  69.7 6.4 %copy-start = (bf16[1536,6144]{1,0:T(8,128)(2,1)S(1)}, bf16[1536,6144]{1,0:T(8,128)(2,1)}, u32[]{:S(2)}) copy-start(bf16[1536,6144]{1,0:T(8,128)(2,1)} %refs_4_.3) | copy-start | bytes 56623108
  76.1 2.5 %copy-start.8 = (bf16[104,1536]{1,0:T(8,128)(2,1)S(1)}, bf16[104,1536]{1,0:T(8,128)(2,1)}, u32[]{:S(2)}) copy-start(bf16[104,1536]{1,0:T(8,128)(2,1)} %copy-done.7) | copy-start | bytes 958468
  86.1 24.2 %collective-permute-start.18 = (bf16[104,4608]{1,0:T(8,128)(2,1)S(1)}, bf16[104,4608]{1,0:T(8,128)(2,1)S(1)}, u32[]{:S(2)}, u32[]{:S(2)}) collective-permute-start(bf16[104,4608]{1,0:T(8,128)(2,1)S(1)} %get-tuple-element.36), channel_id=1, source_target_pairs={{0,2},{2,0},{1,3},{3,1},{4,6},{6,4},{5,7},{7,5},{8,10},{10,8},{9,1... | collective-permute-start | bytes 2875400 | tf_op jit(solution)/shard_map/ppermute | solution.py:33
  98.6 3.6 %collective-permute-start.7 = (bf16[112,1536]{1,0:T(8,128)(2,1)S(1)}, bf16[112,1536]{1,0:T(8,128)(2,1)S(1)}, u32[]{:S(2)}, u32[]{:S(2)}) collective-permute-start(bf16[112,1536]{1,0:T(8,128)(2,1)S(1)} %slice.110), channel_id=1, source_target_pairs={{0,1},{1,0},{2,3},{3,2},{4,5},{5,4},{6,7},{7,6},{8,9},{9,8},{10,11... | collective-permute-start | bytes 1032200 | tf_op jit(solution)/shard_map/ppermute | solution.py:20
  101.9 26.4 %collective-permute-start.15 = (bf16[104,1536]{1,0:T(8,128)(2,1)S(1)}, bf16[104,1536]{1,0:T(8,128)(2,1)S(1)}, u32[]{:S(2)}, u32[]{:S(2)}) collective-permute-start(bf16[104,1536]{1,0:T(8,128)(2,1)S(1)} %get-tuple-element.32), channel_id=1, source_target_pairs={{0,2},{2,0},{1,3},{3,1},{4,6},{6,4},{5,7},{7,5},{8,10},{10,8},{9,1... | collective-permute-start | bytes 958472 | tf_op jit(solution)/shard_map/ppermute | solution.py:33
  110.3 9.3 %collective-permute-start.8 = (bf16[112,768]{1,0:T(8,128)(2,1)S(1)}, bf16[112,768]{1,0:T(8,128)(2,1)S(1)}, u32[]{:S(2)}, u32[]{:S(2)}) collective-permute-start(bf16[112,768]{1,0:T(8,128)(2,1)S(1)} %get-tuple-element.26), channel_id=1, source_target_pairs={{0,4},{4,8},{8,12},{12,0},{1,5},{5,9},{9,13},{13,1},{2,6},{6,10},{... | collective-permute-start | bytes 516104 | tf_op jit(solution)/shard_map/ppermute | solution.py:49
  112.2 7.9 %collective-permute-start.10 = (bf16[112,768]{1,0:T(8,128)(2,1)S(1)}, bf16[112,768]{1,0:T(8,128)(2,1)S(1)}, u32[]{:S(2)}, u32[]{:S(2)}) collective-permute-start(bf16[112,768]{1,0:T(8,128)(2,1)S(1)} %get-tuple-element.27), channel_id=1, source_target_pairs={{0,12},{4,0},{8,4},{12,8},{1,13},{5,1},{9,5},{13,9},{2,14},{6,2},{... | collective-permute-start | bytes 516104 | tf_op jit(solution)/shard_map/ppermute | solution.py:49
  114.3 13.8 %collective-permute-start.9 = (bf16[112,768]{1,0:T(8,128)(2,1)S(1)}, bf16[112,768]{1,0:T(8,128)(2,1)S(1)}, u32[]{:S(2)}, u32[]{:S(2)}) collective-permute-start(bf16[112,768]{1,0:T(8,128)(2,1)S(1)} %get-tuple-element.28), channel_id=1, source_target_pairs={{0,8},{4,12},{8,0},{12,4},{1,9},{5,13},{9,1},{13,5},{2,10},{6,14},... | collective-permute-start | bytes 516104 | tf_op jit(solution)/shard_map/ppermute | solution.py:49
  117.6 15.6 %collective-permute-start.19 = (bf16[112,4608]{1,0:T(8,128)(2,1)S(1)}, bf16[112,4608]{1,0:T(8,128)(2,1)S(1)}, u32[]{:S(2)}, u32[]{:S(2)}) collective-permute-start(bf16[112,4608]{1,0:T(8,128)(2,1)S(1)} %pad.15.m_ref.refs_2_), channel_id=1, source_target_pairs={{0,1},{1,0},{2,3},{3,2},{4,5},{5,4},{6,7},{7,6},{8,9},{9,8},{10,11... | collective-permute-start | bytes 3096584 | tf_op jit(solution)/shard_map/ppermute | solution.py:20
  128.1 1.7 copy-start.4
  128.1 1.7 copy-start.5
  128.1 1.7 copy-start.6
  129.8 14.1 %collective-permute-start.16 = (bf16[112,1536]{1,0:T(8,128)(2,1)S(1)}, bf16[112,1536]{1,0:T(8,128)(2,1)S(1)}, u32[]{:S(2)}, u32[]{:S(2)}) collective-permute-start(bf16[112,1536]{1,0:T(8,128)(2,1)S(1)} %pad.14.m_ref.refs_2_), channel_id=1, source_target_pairs={{0,1},{1,0},{2,3},{3,2},{4,5},{5,4},{6,7},{7,6},{8,9},{9,8},{10,11... | collective-permute-start | bytes 1032200 | tf_op jit(solution)/shard_map/ppermute | solution.py:20
  130.8 22.2 %collective-permute-start.13 = (bf16[112,768]{1,0:T(8,128)(2,1)S(1)}, bf16[112,768]{1,0:T(8,128)(2,1)S(1)}, u32[]{:S(2)}, u32[]{:S(2)}) collective-permute-start(bf16[112,768]{1,0:T(8,128)(2,1)S(1)} %get-tuple-element.17), channel_id=1, source_target_pairs={{0,12},{4,0},{8,4},{12,8},{1,13},{5,1},{9,5},{13,9},{2,14},{6,2},{... | collective-permute-start | bytes 516104 | tf_op jit(solution)/shard_map/ppermute | solution.py:60
  132.6 20.3 %collective-permute-start.12 = (bf16[112,768]{1,0:T(8,128)(2,1)S(1)}, bf16[112,768]{1,0:T(8,128)(2,1)S(1)}, u32[]{:S(2)}, u32[]{:S(2)}) collective-permute-start(bf16[112,768]{1,0:T(8,128)(2,1)S(1)} %get-tuple-element.17), channel_id=1, source_target_pairs={{0,8},{4,12},{8,0},{12,4},{1,9},{5,13},{9,1},{13,5},{2,10},{6,14},... | collective-permute-start | bytes 516104 | tf_op jit(solution)/shard_map/ppermute | solution.py:60
  132.6 20.3 %collective-permute-start.11 = (bf16[112,768]{1,0:T(8,128)(2,1)S(1)}, bf16[112,768]{1,0:T(8,128)(2,1)S(1)}, u32[]{:S(2)}, u32[]{:S(2)}) collective-permute-start(bf16[112,768]{1,0:T(8,128)(2,1)S(1)} %get-tuple-element.17), channel_id=1, source_target_pairs={{0,4},{4,8},{8,12},{12,0},{1,5},{5,9},{9,13},{13,1},{2,6},{6,10},{... | collective-permute-start | bytes 516104 | tf_op jit(solution)/shard_map/ppermute | solution.py:60
  143.9 6.4 %copy-start.1 = (bf16[1536,6144]{1,0:T(8,128)(2,1)S(1)}, bf16[1536,6144]{1,0:T(8,128)(2,1)}, u32[]{:S(2)}) copy-start(bf16[1536,6144]{1,0:T(8,128)(2,1)} %refs_4_.3) | copy-start | bytes 56623108
  152.8 1.7 collective-permute-start.20
  154.8 25.2 %collective-permute-start.21 = (bf16[104,768]{1,0:T(8,128)(2,1)S(1)}, bf16[104,768]{1,0:T(8,128)(2,1)S(1)}, u32[]{:S(2)}, u32[]{:S(2)}) collective-permute-start(bf16[104,768]{1,0:T(8,128)(2,1)S(1)} %get-tuple-element.29), channel_id=1, source_target_pairs={{0,4},{4,8},{8,12},{12,0},{1,5},{5,9},{9,13},{13,1},{2,6},{6,10},{... | collective-permute-start | bytes 479240 | tf_op jit(solution)/shard_map/ppermute | solution.py:49
  157.7 22.3 %collective-permute-start.23 = (bf16[104,768]{1,0:T(8,128)(2,1)S(1)}, bf16[104,768]{1,0:T(8,128)(2,1)S(1)}, u32[]{:S(2)}, u32[]{:S(2)}) collective-permute-start(bf16[104,768]{1,0:T(8,128)(2,1)S(1)} %get-tuple-element.30), channel_id=1, source_target_pairs={{0,12},{4,0},{8,4},{12,8},{1,13},{5,1},{9,5},{13,9},{2,14},{6,2},{... | collective-permute-start | bytes 479240 | tf_op jit(solution)/shard_map/ppermute | solution.py:49
  158.7 21.4 %collective-permute-start.22 = (bf16[104,768]{1,0:T(8,128)(2,1)S(1)}, bf16[104,768]{1,0:T(8,128)(2,1)S(1)}, u32[]{:S(2)}, u32[]{:S(2)}) collective-permute-start(bf16[104,768]{1,0:T(8,128)(2,1)S(1)} %get-tuple-element.31), channel_id=1, source_target_pairs={{0,8},{4,12},{8,0},{12,4},{1,9},{5,13},{9,1},{13,5},{2,10},{6,14},... | collective-permute-start | bytes 479240 | tf_op jit(solution)/shard_map/ppermute | solution.py:49
  180.2 16.3 %collective-permute-start.26 = (bf16[104,768]{1,0:T(8,128)(2,1)S(1)}, bf16[104,768]{1,0:T(8,128)(2,1)S(1)}, u32[]{:S(2)}, u32[]{:S(2)}) collective-permute-start(bf16[104,768]{1,0:T(8,128)(2,1)S(1)} %get-tuple-element.19), channel_id=1, source_target_pairs={{0,12},{4,0},{8,4},{12,8},{1,13},{5,1},{9,5},{13,9},{2,14},{6,2},{... | collective-permute-start | bytes 479240 | tf_op jit(solution)/shard_map/ppermute | solution.py:60
  182.9 13.6 %collective-permute-start.25 = (bf16[104,768]{1,0:T(8,128)(2,1)S(1)}, bf16[104,768]{1,0:T(8,128)(2,1)S(1)}, u32[]{:S(2)}, u32[]{:S(2)}) collective-permute-start(bf16[104,768]{1,0:T(8,128)(2,1)S(1)} %get-tuple-element.19), channel_id=1, source_target_pairs={{0,8},{4,12},{8,0},{12,4},{1,9},{5,13},{9,1},{13,5},{2,10},{6,14},... | collective-permute-start | bytes 479240 | tf_op jit(solution)/shard_map/ppermute | solution.py:60
  182.9 11.1 %collective-permute-start.24 = (bf16[104,768]{1,0:T(8,128)(2,1)S(1)}, bf16[104,768]{1,0:T(8,128)(2,1)S(1)}, u32[]{:S(2)}, u32[]{:S(2)}) collective-permute-start(bf16[104,768]{1,0:T(8,128)(2,1)S(1)} %get-tuple-element.19), channel_id=1, source_target_pairs={{0,4},{4,8},{8,12},{12,0},{1,5},{5,9},{9,13},{13,1},{2,6},{6,10},{... | collective-permute-start | bytes 479240 | tf_op jit(solution)/shard_map/ppermute | solution.py:60

commit v4 on v3

v4 whole, which is shorter than its diff:
```python
import functools

import jax
import jax.numpy as jnp
from jax import lax
from jax.experimental import pallas as pl
from jax.experimental.pallas import tpu as pltpu
from jax.sharding import PartitionSpec as P

BF = jnp.bfloat16
F32 = jnp.float32


def gelu_slope(pre):
    cdf = 0.5 * (1.0 + jax.scipy.special.erf(pre * 0.7071067811865476))
    return cdf + pre * jnp.exp(-0.5 * pre * pre) * 0.3989422804014327


def swap(x):
    return lax.ppermute(x, "tok", [(0, 1), (1, 0)])


def mm(a, b, dims):
    return lax.dot_general(a, b, (dims, ((), ())), preferred_element_type=F32)


def after(x, *others):
    return lax.optimization_barrier((x,) + others)[0]


def send_partial(part, n):
    if n == 2:
        return part, lax.ppermute(part.astype(BF), "in", [(0, 1), (1, 0)])
    return None, lax.psum(part, "in")


def direct(x, n):
    return 1 < n <= 8 and x.shape[1] % (128 * n) == 0


def scatter_out(x, n):
    w = x.shape[1] // n
    me = lax.axis_index("out")
    total = lax.dynamic_slice_in_dim(x, me * w, w, 1)
    xb = x.astype(BF)
    for k in range(1, n):
        to = lax.rem(me + k, n)
        piece = lax.dynamic_slice_in_dim(xb, to * w, w, 1)
        got = lax.ppermute(piece, "out", [(i, (i + k) % n) for i in range(n)])
        total = total + got.astype(F32)
    return total.astype(BF), xb


def gather_out(mine, n):
    w = mine.shape[1]
    me = lax.axis_index("out")
    out = jnp.zeros((mine.shape[0], w * n), BF)
    out = lax.dynamic_update_slice_in_dim(out, mine, me * w, 1)
    for k in range(1, n):
        got = lax.ppermute(mine, "out", [(i, (i + k) % n) for i in range(n)])
        out = lax.dynamic_update_slice_in_dim(out, got, lax.rem(me - k + n, n) * w, 1)
    return out


def block_of(n, sizes):
    for b in sizes:
        if n % b == 0:
            return b
    return n


def dx_kernel(m_ref, o_ref, w_ref, sum_ref, acc_ref):
    i = pl.program_id(0)

    @pl.when(i == 0)
    def _():
        acc_ref[...] = jnp.zeros_like(acc_ref)

    g = jnp.concatenate([m_ref[...], o_ref[...]], axis=0)
    acc_ref[...] += lax.dot_general(
        w_ref[...], g, (((1,), (1,)), ((), ())), preferred_element_type=F32
    )

    @pl.when(i == pl.num_programs(0) - 1)
    def _():
        sum_ref[...] = acc_ref[...].T


def dx_partial(mine, other, weight, unit):
    rows = weight.shape[0]
    m, width = mine.shape
    g_block = pl.BlockSpec((m, unit), lambda i: (0, i))
    whole = pl.BlockSpec((2 * m, rows), lambda i: (0, 0))
    return pl.pallas_call(
        dx_kernel,
        grid=(width // unit,),
        in_specs=[
            g_block,
            g_block,
            pl.BlockSpec((rows, unit), lambda i: (0, i)),
        ],
        out_specs=whole,
        out_shape=jax.ShapeDtypeStruct((2 * m, rows), F32),
        scratch_shapes=[pltpu.VMEM((rows, 2 * m), F32)],
        cost_estimate=pl.CostEstimate(
            flops=4 * m * rows * width, bytes_accessed=2 * rows * width, transcendentals=0
        ),
        compiler_params=pltpu.CompilerParams(vmem_limit_bytes=48 * 2**20),
    )(mine, other, weight)


def score_kernel(parts, x_ref, *refs):
    g_refs, (w_ref, s_ref), o_ref = refs[:parts], refs[parts : parts + 2], refs[-1]
    rows = w_ref.shape[0]
    step = block_of(rows, (384, 256, 128))
    g = jnp.concatenate([ref[...] for ref in g_refs], axis=0)
    for r in range(0, rows, step):
        part = pl.ds(r, step)
        gw = jnp.dot(x_ref[part, :], g, preferred_element_type=F32)
        o_ref[part, :] = (
            s_ref[part, :].astype(F32) - w_ref[part, :].astype(F32) * gw
        ).astype(BF)


def score_part(x_t, gs, weight, score, first, count, w, earlier):
    rows, ff = weight.shape
    m, width = gs[0].shape[0], count * w
    block = pl.BlockSpec((rows, w), lambda i: (0, i + first))
    specs = [pl.BlockSpec(x_t.shape, lambda i: (0, 0))]
    specs += [pl.BlockSpec((m, w), lambda i: (0, i + first)) for _ in gs]
    specs += [block, block]
    args = [x_t, *gs, weight, score]
    alias = {}
    if earlier is not None:
        alias = {len(args): 0}
        specs.append(pl.BlockSpec(memory_space=pl.ANY))
        args.append(earlier)
    return pl.pallas_call(
        functools.partial(score_kernel, len(gs)),
        grid=(count,),
        in_specs=specs,
        out_specs=block,
        out_shape=jax.ShapeDtypeStruct((rows, ff), BF),
        input_output_aliases=alias,
        cost_estimate=pl.CostEstimate(
            flops=2 * x_t.shape[1] * rows * width,
            bytes_accessed=6 * rows * width,
            transcendentals=0,
        ),
        compiler_params=pltpu.CompilerParams(vmem_limit_bytes=40 * 2**20),
    )(*args)


def make(n_in, n_out):
    def on_device(inputs, grad_act, weight, score):
        rows, ff = weight.shape
        tokens = inputs.shape[0]
        t = lax.axis_index("tok")
        full = -(-tokens // 16) * 16
        pad = ((0, full - tokens), (0, 0))
        x_mine = lax.dynamic_slice_in_dim(inputs, t * rows, rows, 1)
        x_other = swap(lax.dynamic_slice_in_dim(inputs, (1 - t) * rows, rows, 1))
        chunks = 4 if ff % (4 * 256) == 0 else 1
        w = ff // chunks
        gm, go = [], []
        for c in range(chunks):
            wc = weight[:, c * w : (c + 1) * w]
            send = mm(x_other, wc, ((1,), (0,))).astype(BF)
            part = mm(x_mine, wc, ((1,), (0,))) + swap(send).astype(F32)
            own, got = send_partial(part, n_in)
            pre = got if own is None else own + got.astype(F32)
            g = (grad_act[:, c * w : (c + 1) * w].astype(F32) * gelu_slope(pre)).astype(BF)
            g = jnp.pad(g, pad)
            gm.append(g)
            go.append(swap(g))
        gs = [jnp.concatenate(gm, axis=1), jnp.concatenate(go, axis=1)]
        unit = block_of(ff, (512, 256, 128))
        total = dx_partial(*gs, weight, unit)
        mine, theirs = total[:tokens], total[full : full + tokens]
        got = swap(theirs.astype(BF)).astype(F32)
        left, right = jnp.where(t == 0, mine, got), jnp.where(t == 0, got, mine)
        term = jnp.concatenate([left, right], axis=1)
        if direct(term, n_out):
            piece, ready = scatter_out(term, n_out)
            waits = [ready, piece]
            grad_inputs = gather_out(piece, n_out)
        else:
            waits = [term, term]
            grad_inputs = lax.psum(term, "out").astype(BF)
        x_t = jnp.concatenate([jnp.pad(x_mine, pad), jnp.pad(x_other, pad)], axis=0).T
        blocks = ff // unit
        half = (blocks + 1) // 2
        new_score = None
        for wait, first, count in ((waits[0], 0, half), (waits[1], half, blocks - half)):
            if count:
                x_now = after(x_t, wait)
                new_score = score_part(
                    x_now, gs, weight, score, first, count, unit, new_score
                )
        return grad_inputs, new_score

    return on_device


def solution(mesh):
    placed = (
        P(("group", "tok"), "in"),
        P(("group", "tok"), "out"),
        P(("in", "tok"), "out"),
        P(("in", "tok"), "out"),
    )
    return jax.shard_map(
        make(mesh.shape["in"], mesh.shape["out"]),
        mesh=mesh,
        in_specs=placed,
        out_specs=(P(("group", "tok"), "in"), P(("group", "in", "tok"), "out")),
        check_vma=False,
    )
```

time: 198 us -> 181 us (0.914)
  waiting for transfers between devices: 47.7 us -> 85.6 us
  matrix products: 37.1 us -> 15.6 us
  Pallas kernels: 55.1 us -> 44.6 us
  starting transfers between devices: 25.9 us -> 15.5 us
  local copies, waits for them, and re-layouts: 20.7 us -> 11 us
  other arithmetic: 9.97 us -> 7.54 us
    dot_general x8, matrix products: 37.1 us -> 15.6 us  [mm(): return lax.dot_general(a, b, (dims, ((), ())), preferred_element_type=F32)]
    ppermute x4, waiting for transfers between devices: 31.3 us -> 51.8 us  [send_partial(): return (part, lax.ppermute(part.astype(BF), 'in', [(0, 1), (1, 0)]))]
    unnamed x35 -> x20, local copies, waits for them, and re-layouts: 16.7 us -> 5.7 us
    ppermute x6 -> x3, waiting for transfers between devices: 3.75 us -> 13.1 us  [gather_out(): got = lax.ppermute(mine, 'out', [(i, (i + k) % n) for i in range(n)])]
    pallas_call x4 -> x1, Pallas kernels: 26.3 us -> 17.7 us  [dx_partial(): pl.pallas_call(dx_kernel, grid=(width // unit,), in_specs=[g_block, g_blo...]
    ppermute x6 -> x3, waiting for transfers between devices: 10.4 us -> 15.2 us  [scatter_out(): got = lax.ppermute(piece, 'out', [(i, (i + k) % n) for i in range(n)])]
    ppermute x6 -> x3, starting transfers between devices: 9.56 us -> 4.93 us  [scatter_out(): got = lax.ppermute(piece, 'out', [(i, (i + k) % n) for i in range(n)])]
    ppermute x6 -> x3, starting transfers between devices: 6.7 us -> 2.34 us  [gather_out(): got = lax.ppermute(mine, 'out', [(i, (i + k) % n) for i in range(n)])]
  transfers between devices with their start and end apart: 27 -> 20, of which waited for: 9 -> 10; matrix products, arithmetic and copies ran while one was open for 16% -> 9% of each run, Pallas kernels for 28% -> 15%
where the time goes in v4:
time: 181 us
  waiting for transfers between devices  85.6 us (47%)
  Pallas kernels  44.6 us (25%)
  matrix products  15.6 us (9%)
  starting transfers between devices  15.5 us (9%)
  local copies, waits for them, and re-layouts  11 us (6%)
  other arithmetic  7.54 us (4%)
    ppermute x4, waiting for transfers between devices, send_partial(): return (part, lax.ppermute(part.astype(BF), 'in', [(0, 1), (1, 0)]))  51.8 us
    pallas_call x2, Pallas kernels, score_part(): pl.pallas_call(functools.partial(score_kernel, len(gs)), grid=(count,), i...  26.9 us
    pallas_call x1, Pallas kernels, dx_partial(): pl.pallas_call(dx_kernel, grid=(width // unit,), in_specs=[g_block, g_blo...  17.7 us
    dot_general x8, matrix products, mm(): return lax.dot_general(a, b, (dims, ((), ())), preferred_element_type=F32)  15.6 us
    ppermute x3, waiting for transfers between devices, scatter_out(): got = lax.ppermute(piece, 'out', [(i, (i + k) % n) for i in range(n)])  15.2 us
    ppermute x3, waiting for transfers between devices, gather_out(): got = lax.ppermute(mine, 'out', [(i, (i + k) % n) for i in range(n)])  13.1 us
    unnamed x20, local copies, waits for them, and re-layouts  5.7 us
    ppermute x10, waiting for transfers between devices, swap(): return lax.ppermute(x, 'tok', [(0, 1), (1, 0)])  5.55 us
  transfers between devices with their start and end apart: 20, of which 10 were waited for; matrix products, arithmetic and copies ran while one was open for 9% of the time, Pallas kernels for 15%

profile of v4, /device:TPU:0, one launch (start us, length us, event | category | flops | bytes accessed | tf_op | source)
XLA Modules:
  0.0 180.8 jit_solution(3927104802839863371)
XLA Ops:
  0.6 1.5 constant_dynamic-slice_fusion.3
  2.2 0.5 collective-permute-start
  2.7 1.7 collective-permute-done
  4.5 4.5 %fusion.19 = bf16[216,1536]{1,0:T(8,128)(2,1)S(1)} fusion(bf16[216,1536]{1,0:T(8,128)(2,1)S(1)} %collective-permute-done, bf16[1536,6144]{1,0:T(8,128)(2,1)} %refs_2_.3), kind=kOutput, calls=%fused_computation.25 | convolution fusion | flops 1019547648 | bytes 6045696 | tf_op jit(solution)/shard_map/dot_general | solution.py:24
  9.0 0.4 collective-permute-start.1
  9.4 3.5 %fusion.28 = bf16[216,1536]{1,0:T(8,128)(2,1)S(1)} fusion(bf16[216,1536]{1,0:T(8,128)(2,1)S(1)} %collective-permute-done, bf16[1536,6144]{1,0:T(8,128)(2,1)} %refs_2_.3), kind=kOutput, calls=%fused_computation.28 | convolution fusion | flops 1019547648 | bytes 6045696 | tf_op jit(solution)/shard_map/dot_general | solution.py:24
  13.0 0.2 collective-permute-start.7
  13.2 1.3 fusion.25
  14.4 0.4 collective-permute-start.5
  14.9 1.3 fusion.22
  16.1 0.2 collective-permute-start.3
  16.3 1.2 fusion.60
  17.6 2.9 %collective-permute-start.8 = (bf16[216,1536]{1,0:T(8,128)(2,1)S(1)}, bf16[216,1536]{1,0:T(8,128)(2,1)S(1)}, u32[]{:S(2)}, u32[]{:S(2)}) collective-permute-start(bf16[216,1536]{1,0:T(8,128)(2,1)S(1)} %get-tuple-element.23), channel_id=1, source_target_pairs={{0,2},{2,0},{1,3},{3,1},{4,6},{6,4},{5,7},{7,5},{8,10},{10,8},{9,1... | collective-permute-start | bytes 1990664 | tf_op jit(solution)/shard_map/ppermute | solution.py:33
  20.5 1.3 fusion.59
  21.9 1.3 fusion.58
  23.2 2.1 %collective-permute-start.4 = (bf16[216,1536]{1,0:T(8,128)(2,1)S(1)}, bf16[216,1536]{1,0:T(8,128)(2,1)S(1)}, u32[]{:S(2)}, u32[]{:S(2)}) collective-permute-start(bf16[216,1536]{1,0:T(8,128)(2,1)S(1)} %get-tuple-element.21), channel_id=1, source_target_pairs={{0,2},{2,0},{1,3},{3,1},{4,6},{6,4},{5,7},{7,5},{8,10},{10,8},{9,1... | collective-permute-start | bytes 1990664 | tf_op jit(solution)/shard_map/ppermute | solution.py:33
  25.2 1.3 fusion.57
  26.6 9.6 %collective-permute-done.8 = bf16[216,1536]{1,0:T(8,128)(2,1)S(1)} collective-permute-done((bf16[216,1536]{1,0:T(8,128)(2,1)S(1)}, bf16[216,1536]{1,0:T(8,128)(2,1)S(1)}, u32[]{:S(2)}, u32[]{:S(2)}) %collective-permute-start.8) | collective-permute-done | bytes 663584 | tf_op jit(solution)/shard_map/ppermute | solution.py:33
  36.2 14.2 %collective-permute-done.6 = bf16[216,1536]{1,0:T(8,128)(2,1)S(1)} collective-permute-done((bf16[216,1536]{1,0:T(8,128)(2,1)S(1)}, bf16[216,1536]{1,0:T(8,128)(2,1)S(1)}, u32[]{:S(2)}, u32[]{:S(2)}) %collective-permute-start.6) | collective-permute-done | bytes 663584 | tf_op jit(solution)/shard_map/ppermute | solution.py:33
  50.4 14.2 %collective-permute-done.4 = bf16[216,1536]{1,0:T(8,128)(2,1)S(1)} collective-permute-done((bf16[216,1536]{1,0:T(8,128)(2,1)S(1)}, bf16[216,1536]{1,0:T(8,128)(2,1)S(1)}, u32[]{:S(2)}, u32[]{:S(2)}) %collective-permute-start.4) | collective-permute-done | bytes 663584 | tf_op jit(solution)/shard_map/ppermute | solution.py:33
  64.7 13.7 %collective-permute-done.2 = bf16[216,1536]{1,0:T(8,128)(2,1)S(1)} collective-permute-done((bf16[216,1536]{1,0:T(8,128)(2,1)S(1)}, bf16[216,1536]{1,0:T(8,128)(2,1)S(1)}, u32[]{:S(2)}, u32[]{:S(2)}) %collective-permute-start.2) | collective-permute-done | bytes 663584 | tf_op jit(solution)/shard_map/ppermute | solution.py:33
  78.4 3.2 %fusion.38 = (bf16[216,1536]{1,0:T(8,128)(2,1)S(1)}, bf16[216,1536]{1,0:T(8,128)(2,1)S(1)}, bf16[216,1536]{1,0:T(8,128)(2,1)S(1)}, bf16[216,1536]{1,0:T(8,128)(2,1)S(1)}) fusion(bf16[216,1536]{1,0:T(8,128)(2,1)S(1)} %collective-permute-done.2, f32[216,1536]{1,0:T(8,128)S(1)} %get-tuple-element.20, bf16[216,1536]{1,0:T(8,128)(2,1)S(1)} %collective-permute-done.1, ...), kind=kLoop, calls=%fused_computation.42 | loop fusion | flops 19906560 | bytes 15925248 | tf_op jit(solution)/shard_map/convert_element_type | solution.py:172
  81.9 0.5 collective-permute-start.12
  82.5 0.4 collective-permute-start.9
  82.9 0.3 pad_maximum_fusion.1.m_ref.refs_0_
  83.2 3.8 %collective-permute-done.9 = bf16[224,1536]{1,0:T(8,128)(2,1)S(1)} collective-permute-done((bf16[224,1536]{1,0:T(8,128)(2,1)S(1)}, bf16[224,1536]{1,0:T(8,128)(2,1)S(1)}, u32[]{:S(2)}, u32[]{:S(2)}) %collective-permute-start.9) | collective-permute-done | bytes 688160 | tf_op jit(solution)/shard_map/ppermute | solution.py:20
  87.4 1.5 copy-done
  88.9 17.7 %shard_map.59 = f32[448,1536]{1,0:T(8,128)S(1)} custom-call(bf16[224,6144]{1,0:T(8,128)(2,1)S(1)} %pad_maximum_fusion.1.m_ref.refs_0_, bf16[224,6144]{1,0:T(8,128)(2,1)} %copy-done, bf16[1536,6144]{1,0:T(8,128)(2,1)} %refs_2_.3), custom_call_target="tpu_custom_call" | custom-call | flops 8455716864 | bytes 18874368 | tf_op jit(solution)/shard_map/pallas_call | solution.py:94
  106.7 1.5 copy-done.2
  108.2 0.9 slice.74
  109.2 1.4 copy.11
  110.6 2.2 %copy.10 = bf16[216,1536]{0,1:T(8,128)(2,1)} copy(bf16[216,1536]{1,0:T(8,128)(2,1)} %copy-done.7) | data formatting | bytes 1327104 | tf_op jit(solution)/shard_map/ppermute | solution.py:20
  112.8 1.8 fusion.32.x_ref
  114.6 1.8 %convert_select_fusion.1 = (f32[216,1536]{1,0:T(8,128)S(1)}, f32[216,1536]{1,0:T(8,128)S(1)}) fusion(bf16[216,1536]{1,0:T(8,128)(2,1)} %collective-permute-done.13, f32[448,1536]{1,0:T(8,128)} %copy-done.2, pred[]{:T(512)S(6)} %eq.4), kind=kLoop, calls=%fused_computation.34 | loop fusion | flops 995328 | bytes 4644865 | tf_op jit(solution)/shard_map/jit(_where)/select_n | solution.py:181
  116.5 0.1 fusion.18
  116.7 1.9 %collective-permute-start.14 = (bf16[216,768]{1,0:T(8,128)(2,1)S(1)}, bf16[216,768]{1,0:T(8,128)(2,1)S(1)}, u32[]{:S(2)}, u32[]{:S(2)}) collective-permute-start(bf16[216,768]{1,0:T(8,128)(2,1)S(1)} %get-tuple-element.14), channel_id=1, source_target_pairs={{0,4},{4,8},{8,12},{12,0},{1,5},{5,9},{9,13},{13,1},{2,6},{6,10},{... | collective-permute-start | bytes 995336 | tf_op jit(solution)/shard_map/ppermute | solution.py:49
  118.6 2.1 %collective-permute-start.16 = (bf16[216,768]{1,0:T(8,128)(2,1)S(1)}, bf16[216,768]{1,0:T(8,128)(2,1)S(1)}, u32[]{:S(2)}, u32[]{:S(2)}) collective-permute-start(bf16[216,768]{1,0:T(8,128)(2,1)S(1)} %get-tuple-element.15), channel_id=1, source_target_pairs={{0,12},{4,0},{8,4},{12,8},{1,13},{5,1},{9,5},{13,9},{2,14},{6,2},{... | collective-permute-start | bytes 995336 | tf_op jit(solution)/shard_map/ppermute | solution.py:49
  120.7 0.9 collective-permute-start.15
  121.7 13.4 %shard_map.60.refs_4_ = bf16[1536,6144]{1,0:T(8,128)(2,1)} custom-call(bf16[1536,448]{1,0:T(8,128)(2,1)S(1)} %fusion.32.x_ref, bf16[224,6144]{1,0:T(8,128)(2,1)S(1)} %pad_maximum_fusion.1.m_ref.refs_0_, bf16[224,6144]{1,0:T(8,128)(2,1)S(1)} %copy-done.1, bf16[1536,6144]{1,0:T(8,128)(2,1)} %refs_2_.3, bf16[1536,6144]{1,0:T(8,128)(2,1)} %refs_3_.3), custom_call_target="tpu_custom_call" | custom-call | flops 4227858432 | bytes 28311552 | tf_op jit(solution)/shard_map/pallas_call | solution.py:138
  135.1 0.4 collective-permute-done.16
  135.5 14.8 %collective-permute-done.15 = bf16[216,768]{1,0:T(8,128)(2,1)S(1)} collective-permute-done((bf16[216,768]{1,0:T(8,128)(2,1)S(1)}, bf16[216,768]{1,0:T(8,128)(2,1)S(1)}, u32[]{:S(2)}, u32[]{:S(2)}) %collective-permute-start.15) | collective-permute-done | bytes 331808 | tf_op jit(solution)/shard_map/ppermute | solution.py:49
  150.5 0.3 constant_dynamic-update-slice_fusion.7
  150.7 1.7 collective-permute-start.19
  152.4 0.6 collective-permute-start.17
  153.1 13.5 %shard_map.61 = bf16[1536,6144]{1,0:T(8,128)(2,1)} custom-call(bf16[1536,448]{1,0:T(8,128)(2,1)S(1)} %fusion.32.x_ref, bf16[224,6144]{1,0:T(8,128)(2,1)S(1)} %pad_maximum_fusion.1.m_ref.refs_0_, bf16[224,6144]{1,0:T(8,128)(2,1)S(1)} %copy-done.1, bf16[1536,6144]{1,0:T(8,128)(2,1)} %refs_2_.3, ...), custom_call_target="tpu_custom_call", output_to_operand_aliasing={{}: (5, {})} | custom-call | flops 4227858432 | bytes 28311552 | tf_op jit(solution)/shard_map/pallas_call | solution.py:138
  166.6 7.7 %collective-permute-done.17 = bf16[216,768]{1,0:T(8,128)(2,1)S(1)} collective-permute-done((bf16[216,768]{1,0:T(8,128)(2,1)S(1)}, bf16[216,768]{1,0:T(8,128)(2,1)S(1)}, u32[]{:S(2)}, u32[]{:S(2)}) %collective-permute-start.17) | collective-permute-done | bytes 331808 | tf_op jit(solution)/shard_map/ppermute | solution.py:60
  174.3 5.3 %collective-permute-done.18 = bf16[216,768]{1,0:T(8,128)(2,1)S(1)} collective-permute-done((bf16[216,768]{1,0:T(8,128)(2,1)S(1)}, bf16[216,768]{1,0:T(8,128)(2,1)S(1)}, u32[]{:S(2)}, u32[]{:S(2)}) %collective-permute-start.18) | collective-permute-done | bytes 331808 | tf_op jit(solution)/shard_map/ppermute | solution.py:60
  179.8 1.1 copy-done.6
  (42 shorter events, 1.4 us)
Async XLA Ops:
  0.6 12.5 %copy-start.3 = (bf16[1536,6144]{1,0:T(8,128)(2,1)S(1)}, bf16[1536,6144]{1,0:T(8,128)(2,1)}, u32[]{:S(2)}) copy-start(bf16[1536,6144]{1,0:T(8,128)(2,1)} %refs_2_.3) | copy-start | bytes 56623108
  2.2 23.0 %copy-start.4 = (bf16[216,1536]{1,0:T(8,128)(2,1)}, bf16[216,1536]{1,0:T(8,128)(2,1)S(1)}, u32[]{:S(2)}) copy-start(bf16[216,1536]{1,0:T(8,128)(2,1)S(1)} %get-tuple-element.18) | copy-start | bytes 1990660
  2.2 2.3 %collective-permute-start = (bf16[216,1536]{1,0:T(8,128)(2,1)S(1)}, bf16[216,1536]{1,0:T(8,128)(2,1)S(1)}, u32[]{:S(2)}, u32[]{:S(2)}) collective-permute-start(bf16[216,1536]{1,0:T(8,128)(2,1)S(1)} %get-tuple-element.17), channel_id=1, source_target_pairs={{0,1},{1,0},{2,3},{3,2},{4,5},{5,4},{6,7},{7,6},{8,9},{9,8},{10,11... | collective-permute-start | bytes 1990664 | tf_op jit(solution)/shard_map/ppermute | solution.py:20
  4.5 10.4 %copy-start.7 = (bf16[216,1536]{1,0:T(8,128)(2,1)}, bf16[216,1536]{1,0:T(8,128)(2,1)S(1)}, u32[]{:S(2)}) copy-start(bf16[216,1536]{1,0:T(8,128)(2,1)S(1)} %collective-permute-done) | copy-start | bytes 1990660
  9.0 16.2 %collective-permute-start.1 = (bf16[216,1536]{1,0:T(8,128)(2,1)S(1)}, bf16[216,1536]{1,0:T(8,128)(2,1)S(1)}, u32[]{:S(2)}, u32[]{:S(2)}) collective-permute-start(bf16[216,1536]{1,0:T(8,128)(2,1)S(1)} %fusion.19), channel_id=1, source_target_pairs={{0,1},{1,0},{2,3},{3,2},{4,5},{5,4},{6,7},{7,6},{8,9},{9,8},{10,11... | collective-permute-start | bytes 1990664 | tf_op jit(solution)/shard_map/ppermute | solution.py:20
  13.0 3.4 %collective-permute-start.7 = (bf16[216,1536]{1,0:T(8,128)(2,1)S(1)}, bf16[216,1536]{1,0:T(8,128)(2,1)S(1)}, u32[]{:S(2)}, u32[]{:S(2)}) collective-permute-start(bf16[216,1536]{1,0:T(8,128)(2,1)S(1)} %fusion.28), channel_id=1, source_target_pairs={{0,1},{1,0},{2,3},{3,2},{4,5},{5,4},{6,7},{7,6},{8,9},{9,8},{10,11... | collective-permute-start | bytes 1990664 | tf_op jit(solution)/shard_map/ppermute | solution.py:20
  14.4 6.1 %collective-permute-start.5 = (bf16[216,1536]{1,0:T(8,128)(2,1)S(1)}, bf16[216,1536]{1,0:T(8,128)(2,1)S(1)}, u32[]{:S(2)}, u32[]{:S(2)}) collective-permute-start(bf16[216,1536]{1,0:T(8,128)(2,1)S(1)} %fusion.25), channel_id=1, source_target_pairs={{0,1},{1,0},{2,3},{3,2},{4,5},{5,4},{6,7},{7,6},{8,9},{9,8},{10,11... | collective-permute-start | bytes 1990664 | tf_op jit(solution)/shard_map/ppermute | solution.py:20
  16.1 5.8 %collective-permute-start.3 = (bf16[216,1536]{1,0:T(8,128)(2,1)S(1)}, bf16[216,1536]{1,0:T(8,128)(2,1)S(1)}, u32[]{:S(2)}, u32[]{:S(2)}) collective-permute-start(bf16[216,1536]{1,0:T(8,128)(2,1)S(1)} %fusion.22), channel_id=1, source_target_pairs={{0,1},{1,0},{2,3},{3,2},{4,5},{5,4},{6,7},{7,6},{8,9},{9,8},{10,11... | collective-permute-start | bytes 1990664 | tf_op jit(solution)/shard_map/ppermute | solution.py:20
  17.6 18.6 %collective-permute-start.8 = (bf16[216,1536]{1,0:T(8,128)(2,1)S(1)}, bf16[216,1536]{1,0:T(8,128)(2,1)S(1)}, u32[]{:S(2)}, u32[]{:S(2)}) collective-permute-start(bf16[216,1536]{1,0:T(8,128)(2,1)S(1)} %get-tuple-element.23), channel_id=1, source_target_pairs={{0,2},{2,0},{1,3},{3,1},{4,6},{6,4},{5,7},{7,5},{8,10},{10,8},{9,1... | collective-permute-start | bytes 1990664 | tf_op jit(solution)/shard_map/ppermute | solution.py:33
  21.8 28.6 %collective-permute-start.6 = (bf16[216,1536]{1,0:T(8,128)(2,1)S(1)}, bf16[216,1536]{1,0:T(8,128)(2,1)S(1)}, u32[]{:S(2)}, u32[]{:S(2)}) collective-permute-start(bf16[216,1536]{1,0:T(8,128)(2,1)S(1)} %get-tuple-element.25), channel_id=1, source_target_pairs={{0,2},{2,0},{1,3},{3,1},{4,6},{6,4},{5,7},{7,5},{8,10},{10,8},{9,1... | collective-permute-start | bytes 1990664 | tf_op jit(solution)/shard_map/ppermute | solution.py:33
  23.2 41.5 %collective-permute-start.4 = (bf16[216,1536]{1,0:T(8,128)(2,1)S(1)}, bf16[216,1536]{1,0:T(8,128)(2,1)S(1)}, u32[]{:S(2)}, u32[]{:S(2)}) collective-permute-start(bf16[216,1536]{1,0:T(8,128)(2,1)S(1)} %get-tuple-element.21), channel_id=1, source_target_pairs={{0,2},{2,0},{1,3},{3,1},{4,6},{6,4},{5,7},{7,5},{8,10},{10,8},{9,1... | collective-permute-start | bytes 1990664 | tf_op jit(solution)/shard_map/ppermute | solution.py:33
  25.2 53.2 %copy-start.5 = (bf16[216,6144]{1,0:T(8,128)(2,1)S(1)}, bf16[216,6144]{1,0:T(8,128)(2,1)}, u32[]{:S(2)}) copy-start(bf16[216,6144]{1,0:T(8,128)(2,1)} %param.5) | copy-start | bytes 7962628
  26.5 51.9 %collective-permute-start.2 = (bf16[216,1536]{1,0:T(8,128)(2,1)S(1)}, bf16[216,1536]{1,0:T(8,128)(2,1)S(1)}, u32[]{:S(2)}, u32[]{:S(2)}) collective-permute-start(bf16[216,1536]{1,0:T(8,128)(2,1)S(1)} %get-tuple-element.19), channel_id=1, source_target_pairs={{0,2},{2,0},{1,3},{3,1},{4,6},{6,4},{5,7},{7,5},{8,10},{10,8},{9,1... | collective-permute-start | bytes 1990664 | tf_op jit(solution)/shard_map/ppermute | solution.py:33
  81.8 5.3 %collective-permute-start.11 = (bf16[224,1536]{1,0:T(8,128)(2,1)S(1)}, bf16[224,1536]{1,0:T(8,128)(2,1)S(1)}, u32[]{:S(2)}, u32[]{:S(2)}) collective-permute-start(bf16[224,1536]{1,0:T(8,128)(2,1)S(1)} %pad.21), channel_id=1, source_target_pairs={{0,1},{1,0},{2,3},{3,2},{4,5},{5,4},{6,7},{7,6},{8,9},{9,8},{10,11... | collective-permute-start | bytes 2064392 | tf_op jit(solution)/shard_map/ppermute | solution.py:20
  81.9 5.4 %collective-permute-start.12 = (bf16[224,1536]{1,0:T(8,128)(2,1)S(1)}, bf16[224,1536]{1,0:T(8,128)(2,1)S(1)}, u32[]{:S(2)}, u32[]{:S(2)}) collective-permute-start(bf16[224,1536]{1,0:T(8,128)(2,1)S(1)} %pad.22), channel_id=1, source_target_pairs={{0,1},{1,0},{2,3},{3,2},{4,5},{5,4},{6,7},{7,6},{8,9},{9,8},{10,11... | collective-permute-start | bytes 2064392 | tf_op jit(solution)/shard_map/ppermute | solution.py:20
  82.4 4.7 %collective-permute-start.10 = (bf16[224,1536]{1,0:T(8,128)(2,1)S(1)}, bf16[224,1536]{1,0:T(8,128)(2,1)S(1)}, u32[]{:S(2)}, u32[]{:S(2)}) collective-permute-start(bf16[224,1536]{1,0:T(8,128)(2,1)S(1)} %pad.20), channel_id=1, source_target_pairs={{0,1},{1,0},{2,3},{3,2},{4,5},{5,4},{6,7},{7,6},{8,9},{9,8},{10,11... | collective-permute-start | bytes 2064392 | tf_op jit(solution)/shard_map/ppermute | solution.py:20
  82.5 4.5 %collective-permute-start.9 = (bf16[224,1536]{1,0:T(8,128)(2,1)S(1)}, bf16[224,1536]{1,0:T(8,128)(2,1)S(1)}, u32[]{:S(2)}, u32[]{:S(2)}) collective-permute-start(bf16[224,1536]{1,0:T(8,128)(2,1)S(1)} %pad.19), channel_id=1, source_target_pairs={{0,1},{1,0},{2,3},{3,2},{4,5},{5,4},{6,7},{7,6},{8,9},{9,8},{10,11... | collective-permute-start | bytes 2064392 | tf_op jit(solution)/shard_map/ppermute | solution.py:20
  87.4 1.5 copy-start
  106.7 1.5 copy-start.2
  109.1 5.5 %collective-permute-start.13 = (bf16[216,1536]{1,0:T(8,128)(2,1)}, bf16[216,1536]{1,0:T(8,128)(2,1)}, u32[]{:S(2)}, u32[]{:S(2)}) collective-permute-start(bf16[216,1536]{1,0:T(8,128)(2,1)} %slice.74), channel_id=1, source_target_pairs={{0,1},{1,0},{2,3},{3,2},{4,5},{5,4},{6,7},{7,6},{8,9},{9,8},{10,11... | collective-permute-start | bytes 1990664 | tf_op jit(solution)/shard_map/ppermute | solution.py:20
  116.5 5.2 %copy-start.1 = (bf16[224,6144]{1,0:T(8,128)(2,1)S(1)}, bf16[224,6144]{1,0:T(8,128)(2,1)}, u32[]{:S(2)}) copy-start(bf16[224,6144]{1,0:T(8,128)(2,1)} %copy-done) | copy-start | bytes 8257540
  116.7 18.4 %collective-permute-start.14 = (bf16[216,768]{1,0:T(8,128)(2,1)S(1)}, bf16[216,768]{1,0:T(8,128)(2,1)S(1)}, u32[]{:S(2)}, u32[]{:S(2)}) collective-permute-start(bf16[216,768]{1,0:T(8,128)(2,1)S(1)} %get-tuple-element.14), channel_id=1, source_target_pairs={{0,4},{4,8},{8,12},{12,0},{1,5},{5,9},{9,13},{13,1},{2,6},{6,10},{... | collective-permute-start | bytes 995336 | tf_op jit(solution)/shard_map/ppermute | solution.py:49
  118.6 16.9 %collective-permute-start.16 = (bf16[216,768]{1,0:T(8,128)(2,1)S(1)}, bf16[216,768]{1,0:T(8,128)(2,1)S(1)}, u32[]{:S(2)}, u32[]{:S(2)}) collective-permute-start(bf16[216,768]{1,0:T(8,128)(2,1)S(1)} %get-tuple-element.15), channel_id=1, source_target_pairs={{0,12},{4,0},{8,4},{12,8},{1,13},{5,1},{9,5},{13,9},{2,14},{6,2},{... | collective-permute-start | bytes 995336 | tf_op jit(solution)/shard_map/ppermute | solution.py:49
  120.7 29.6 %collective-permute-start.15 = (bf16[216,768]{1,0:T(8,128)(2,1)S(1)}, bf16[216,768]{1,0:T(8,128)(2,1)S(1)}, u32[]{:S(2)}, u32[]{:S(2)}) collective-permute-start(bf16[216,768]{1,0:T(8,128)(2,1)S(1)} %get-tuple-element.16), channel_id=1, source_target_pairs={{0,8},{4,12},{8,0},{12,4},{1,9},{5,13},{9,1},{13,5},{2,10},{6,14},... | collective-permute-start | bytes 995336 | tf_op jit(solution)/shard_map/ppermute | solution.py:49
  150.7 29.0 %collective-permute-start.19 = (bf16[216,768]{1,0:T(8,128)(2,1)S(1)}, bf16[216,768]{1,0:T(8,128)(2,1)S(1)}, u32[]{:S(2)}, u32[]{:S(2)}) collective-permute-start(bf16[216,768]{1,0:T(8,128)(2,1)S(1)} %get-tuple-element.7), channel_id=1, source_target_pairs={{0,12},{4,0},{8,4},{12,8},{1,13},{5,1},{9,5},{13,9},{2,14},{6,2},{... | collective-permute-start | bytes 995336 | tf_op jit(solution)/shard_map/ppermute | solution.py:60
  152.4 27.2 %collective-permute-start.18 = (bf16[216,768]{1,0:T(8,128)(2,1)S(1)}, bf16[216,768]{1,0:T(8,128)(2,1)S(1)}, u32[]{:S(2)}, u32[]{:S(2)}) collective-permute-start(bf16[216,768]{1,0:T(8,128)(2,1)S(1)} %get-tuple-element.7), channel_id=1, source_target_pairs={{0,8},{4,12},{8,0},{12,4},{1,9},{5,13},{9,1},{13,5},{2,10},{6,14},... | collective-permute-start | bytes 995336 | tf_op jit(solution)/shard_map/ppermute | solution.py:60
  152.4 21.8 %collective-permute-start.17 = (bf16[216,768]{1,0:T(8,128)(2,1)S(1)}, bf16[216,768]{1,0:T(8,128)(2,1)S(1)}, u32[]{:S(2)}, u32[]{:S(2)}) collective-permute-start(bf16[216,768]{1,0:T(8,128)(2,1)S(1)} %get-tuple-element.7), channel_id=1, source_target_pairs={{0,4},{4,8},{8,12},{12,0},{1,5},{5,9},{9,13},{13,1},{2,6},{6,10},{... | collective-permute-start | bytes 995336 | tf_op jit(solution)/shard_map/ppermute | solution.py:60
  179.7 1.1 copy-start.6

commit v5 on v4

--- a/solution.py
+++ b/solution.py
@@ -162,20 +162,30 @@
         x_other = swap(lax.dynamic_slice_in_dim(inputs, (1 - t) * rows, rows, 1))
         chunks = 4 if ff % (4 * 256) == 0 else 1
         w = ff // chunks
-        gm, go = [], []
+        gm, go, sent = [], [], []
+        unit = block_of(w, (512, 256, 128))
         for c in range(chunks):
             wc = weight[:, c * w : (c + 1) * w]
             send = mm(x_other, wc, ((1,), (0,))).astype(BF)
             part = mm(x_mine, wc, ((1,), (0,))) + swap(send).astype(F32)
-            own, got = send_partial(part, n_in)
+            sent.append(send_partial(part, n_in))
+        early = None
+        for c, (own, got) in enumerate(sent):
+            if 0 < c == chunks - 1:
+                ga = [jnp.concatenate(x, axis=1) for x in (gm, go)]
+                early = dx_partial(*ga, weight, unit)
+                got = after(got, early)
             pre = got if own is None else own + got.astype(F32)
             g = (grad_act[:, c * w : (c + 1) * w].astype(F32) * gelu_slope(pre)).astype(BF)
             g = jnp.pad(g, pad)
             gm.append(g)
             go.append(swap(g))
         gs = [jnp.concatenate(gm, axis=1), jnp.concatenate(go, axis=1)]
-        unit = block_of(ff, (512, 256, 128))
-        total = dx_partial(*gs, weight, unit)
+        if early is None:
+            total = dx_partial(*gs, weight, unit)
+        else:
+            last = jnp.concatenate([gm[-1], go[-1]], axis=0)
+            total = early + mm(last, weight[:, ff - w :], ((1,), (1,)))
         mine, theirs = total[:tokens], total[full : full + tokens]
         got = swap(theirs.astype(BF)).astype(F32)
         left, right = jnp.where(t == 0, mine, got), jnp.where(t == 0, got, mine)

time: 181 us -> 169 us (0.934)
  waiting for transfers between devices: 85.6 us -> 66.9 us
  matrix products: 15.6 us -> 29.8 us
  local copies, waits for them, and re-layouts: 11 us -> 3.91 us
  Pallas kernels: 44.6 us -> 42 us
    ppermute x4, waiting for transfers between devices: 51.8 us -> 34 us  [send_partial(): return (part, lax.ppermute(part.astype(BF), 'in', [(0, 1), (1, 0)]))]
    dot_general x8 -> x9, matrix products: 15.6 us -> 29.8 us  [mm(): return lax.dot_general(a, b, (dims, ((), ())), preferred_element_type=F32)]
    unnamed x20 -> x18, local copies, waits for them, and re-layouts: 5.7 us -> 1.59 us
    convert_element_type x1 -> x2, other arithmetic: 3.23 us -> 6.49 us  [on_device(): (grad_act[:, c * w:(c + 1) * w].astype(F32) * gelu_slope(pre)).astype(BF)]
    pallas_call x1, Pallas kernels: 17.7 us -> 15 us  [dx_partial(): pl.pallas_call(dx_kernel, grid=(width // unit,), in_specs=[g_block, g_blo...]
    ppermute x1, local copies, waits for them, and re-layouts: 2.24 us -> 0.27 us  [swap(): return lax.ppermute(x, 'tok', [(0, 1), (1, 0)])]
  transfers between devices with their start and end apart: 20 -> 20, of which waited for: 10 -> 11; matrix products, arithmetic and copies ran while one was open for 9% -> 17% of each run, Pallas kernels for 15% -> 25%
where the time goes in v5:
time: 169 us; the launch traced here: 168 us
  waiting for transfers between devices  66.9 us (40%)
  Pallas kernels  42 us (25%)
  matrix products  29.8 us (18%)
  starting transfers between devices  16.3 us (10%)
  other arithmetic  8.45 us (5%)
  local copies, waits for them, and re-layouts  3.91 us (2%)
    ppermute x4, waiting for transfers between devices, send_partial(): return (part, lax.ppermute(part.astype(BF), 'in', [(0, 1), (1, 0)]))  34 us
    dot_general x9, matrix products, mm(): return lax.dot_general(a, b, (dims, ((), ())), preferred_element_type=F32)  29.8 us
    pallas_call x2, Pallas kernels, score_part(): pl.pallas_call(functools.partial(score_kernel, len(gs)), grid=(count,), i...  26.9 us
    ppermute x3, waiting for transfers between devices, scatter_out(): got = lax.ppermute(piece, 'out', [(i, (i + k) % n) for i in range(n)])  15.1 us
    pallas_call x1, Pallas kernels, dx_partial(): pl.pallas_call(dx_kernel, grid=(width // unit,), in_specs=[g_block, g_blo...  15 us
    ppermute x3, waiting for transfers between devices, gather_out(): got = lax.ppermute(mine, 'out', [(i, (i + k) % n) for i in range(n)])  13.1 us
    convert_element_type x2, other arithmetic, on_device(): (grad_act[:, c * w:(c + 1) * w].astype(F32) * gelu_slope(pre)).astype(BF)  6.49 us
    ppermute x4, starting transfers between devices, send_partial(): return (part, lax.ppermute(part.astype(BF), 'in', [(0, 1), (1, 0)]))  6.47 us
  transfers between devices with their start and end apart: 20, of which 11 were waited for; matrix products, arithmetic and copies ran while one was open for 17% of the time, Pallas kernels for 25%

profile of v5, /device:TPU:0, one launch (start us, length us, event | category | flops | bytes accessed | tf_op | source)
XLA Modules:
  0.0 168.4 jit_solution(13473901196615387869)
XLA Ops:
  0.6 1.4 constant_dynamic-slice_fusion.3
  2.0 0.5 collective-permute-start
  2.5 0.3 copy.11
  2.8 1.4 collective-permute-done
  4.3 3.7 %fusion.33 = bf16[216,1536]{1,0:T(8,128)(2,1)S(1)} fusion(bf16[216,1536]{1,0:T(8,128)(2,1)S(1)} %collective-permute-done, bf16[1536,6144]{1,0:T(8,128)(2,1)} %refs_2_.3), kind=kOutput, calls=%fused_computation.31 | convolution fusion | flops 1019547648 | bytes 6045696 | tf_op jit(solution)/shard_map/dot_general | solution.py:24
  8.0 0.4 collective-permute-start.5
  8.4 4.3 %fusion.30 = bf16[216,1536]{1,0:T(8,128)(2,1)S(1)} fusion(bf16[216,1536]{1,0:T(8,128)(2,1)S(1)} %collective-permute-done, bf16[1536,6144]{1,0:T(8,128)(2,1)} %refs_2_.3), kind=kOutput, calls=%fused_computation.30 | convolution fusion | flops 1019547648 | bytes 6045696 | tf_op jit(solution)/shard_map/dot_general | solution.py:24
  12.7 0.2 collective-permute-start.3
  12.9 3.5 %fusion.27 = bf16[216,1536]{1,0:T(8,128)(2,1)S(1)} fusion(bf16[216,1536]{1,0:T(8,128)(2,1)S(1)} %collective-permute-done, bf16[1536,6144]{1,0:T(8,128)(2,1)} %refs_2_.3), kind=kOutput, calls=%fused_computation.29 | convolution fusion | flops 1019547648 | bytes 6045696 | tf_op jit(solution)/shard_map/dot_general | solution.py:24
  16.4 0.4 collective-permute-start.1
  16.9 2.6 %fusion.67 = (bf16[216,1536]{1,0:T(8,128)(2,1)}, f32[216,1536]{1,0:T(8,128)}) fusion(bf16[216,1536]{1,0:T(8,128)(2,1)S(1)} %collective-permute-done.5, bf16[216,1536]{1,0:T(8,128)(2,1)S(1)} %get-tuple-element.19, bf16[1536,6144]{1,0:T(8,128)(2,1)S(1)} %copy-done), kind=kOutput, calls=%fused_computation.76 | convolution fusion | flops 1020211200 | bytes 8036352 | tf_op jit(solution)/shard_map/dot_general | solution.py:24
  19.5 2.6 %collective-permute-start.6 = (bf16[216,1536]{1,0:T(8,128)(2,1)}, bf16[216,1536]{1,0:T(8,128)(2,1)}, u32[]{:S(2)}, u32[]{:S(2)}) collective-permute-start(bf16[216,1536]{1,0:T(8,128)(2,1)} %get-tuple-element.24), channel_id=1, source_target_pairs={{0,2},{2,0},{1,3},{3,1},{4,6},{6,4},{5,7},{7,5},{8,10},{10,8},{9,1... | collective-permute-start | bytes 1990664 | tf_op jit(solution)/shard_map/ppermute | solution.py:33
  22.1 2.6 %fusion.66 = (bf16[216,1536]{1,0:T(8,128)(2,1)}, f32[216,1536]{1,0:T(8,128)}) fusion(bf16[216,1536]{1,0:T(8,128)(2,1)S(1)} %collective-permute-done.3, bf16[216,1536]{1,0:T(8,128)(2,1)S(1)} %get-tuple-element.19, bf16[1536,6144]{1,0:T(8,128)(2,1)S(1)} %copy-done), kind=kOutput, calls=%fused_computation.75 | convolution fusion | flops 1020211200 | bytes 8036352 | tf_op jit(solution)/shard_map/dot_general | solution.py:24
  24.7 2.6 %fusion.65 = (bf16[216,1536]{1,0:T(8,128)(2,1)}, f32[216,1536]{1,0:T(8,128)}) fusion(bf16[216,1536]{1,0:T(8,128)(2,1)S(1)} %collective-permute-done.1, bf16[216,1536]{1,0:T(8,128)(2,1)S(1)} %get-tuple-element.19, bf16[1536,6144]{1,0:T(8,128)(2,1)S(1)} %copy-done), kind=kOutput, calls=%fused_computation.74 | convolution fusion | flops 1020211200 | bytes 8036352 | tf_op jit(solution)/shard_map/dot_general | solution.py:24
  27.4 2.0 %collective-permute-start.2 = (bf16[216,1536]{1,0:T(8,128)(2,1)}, bf16[216,1536]{1,0:T(8,128)(2,1)}, u32[]{:S(2)}, u32[]{:S(2)}) collective-permute-start(bf16[216,1536]{1,0:T(8,128)(2,1)} %get-tuple-element.20), channel_id=1, source_target_pairs={{0,2},{2,0},{1,3},{3,1},{4,6},{6,4},{5,7},{7,5},{8,10},{10,8},{9,1... | collective-permute-start | bytes 1990664 | tf_op jit(solution)/shard_map/ppermute | solution.py:33
  29.4 2.1 %fusion.24 = bf16[216,1536]{1,0:T(8,128)(2,1)} fusion(bf16[216,1536]{1,0:T(8,128)(2,1)S(1)} %collective-permute-done, bf16[1536,6144]{1,0:T(8,128)(2,1)S(1)} %copy-done), kind=kOutput, calls=%fused_computation.28 | convolution fusion | flops 1019547648 | bytes 6045696 | tf_op jit(solution)/shard_map/dot_general | solution.py:24
  31.5 0.3 copy.10
  31.8 0.7 fusion.37.x_ref
  32.5 5.7 %collective-permute-done.6 = bf16[216,1536]{1,0:T(8,128)(2,1)} collective-permute-done((bf16[216,1536]{1,0:T(8,128)(2,1)}, bf16[216,1536]{1,0:T(8,128)(2,1)}, u32[]{:S(2)}, u32[]{:S(2)}) %collective-permute-start.6) | collective-permute-done | bytes 663584 | tf_op jit(solution)/shard_map/ppermute | solution.py:33
  38.2 14.2 %collective-permute-done.4 = bf16[216,1536]{1,0:T(8,128)(2,1)} collective-permute-done((bf16[216,1536]{1,0:T(8,128)(2,1)}, bf16[216,1536]{1,0:T(8,128)(2,1)}, u32[]{:S(2)}, u32[]{:S(2)}) %collective-permute-start.4) | collective-permute-done | bytes 663584 | tf_op jit(solution)/shard_map/ppermute | solution.py:33
  52.4 13.9 %collective-permute-done.2 = bf16[216,1536]{1,0:T(8,128)(2,1)} collective-permute-done((bf16[216,1536]{1,0:T(8,128)(2,1)}, bf16[216,1536]{1,0:T(8,128)(2,1)}, u32[]{:S(2)}, u32[]{:S(2)}) %collective-permute-start.2) | collective-permute-done | bytes 663584 | tf_op jit(solution)/shard_map/ppermute | solution.py:33
  66.3 4.6 %fusion.46 = (bf16[216,1536]{1,0:T(8,128)(2,1)S(1)}, bf16[216,1536]{1,0:T(8,128)(2,1)S(1)}, bf16[216,1536]{1,0:T(8,128)(2,1)S(1)}) fusion(bf16[216,1536]{1,0:T(8,128)(2,1)} %collective-permute-done.2, f32[216,1536]{1,0:T(8,128)} %get-tuple-element.21, bf16[216,1536]{1,0:T(8,128)(2,1)} %copy-done.6, bf16[216,6144]{1,0:T(8,128)(2,1)S(1)} %copy-done.2, ...), kind=kLoop, calls=%fused_computation.50 | loop fusion | flops 14929920 | bytes 11943936 | tf_op jit(solution)/shard_map/convert_element_type | solution.py:179
  71.2 0.5 collective-permute-start.8
  71.8 3.7 %fusion.68 = (bf16[216,1536]{1,0:T(8,128)(2,1)S(1)}, f32[216,1536]{1,0:T(8,128)S(1)}) fusion(bf16[216,1536]{1,0:T(8,128)(2,1)} %collective-permute-done.10, bf16[216,1536]{1,0:T(8,128)(2,1)S(1)} %get-tuple-element.19, bf16[1536,6144]{1,0:T(8,128)(2,1)} %refs_2_.3), kind=kOutput, calls=%fused_computation.77 | convolution fusion | flops 1020211200 | bytes 8036352 | tf_op jit(solution)/shard_map/dot_general | solution.py:24
  75.5 1.8 %collective-permute-start.11 = (bf16[216,1536]{1,0:T(8,128)(2,1)S(1)}, bf16[216,1536]{1,0:T(8,128)(2,1)S(1)}, u32[]{:S(2)}, u32[]{:S(2)}) collective-permute-start(bf16[216,1536]{1,0:T(8,128)(2,1)S(1)} %get-tuple-element.26), channel_id=1, source_target_pairs={{0,2},{2,0},{1,3},{3,1},{4,6},{6,4},{5,7},{7,5},{8,10},{10,8},{9,1... | collective-permute-start | bytes 1990664 | tf_op jit(solution)/shard_map/ppermute | solution.py:33
  77.6 15.0 %shard_map.59 = f32[448,1536]{1,0:T(8,128)} custom-call(bf16[224,4608]{1,0:T(8,128)(2,1)S(1)} %pad_maximum_fusion.2.m_ref, bf16[224,4608]{1,0:T(8,128)(2,1)S(1)} %pad_maximum_fusion.3.o_ref, bf16[1536,6144]{1,0:T(8,128)(2,1)} %refs_2_.3), custom_call_target="tpu_custom_call" | custom-call | flops 6341787648 | bytes 14155776 | tf_op jit(solution)/shard_map/pallas_call | solution.py:94
  92.7 0.2 collective-permute-done.11
  92.8 1.8 %fusion.64 = bf16[216,1536]{1,0:T(8,128)(2,1)S(1)} fusion(bf16[216,1536]{1,0:T(8,128)(2,1)S(1)} %collective-permute-done.11, f32[216,1536]{1,0:T(8,128)S(1)} %get-tuple-element.27, bf16[216,1536]{1,0:T(8,128)(2,1)} %collective-permute-done.10, bf16[216,6144]{1,0:T(8,128)(2,1)S(1)} %copy-done.2), kind=kLoop, calls=%fused_computation.68 | loop fusion | flops 4976640 | bytes 3981312 | tf_op jit(solution)/shard_map/convert_element_type | solution.py:179
  94.9 0.3 pad_maximum_fusion.1.refs_0_
  95.2 1.7 %collective-permute-done.12 = bf16[224,1536]{1,0:T(8,128)(2,1)S(1)} collective-permute-done((bf16[224,1536]{1,0:T(8,128)(2,1)S(1)}, bf16[224,1536]{1,0:T(8,128)(2,1)S(1)}, u32[]{:S(2)}, u32[]{:S(2)}) %collective-permute-start.12) | collective-permute-done | bytes 688160 | tf_op jit(solution)/shard_map/ppermute | solution.py:20
  97.0 4.7 %fusion.20 = f32[448,1536]{1,0:T(8,128)S(1)} fusion(f32[448,1536]{1,0:T(8,128)S(1)} %copy-done.1, bf16[1536,6144]{1,0:T(8,128)(2,1)} %refs_2_.3, bf16[224,1536]{1,0:T(8,128)(2,1)S(1)} %collective-permute-done.12, bf16[224,1536]{1,0:T(8,128)(2,1)S(1)} %pad.22), kind=kOutput, calls=%fused_computation.25 | convolution fusion | flops 2117369856 | bytes 11599872 | tf_op jit(solution)/shard_map/dot_general | solution.py:24
  101.7 0.3 collective-permute-start.13
  102.3 1.6 collective-permute-done.13
  103.9 0.3 convert_select_fusion.1
  104.2 0.1 fusion.23
  104.5 1.9 %collective-permute-start.14 = (bf16[216,768]{1,0:T(8,128)(2,1)S(1)}, bf16[216,768]{1,0:T(8,128)(2,1)S(1)}, u32[]{:S(2)}, u32[]{:S(2)}) collective-permute-start(bf16[216,768]{1,0:T(8,128)(2,1)S(1)} %get-tuple-element.15), channel_id=1, source_target_pairs={{0,4},{4,8},{8,12},{12,0},{1,5},{5,9},{9,13},{13,1},{2,6},{6,10},{... | collective-permute-start | bytes 995336 | tf_op jit(solution)/shard_map/ppermute | solution.py:49
  106.3 2.1 %collective-permute-start.16 = (bf16[216,768]{1,0:T(8,128)(2,1)S(1)}, bf16[216,768]{1,0:T(8,128)(2,1)S(1)}, u32[]{:S(2)}, u32[]{:S(2)}) collective-permute-start(bf16[216,768]{1,0:T(8,128)(2,1)S(1)} %get-tuple-element.16), channel_id=1, source_target_pairs={{0,12},{4,0},{8,4},{12,8},{1,13},{5,1},{9,5},{13,9},{2,14},{6,2},{... | collective-permute-start | bytes 995336 | tf_op jit(solution)/shard_map/ppermute | solution.py:49
  108.4 0.9 collective-permute-start.15
  109.4 13.4 %shard_map.60.refs_4_ = bf16[1536,6144]{1,0:T(8,128)(2,1)} custom-call(bf16[1536,448]{1,0:T(8,128)(2,1)S(1)} %fusion.37.x_ref, bf16[224,6144]{1,0:T(8,128)(2,1)S(1)} %pad_maximum_fusion.1.refs_0_, bf16[224,6144]{1,0:T(8,128)(2,1)S(1)} %constant_dynamic-update-slice_fusion.refs_1_, bf16[1536,6144]{1,0:T(8,128)(2,1)} %refs_2_.3, bf16[1536,6144]{1,0:T(8,128)(2,1)} %refs_3_.3), custom_call_target="tpu_custom_call" | custom-call | flops 4227858432 | bytes 28311552 | tf_op jit(solution)/shard_map/pallas_call | solution.py:138
  122.8 0.3 collective-permute-done.16
  123.1 14.8 %collective-permute-done.15 = bf16[216,768]{1,0:T(8,128)(2,1)S(1)} collective-permute-done((bf16[216,768]{1,0:T(8,128)(2,1)S(1)}, bf16[216,768]{1,0:T(8,128)(2,1)S(1)}, u32[]{:S(2)}, u32[]{:S(2)}) %collective-permute-start.15) | collective-permute-done | bytes 331808 | tf_op jit(solution)/shard_map/ppermute | solution.py:49
  138.0 0.3 constant_dynamic-update-slice_fusion.7
  138.3 1.7 collective-permute-start.19
  140.0 0.6 collective-permute-start.17
  140.6 13.5 %shard_map.61 = bf16[1536,6144]{1,0:T(8,128)(2,1)} custom-call(bf16[1536,448]{1,0:T(8,128)(2,1)S(1)} %fusion.37.x_ref, bf16[224,6144]{1,0:T(8,128)(2,1)S(1)} %pad_maximum_fusion.1.refs_0_, bf16[224,6144]{1,0:T(8,128)(2,1)S(1)} %constant_dynamic-update-slice_fusion.refs_1_, bf16[1536,6144]{1,0:T(8,128)(2,1)} %refs_2_.3, ...), custom_call_target="tpu_custom_call", output_to_operand_aliasing={{}: (5, {})} | custom-call | flops 4227858432 | bytes 28311552 | tf_op jit(solution)/shard_map/pallas_call | solution.py:138
  154.1 7.6 %collective-permute-done.17 = bf16[216,768]{1,0:T(8,128)(2,1)S(1)} collective-permute-done((bf16[216,768]{1,0:T(8,128)(2,1)S(1)}, bf16[216,768]{1,0:T(8,128)(2,1)S(1)}, u32[]{:S(2)}, u32[]{:S(2)}) %collective-permute-start.17) | collective-permute-done | bytes 331808 | tf_op jit(solution)/shard_map/ppermute | solution.py:60
  161.7 5.5 %collective-permute-done.18 = bf16[216,768]{1,0:T(8,128)(2,1)S(1)} collective-permute-done((bf16[216,768]{1,0:T(8,128)(2,1)S(1)}, bf16[216,768]{1,0:T(8,128)(2,1)S(1)}, u32[]{:S(2)}, u32[]{:S(2)}) %collective-permute-start.18) | collective-permute-done | bytes 331808 | tf_op jit(solution)/shard_map/ppermute | solution.py:60
  167.3 1.1 copy-done.3
  (44 shorter events, 1.5 us)
Async XLA Ops:
  2.0 2.3 %collective-permute-start = (bf16[216,1536]{1,0:T(8,128)(2,1)S(1)}, bf16[216,1536]{1,0:T(8,128)(2,1)S(1)}, u32[]{:S(2)}, u32[]{:S(2)}) collective-permute-start(bf16[216,1536]{1,0:T(8,128)(2,1)S(1)} %get-tuple-element.18), channel_id=1, source_target_pairs={{0,1},{1,0},{2,3},{3,2},{4,5},{5,4},{6,7},{7,6},{8,9},{9,8},{10,11... | collective-permute-start | bytes 1990664 | tf_op jit(solution)/shard_map/ppermute | solution.py:20
  4.3 12.6 %copy-start = (bf16[1536,6144]{1,0:T(8,128)(2,1)S(1)}, bf16[1536,6144]{1,0:T(8,128)(2,1)}, u32[]{:S(2)}) copy-start(bf16[1536,6144]{1,0:T(8,128)(2,1)} %refs_2_.3) | copy-start | bytes 56623108
  8.0 8.9 %collective-permute-start.5 = (bf16[216,1536]{1,0:T(8,128)(2,1)S(1)}, bf16[216,1536]{1,0:T(8,128)(2,1)S(1)}, u32[]{:S(2)}, u32[]{:S(2)}) collective-permute-start(bf16[216,1536]{1,0:T(8,128)(2,1)S(1)} %fusion.33), channel_id=1, source_target_pairs={{0,1},{1,0},{2,3},{3,2},{4,5},{5,4},{6,7},{7,6},{8,9},{9,8},{10,11... | collective-permute-start | bytes 1990664 | tf_op jit(solution)/shard_map/ppermute | solution.py:20
  12.7 9.4 %collective-permute-start.3 = (bf16[216,1536]{1,0:T(8,128)(2,1)S(1)}, bf16[216,1536]{1,0:T(8,128)(2,1)S(1)}, u32[]{:S(2)}, u32[]{:S(2)}) collective-permute-start(bf16[216,1536]{1,0:T(8,128)(2,1)S(1)} %fusion.30), channel_id=1, source_target_pairs={{0,1},{1,0},{2,3},{3,2},{4,5},{5,4},{6,7},{7,6},{8,9},{9,8},{10,11... | collective-permute-start | bytes 1990664 | tf_op jit(solution)/shard_map/ppermute | solution.py:20
  16.4 8.3 %collective-permute-start.1 = (bf16[216,1536]{1,0:T(8,128)(2,1)S(1)}, bf16[216,1536]{1,0:T(8,128)(2,1)S(1)}, u32[]{:S(2)}, u32[]{:S(2)}) collective-permute-start(bf16[216,1536]{1,0:T(8,128)(2,1)S(1)} %fusion.27), channel_id=1, source_target_pairs={{0,1},{1,0},{2,3},{3,2},{4,5},{5,4},{6,7},{7,6},{8,9},{9,8},{10,11... | collective-permute-start | bytes 1990664 | tf_op jit(solution)/shard_map/ppermute | solution.py:20
  16.9 2.6 %copy-start.4 = (bf16[216,1536]{1,0:T(8,128)(2,1)}, bf16[216,1536]{1,0:T(8,128)(2,1)S(1)}, u32[]{:S(2)}) copy-start(bf16[216,1536]{1,0:T(8,128)(2,1)S(1)} %collective-permute-done.5) | copy-start | bytes 1990660
  19.5 18.7 %collective-permute-start.6 = (bf16[216,1536]{1,0:T(8,128)(2,1)}, bf16[216,1536]{1,0:T(8,128)(2,1)}, u32[]{:S(2)}, u32[]{:S(2)}) collective-permute-start(bf16[216,1536]{1,0:T(8,128)(2,1)} %get-tuple-element.24), channel_id=1, source_target_pairs={{0,2},{2,0},{1,3},{3,1},{4,6},{6,4},{5,7},{7,5},{8,10},{10,8},{9,1... | collective-permute-start | bytes 1990664 | tf_op jit(solution)/shard_map/ppermute | solution.py:33
  22.1 2.6 %copy-start.5 = (bf16[216,1536]{1,0:T(8,128)(2,1)}, bf16[216,1536]{1,0:T(8,128)(2,1)S(1)}, u32[]{:S(2)}) copy-start(bf16[216,1536]{1,0:T(8,128)(2,1)S(1)} %collective-permute-done.3) | copy-start | bytes 1990660
  24.7 27.7 %collective-permute-start.4 = (bf16[216,1536]{1,0:T(8,128)(2,1)}, bf16[216,1536]{1,0:T(8,128)(2,1)}, u32[]{:S(2)}, u32[]{:S(2)}) collective-permute-start(bf16[216,1536]{1,0:T(8,128)(2,1)} %get-tuple-element.22), channel_id=1, source_target_pairs={{0,2},{2,0},{1,3},{3,1},{4,6},{6,4},{5,7},{7,5},{8,10},{10,8},{9,1... | collective-permute-start | bytes 1990664 | tf_op jit(solution)/shard_map/ppermute | solution.py:33
  24.7 2.6 %copy-start.6 = (bf16[216,1536]{1,0:T(8,128)(2,1)}, bf16[216,1536]{1,0:T(8,128)(2,1)S(1)}, u32[]{:S(2)}) copy-start(bf16[216,1536]{1,0:T(8,128)(2,1)S(1)} %collective-permute-done.1) | copy-start | bytes 1990660
  27.4 38.9 %collective-permute-start.2 = (bf16[216,1536]{1,0:T(8,128)(2,1)}, bf16[216,1536]{1,0:T(8,128)(2,1)}, u32[]{:S(2)}, u32[]{:S(2)}) collective-permute-start(bf16[216,1536]{1,0:T(8,128)(2,1)} %get-tuple-element.20), channel_id=1, source_target_pairs={{0,2},{2,0},{1,3},{3,1},{4,6},{6,4},{5,7},{7,5},{8,10},{10,8},{9,1... | collective-permute-start | bytes 1990664 | tf_op jit(solution)/shard_map/ppermute | solution.py:33
  31.5 40.3 %collective-permute-start.10 = (bf16[216,1536]{1,0:T(8,128)(2,1)}, bf16[216,1536]{1,0:T(8,128)(2,1)}, u32[]{:S(2)}, u32[]{:S(2)}) collective-permute-start(bf16[216,1536]{1,0:T(8,128)(2,1)} %fusion.24), channel_id=1, source_target_pairs={{0,1},{1,0},{2,3},{3,2},{4,5},{5,4},{6,7},{7,6},{8,9},{9,8},{10,11... | collective-permute-start | bytes 1990664 | tf_op jit(solution)/shard_map/ppermute | solution.py:20
  31.8 34.5 %copy-start.2 = (bf16[216,6144]{1,0:T(8,128)(2,1)S(1)}, bf16[216,6144]{1,0:T(8,128)(2,1)}, u32[]{:S(2)}) copy-start(bf16[216,6144]{1,0:T(8,128)(2,1)} %param.5) | copy-start | bytes 7962628
  71.1 6.3 %collective-permute-start.9 = (bf16[224,1536]{1,0:T(8,128)(2,1)S(1)}, bf16[224,1536]{1,0:T(8,128)(2,1)S(1)}, u32[]{:S(2)}, u32[]{:S(2)}) collective-permute-start(bf16[224,1536]{1,0:T(8,128)(2,1)S(1)} %pad.21), channel_id=1, source_target_pairs={{0,1},{1,0},{2,3},{3,2},{4,5},{5,4},{6,7},{7,6},{8,9},{9,8},{10,11... | collective-permute-start | bytes 2064392 | tf_op jit(solution)/shard_map/ppermute | solution.py:20
  71.2 6.3 %collective-permute-start.8 = (bf16[224,1536]{1,0:T(8,128)(2,1)S(1)}, bf16[224,1536]{1,0:T(8,128)(2,1)S(1)}, u32[]{:S(2)}, u32[]{:S(2)}) collective-permute-start(bf16[224,1536]{1,0:T(8,128)(2,1)S(1)} %pad.20), channel_id=1, source_target_pairs={{0,1},{1,0},{2,3},{3,2},{4,5},{5,4},{6,7},{7,6},{8,9},{9,8},{10,11... | collective-permute-start | bytes 2064392 | tf_op jit(solution)/shard_map/ppermute | solution.py:20
  71.7 5.8 %collective-permute-start.7 = (bf16[224,1536]{1,0:T(8,128)(2,1)S(1)}, bf16[224,1536]{1,0:T(8,128)(2,1)S(1)}, u32[]{:S(2)}, u32[]{:S(2)}) collective-permute-start(bf16[224,1536]{1,0:T(8,128)(2,1)S(1)} %pad.19), channel_id=1, source_target_pairs={{0,1},{1,0},{2,3},{3,2},{4,5},{5,4},{6,7},{7,6},{8,9},{9,8},{10,11... | collective-permute-start | bytes 2064392 | tf_op jit(solution)/shard_map/ppermute | solution.py:20
  75.5 17.3 %collective-permute-start.11 = (bf16[216,1536]{1,0:T(8,128)(2,1)S(1)}, bf16[216,1536]{1,0:T(8,128)(2,1)S(1)}, u32[]{:S(2)}, u32[]{:S(2)}) collective-permute-start(bf16[216,1536]{1,0:T(8,128)(2,1)S(1)} %get-tuple-element.26), channel_id=1, source_target_pairs={{0,2},{2,0},{1,3},{3,1},{4,6},{6,4},{5,7},{7,5},{8,10},{10,8},{9,1... | collective-permute-start | bytes 1990664 | tf_op jit(solution)/shard_map/ppermute | solution.py:33
  94.7 2.2 %collective-permute-start.12 = (bf16[224,1536]{1,0:T(8,128)(2,1)S(1)}, bf16[224,1536]{1,0:T(8,128)(2,1)S(1)}, u32[]{:S(2)}, u32[]{:S(2)}) collective-permute-start(bf16[224,1536]{1,0:T(8,128)(2,1)S(1)} %pad.22), channel_id=1, source_target_pairs={{0,1},{1,0},{2,3},{3,2},{4,5},{5,4},{6,7},{7,6},{8,9},{9,8},{10,11... | collective-permute-start | bytes 2064392 | tf_op jit(solution)/shard_map/ppermute | solution.py:20
  94.9 2.1 %copy-start.1 = (f32[448,1536]{1,0:T(8,128)S(1)}, f32[448,1536]{1,0:T(8,128)}, u32[]{:S(2)}) copy-start(f32[448,1536]{1,0:T(8,128)} %shard_map.59) | copy-start | bytes 8257540
  101.7 2.2 %collective-permute-start.13 = (bf16[216,1536]{1,0:T(8,128)(2,1)S(1)}, bf16[216,1536]{1,0:T(8,128)(2,1)S(1)}, u32[]{:S(2)}, u32[]{:S(2)}) collective-permute-start(bf16[216,1536]{1,0:T(8,128)(2,1)S(1)} %slice.79), channel_id=1, source_target_pairs={{0,1},{1,0},{2,3},{3,2},{4,5},{5,4},{6,7},{7,6},{8,9},{9,8},{10,11... | collective-permute-start | bytes 1990664 | tf_op jit(solution)/shard_map/ppermute | solution.py:20
  104.5 18.4 %collective-permute-start.14 = (bf16[216,768]{1,0:T(8,128)(2,1)S(1)}, bf16[216,768]{1,0:T(8,128)(2,1)S(1)}, u32[]{:S(2)}, u32[]{:S(2)}) collective-permute-start(bf16[216,768]{1,0:T(8,128)(2,1)S(1)} %get-tuple-element.15), channel_id=1, source_target_pairs={{0,4},{4,8},{8,12},{12,0},{1,5},{5,9},{9,13},{13,1},{2,6},{6,10},{... | collective-permute-start | bytes 995336 | tf_op jit(solution)/shard_map/ppermute | solution.py:49
  106.3 16.8 %collective-permute-start.16 = (bf16[216,768]{1,0:T(8,128)(2,1)S(1)}, bf16[216,768]{1,0:T(8,128)(2,1)S(1)}, u32[]{:S(2)}, u32[]{:S(2)}) collective-permute-start(bf16[216,768]{1,0:T(8,128)(2,1)S(1)} %get-tuple-element.16), channel_id=1, source_target_pairs={{0,12},{4,0},{8,4},{12,8},{1,13},{5,1},{9,5},{13,9},{2,14},{6,2},{... | collective-permute-start | bytes 995336 | tf_op jit(solution)/shard_map/ppermute | solution.py:49
  108.4 29.5 %collective-permute-start.15 = (bf16[216,768]{1,0:T(8,128)(2,1)S(1)}, bf16[216,768]{1,0:T(8,128)(2,1)S(1)}, u32[]{:S(2)}, u32[]{:S(2)}) collective-permute-start(bf16[216,768]{1,0:T(8,128)(2,1)S(1)} %get-tuple-element.17), channel_id=1, source_target_pairs={{0,8},{4,12},{8,0},{12,4},{1,9},{5,13},{9,1},{13,5},{2,10},{6,14},... | collective-permute-start | bytes 995336 | tf_op jit(solution)/shard_map/ppermute | solution.py:49
  138.3 29.0 %collective-permute-start.19 = (bf16[216,768]{1,0:T(8,128)(2,1)S(1)}, bf16[216,768]{1,0:T(8,128)(2,1)S(1)}, u32[]{:S(2)}, u32[]{:S(2)}) collective-permute-start(bf16[216,768]{1,0:T(8,128)(2,1)S(1)} %get-tuple-element.9), channel_id=1, source_target_pairs={{0,12},{4,0},{8,4},{12,8},{1,13},{5,1},{9,5},{13,9},{2,14},{6,2},{... | collective-permute-start | bytes 995336 | tf_op jit(solution)/shard_map/ppermute | solution.py:60
  140.0 27.2 %collective-permute-start.18 = (bf16[216,768]{1,0:T(8,128)(2,1)S(1)}, bf16[216,768]{1,0:T(8,128)(2,1)S(1)}, u32[]{:S(2)}, u32[]{:S(2)}) collective-permute-start(bf16[216,768]{1,0:T(8,128)(2,1)S(1)} %get-tuple-element.9), channel_id=1, source_target_pairs={{0,8},{4,12},{8,0},{12,4},{1,9},{5,13},{9,1},{13,5},{2,10},{6,14},... | collective-permute-start | bytes 995336 | tf_op jit(solution)/shard_map/ppermute | solution.py:60
  140.0 21.7 %collective-permute-start.17 = (bf16[216,768]{1,0:T(8,128)(2,1)S(1)}, bf16[216,768]{1,0:T(8,128)(2,1)S(1)}, u32[]{:S(2)}, u32[]{:S(2)}) collective-permute-start(bf16[216,768]{1,0:T(8,128)(2,1)S(1)} %get-tuple-element.9), channel_id=1, source_target_pairs={{0,4},{4,8},{8,12},{12,0},{1,5},{5,9},{9,13},{13,1},{2,6},{6,10},{... | collective-permute-start | bytes 995336 | tf_op jit(solution)/shard_map/ppermute | solution.py:60
  167.3 1.1 copy-start.3
